TPU v7x, 32 devices: a whole 2x2x4 slice. The times are simulated.
32 devices in a mesh: parts: 2 (over y), gx: 4 (over z), gy: 4 (over x, core).
Axes of the slice: x: 2, y: 2, z: 4, core: 2. Of those that a mesh axis runs over, the one named last changes fastest.
Arguments:
- force: float32 [3, 17, 48, 512], P(None, None, ('parts', 'gx'), 'gy'), parts along dimension 2, may hold values from -6 to 6
- phase: int32 [16, 48, 512], P(None, ('parts', 'gx'), 'gy'), parts along dimension 1, may hold values from 0 to 3
- fixed: int32 [17, 48, 512], P(None, ('parts', 'gx'), 'gy'), parts along dimension 1, may hold values 0 or 1
Outputs:
- displacement: float32 [3, 17, 48, 512], P(None, None, ('parts', 'gx'), 'gy'), parts along dimension 2
- sensitivity: float32 [16, 48, 512], P(None, ('parts', 'gx'), 'gy'), parts along dimension 1
There are 2 independent parts, one for each index of `parts`. A program takes and returns all parts, laid end to end along the dimension named above; each array names one. Nothing has to cross between parts.
All inputs are finite; a program needn't handle non-finite values. No bound on the sum of `fixed` on one device may be relied on, other than what follows from the above.
Results may differ from a plain program's by a relative error of at most 0.0003.
Values sent between devices are 32-bit elements; how exact they have to be, the bound alone decides.
No kernel may reach another device: no remote copies, remote signals or barrier semaphores. Data moves between devices by JAX's collectives and lax.ppermute only.
A program may use at most 64 MiB of HBM per device.

v0:
```python
import math

import jax
import jax.numpy as jnp
import numpy as np
from jax import lax
from jax.sharding import PartitionSpec as P

ITERS = 2


corner_list = tuple(((a, b, c) for a in (0, 1) for b in (0, 1) for c in (0, 1)))
phase_stiffness = (0.125, 0.343, 0.614, 1.0)
phase_slope = (0.75, 1.47, 2.17, 3.0)


def padded(cells, sides, width):
    for axis, dim in sides:
        count = lax.axis_size(axis)
        head = lax.slice_in_dim(cells, 0, width, axis=dim)
        tail = lax.slice_in_dim(cells, cells.shape[dim] - width, cells.shape[dim], axis=dim)
        cells = jnp.concatenate(
            [
                lax.ppermute(tail, axis, [(i, (i + 1) % count) for i in range(count)]),
                cells,
                lax.ppermute(head, axis, [((i + 1) % count, i) for i in range(count)]),
            ],
            axis=dim,
        )
    return cells


def shifted(x, axis, by):
    count = lax.axis_size(axis)
    return lax.ppermute(x, axis, [(i, (i + by) % count) for i in range(count)])


def element_matrix():
    poisson = 0.3
    lame_first = poisson / ((1.0 + poisson) * (1.0 - 2.0 * poisson))
    shear = 1.0 / (2.0 * (1.0 + poisson))
    elastic = np.zeros((6, 6))
    elastic[:3, :3] = lame_first
    for index in range(3):
        elastic[index, index] += 2.0 * shear
        elastic[3 + index, 3 + index] = shear
    gauss_points = (0.5 - 0.5 / math.sqrt(3.0), 0.5 + 0.5 / math.sqrt(3.0))
    stiffness = np.zeros((24, 24))
    for first in gauss_points:
        for second in gauss_points:
            for third in gauss_points:
                point = (first, second, third)
                strain_map = np.zeros((6, 24))
                for node, bits in enumerate(corner_list):
                    grads = []
                    for axis in range(3):
                        factor = 1.0
                        for other in range(3):
                            if other == axis:
                                factor *= 1.0 if bits[other] else -1.0
                            else:
                                factor *= point[other] if bits[other] else 1.0 - point[other]
                        grads.append(factor)
                    for axis in range(3):
                        strain_map[axis, 3 * node + axis] = grads[axis]
                    strain_map[3, 3 * node + 1] = grads[2]
                    strain_map[3, 3 * node + 2] = grads[1]
                    strain_map[4, 3 * node + 0] = grads[2]
                    strain_map[4, 3 * node + 2] = grads[0]
                    strain_map[5, 3 * node + 0] = grads[1]
                    strain_map[5, 3 * node + 1] = grads[0]
                stiffness += strain_map.T @ elastic @ strain_map / 8.0
    return stiffness


def phase_values(phase, table):
    total = jnp.zeros(phase.shape, jnp.float32)
    for index, value in enumerate(table):
        total = total + jnp.where(phase == index, jnp.float32(value), jnp.float32(0.0))
    return total


def stack_corners(wide):
    layers = wide.shape[1] - 1
    span_x = wide.shape[2] - 1
    span_y = wide.shape[3] - 1
    return jnp.concatenate(
        [wide[:, a : a + layers, b : b + span_x, c : c + span_y] for a, b, c in corner_list], 0
    )


def spread_nodes(terms):
    total = None
    for node, (a, b, c) in enumerate(corner_list):
        piece = jnp.pad(
            terms[3 * node : 3 * node + 3], ((0, 0), (a, 1 - a), (b, 1 - b), (c, 1 - c))
        )
        total = piece if total is None else total + piece
    return total


def element_forces(stiff, stacked):
    flat = jnp.dot(stiff, stacked.reshape(24, -1), precision=lax.Precision.HIGHEST)
    return flat.reshape(stacked.shape)


def body(force, phase, fixed):
    stiff = jnp.asarray(element_matrix(), jnp.float32)
    free = (1 - fixed).astype(jnp.float32)[None]
    scale = phase_values(phase, phase_stiffness)
    slope = phase_values(phase, phase_slope)
    diag_entries = jnp.diagonal(stiff)[:, None, None, None]

    def widen(field):
        return padded(field, (("gx", 2), ("gy", 3)), 1)

    prior_row = shifted(scale[:, -1:, :], "gx", 1)
    rowed = jnp.concatenate([prior_row, scale], 1)
    prior_column = shifted(rowed[:, :, -1:], "gy", 1)
    scale_wide = jnp.concatenate([prior_column, rowed], 2)
    stiff_diagonal = spread_nodes(diag_entries * scale_wide[None])[:, :, 1:-1, 1:-1]
    diag = free * stiff_diagonal + (1.0 - free)
    rhs = free * force
    displacement = jnp.zeros_like(rhs)
    residual = rhs

    def residual_norm(current):
        return lax.psum(jnp.sum(current * current / diag), ("gx", "gy"))

    direction = residual / diag
    norm_now = residual_norm(residual)
    for step in range(ITERS):
        terms = element_forces(stiff, stack_corners(widen(free * direction))) * scale_wide[None]
        image = free * spread_nodes(terms)[:, :, 1:-1, 1:-1] + (1.0 - free) * direction
        alpha = norm_now / lax.psum(jnp.sum(direction * image), ("gx", "gy"))
        displacement = displacement + alpha * direction
        residual = residual - alpha * image
        if step + 1 < ITERS:
            norm_next = residual_norm(residual)
            direction = residual / diag + norm_next / norm_now * direction
            norm_now = norm_next
    stacked = stack_corners(widen(displacement)[:, :, 1:, 1:])
    energy = jnp.sum(stacked * element_forces(stiff, stacked), 0)
    return (displacement, -slope * energy)


def solution(mesh):
    return jax.shard_map(
        body,
        mesh=mesh,
        in_specs=(
            P(None, None, ("parts", "gx"), "gy"),
            P(None, ("parts", "gx"), "gy"),
            P(None, ("parts", "gx"), "gy"),
        ),
        out_specs=(P(None, None, ("parts", "gx"), "gy"), P(None, ("parts", "gx"), "gy")),
        check_vma=False,
    )
```

profile of v0, /device:TPU:0, one launch (start us, length us, event | category | flops | bytes accessed | tf_op | source)
XLA Modules:
  0.0 204.9 jit_solution(14656841411601756886)
XLA Ops:
  0.6 0.8 select_add_fusion
  1.5 3.1 %collective-permute-start = (f32[16,1,128]{2,1,0:T(1,128)S(1)}, f32[16,1,128]{2,1,0:T(1,128)S(1)}, u32[]{:S(2)}, u32[]{:S(2)}) collective-permute-start(f32[16,1,128]{2,1,0:T(1,128)S(1)} %slice.292), channel_id=1, source_target_pairs={{0,4},{4,8},{8,12},{12,0},{1,5},{5,9},{9,13},{13,1},{2,6},{6,10},{... | collective-permute-start | bytes 24584 | tf_op jit(solution)/shard_map/ppermute | solution.py:35
  4.6 0.9 subtract_convert_fusion
  5.5 0.9 broadcast_subtract_fusion
  6.3 1.9 collective-permute-done
  8.4 1.5 gather_fusion
  9.9 2.1 %collective-permute-done.1 = f32[16,7,1]{2,1,0:T(8,128)S(1)} collective-permute-done((f32[16,7,1]{2,1,0:T(8,128)S(1)}, f32[16,7,1]{2,1,0:T(8,128)S(1)}, u32[]{:S(2)}, u32[]{:S(2)}) %collective-permute-start.1) | collective-permute-done | bytes 480 | tf_op jit(solution)/shard_map/ppermute | solution.py:35
  14.2 0.9 fusion.28
  15.9 3.8 %collective-permute-start.3 = (f32[3,17,1,128]{3,2,1,0:T(1,128)S(1)}, f32[3,17,1,128]{3,2,1,0:T(1,128)S(1)}, u32[]{:S(2)}, u32[]{:S(2)}) collective-permute-start(f32[3,17,1,128]{3,2,1,0:T(1,128)S(1)} %get-tuple-element.62), channel_id=1, source_target_pairs={{4,0},{8,4},{12,8},{0,12},{5,1},{9,5},{13,9},{1,13},{6,2},{10,6},{... | collective-permute-start | bytes 78344 | tf_op jit(solution)/shard_map/ppermute | solution.py:26
  19.7 1.8 collective-permute-done.2
  22.3 3.8 %collective-permute-done.5 = f32[3,17,8,1]{3,2,1,0:T(8,128)S(1)} collective-permute-done((f32[3,17,8,1]{3,2,1,0:T(8,128)S(1)}, f32[3,17,8,1]{3,2,1,0:T(8,128)S(1)}, u32[]{:S(2)}, u32[]{:S(2)}) %collective-permute-start.5) | collective-permute-done | bytes 1664 | tf_op jit(solution)/shard_map/ppermute | solution.py:26
  26.1 3.0 %collective-permute-done.4 = f32[3,17,8,1]{3,2,1,0:T(8,128)S(1)} collective-permute-done((f32[3,17,8,1]{3,2,1,0:T(8,128)S(1)}, f32[3,17,8,1]{3,2,1,0:T(8,128)S(1)}, u32[]{:S(2)}, u32[]{:S(2)}) %collective-permute-start.4) | collective-permute-done | bytes 1664 | tf_op jit(solution)/shard_map/ppermute | solution.py:24
  29.6 0.8 slice_dynamic-update-slice_fusion.15
  31.1 0.8 slice_dynamic-update-slice_fusion.13
  31.9 0.8 slice_dynamic-update-slice_fusion.12
  32.7 0.8 slice_dynamic-update-slice_fusion.11
  33.5 0.8 slice_dynamic-update-slice_fusion.10
  34.3 0.8 slice_dynamic-update-slice_fusion.9
  35.1 0.8 slice_dynamic-update-slice_fusion.8
  35.9 2.9 %reshape.34 = f32[24,14448]{1,0:T(8,128)S(1)} reshape(f32[24,16,7,129]{3,2,1,0:T(8,128)} %slice_dynamic-update-slice_fusion.8) | data formatting | bytes 2774016 | tf_op jit(solution)/shard_map/reshape | solution.py:103
  38.7 2.4 %fusion.43 = f32[24,14448]{1,0:T(8,128)} fusion(f32[24,24]{1,0:T(8,128)S(1)} %copy-done, f32[24,14448]{1,0:T(8,128)S(1)} %reshape.34), kind=kOutput, calls=%fused_computation.107 | convolution fusion | flops 99864576 | bytes 2776320 | tf_op jit(solution)/shard_map/dot_general | solution.py:103
  41.1 4.4 %reshape.35 = f32[24,16,7,129]{3,2,1,0:T(8,128)S(1)} reshape(f32[24,14448]{1,0:T(8,128)} %fusion.43) | data formatting | bytes 2774016 | tf_op jit(solution)/shard_map/reshape | solution.py:104
  45.5 1.2 broadcast_multiply_fusion.1
  47.7 1.0 multiply_reduce_fusion.1
  48.7 32.6 %all-reduce.24 = (f32[]{:T(128)}, f32[]{:T(128)}) all-reduce(f32[]{:T(128)} %get-tuple-element.14, f32[]{:T(128)} %get-tuple-element.12), channel_id=1, replica_groups=mesh['parts'=2,'gx'=4,'gy'=4] {'gx','gy'}, use_global_device_ids=true, to_apply=%region_1.2 | all-reduce | flops 2 | bytes 16 | tf_op jit(solution)/shard_map/psum | solution.py:128
  83.2 30.1 %psum.30 = f32[]{:T(128)} all-reduce(f32[]{:T(128)} %fusion.29), channel_id=1, replica_groups=mesh['parts'=2,'gx'=4,'gy'=4] {'gx','gy'}, use_global_device_ids=true, to_apply=%region_5.6 | all-reduce | flops 1 | bytes 8 | tf_op jit(solution)/shard_map/psum | solution.py:128
  115.5 3.8 %collective-permute-start.7 = (f32[3,17,1,128]{3,2,1,0:T(1,128)S(1)}, f32[3,17,1,128]{3,2,1,0:T(1,128)S(1)}, u32[]{:S(2)}, u32[]{:S(2)}) collective-permute-start(f32[3,17,1,128]{3,2,1,0:T(1,128)S(1)} %get-tuple-element.58), channel_id=1, source_target_pairs={{4,0},{8,4},{12,8},{0,12},{5,1},{9,5},{13,9},{1,13},{6,2},{10,6},{... | collective-permute-start | bytes 78344 | tf_op jit(solution)/shard_map/ppermute | solution.py:26
  119.3 1.8 collective-permute-done.6
  121.9 4.9 %collective-permute-done.9 = f32[3,17,8,1]{3,2,1,0:T(8,128)S(1)} collective-permute-done((f32[3,17,8,1]{3,2,1,0:T(8,128)S(1)}, f32[3,17,8,1]{3,2,1,0:T(8,128)S(1)}, u32[]{:S(2)}, u32[]{:S(2)}) %collective-permute-start.9) | collective-permute-done | bytes 1664 | tf_op jit(solution)/shard_map/ppermute | solution.py:26
  126.8 1.0 collective-permute-done.8
  129.7 0.8 slice_dynamic-update-slice_fusion.5
  130.5 0.8 slice_dynamic-update-slice_fusion.4
  131.3 0.8 slice_dynamic-update-slice_fusion.3
  132.0 0.8 slice_dynamic-update-slice_fusion.2
  132.8 0.8 slice_dynamic-update-slice_fusion.1
  133.6 0.8 slice_dynamic-update-slice_fusion
  134.4 2.9 %reshape.36 = f32[24,14448]{1,0:T(8,128)S(1)} reshape(f32[24,16,7,129]{3,2,1,0:T(8,128)} %slice_dynamic-update-slice_fusion) | data formatting | bytes 2774016 | tf_op jit(solution)/shard_map/reshape | solution.py:103
  137.3 2.3 %fusion.44 = f32[24,14448]{1,0:T(8,128)} fusion(f32[24,24]{1,0:T(8,128)S(1)} %copy-done, f32[24,14448]{1,0:T(8,128)S(1)} %reshape.36), kind=kOutput, calls=%fused_computation.108 | convolution fusion | flops 99864576 | bytes 2776320 | tf_op jit(solution)/shard_map/dot_general | solution.py:103
  139.6 4.4 %reshape.37 = f32[24,16,7,129]{3,2,1,0:T(8,128)S(1)} reshape(f32[24,14448]{1,0:T(8,128)} %fusion.44) | data formatting | bytes 2774016 | tf_op jit(solution)/shard_map/reshape | solution.py:104
  145.2 0.9 fusion.30
  146.1 34.4 %psum.31 = f32[]{:T(128)} all-reduce(f32[]{:T(128)} %fusion.30), channel_id=1, replica_groups=mesh['parts'=2,'gx'=4,'gy'=4] {'gx','gy'}, use_global_device_ids=true, to_apply=%region_7.8 | all-reduce | flops 1 | bytes 8 | tf_op jit(solution)/shard_map/psum | solution.py:135
  182.0 3.8 %collective-permute-start.11 = (f32[3,17,1,128]{3,2,1,0:T(1,128)S(1)}, f32[3,17,1,128]{3,2,1,0:T(1,128)S(1)}, u32[]{:S(2)}, u32[]{:S(2)}) collective-permute-start(f32[3,17,1,128]{3,2,1,0:T(1,128)S(1)} %get-tuple-element.54), channel_id=1, source_target_pairs={{4,0},{8,4},{12,8},{0,12},{5,1},{9,5},{13,9},{1,13},{6,2},{10,6},{... | collective-permute-start | bytes 78344 | tf_op jit(solution)/shard_map/ppermute | solution.py:26
  185.8 1.8 collective-permute-done.10
  187.8 3.3 %collective-permute-done.12 = f32[3,17,8,1]{3,2,1,0:T(8,128)S(1)} collective-permute-done((f32[3,17,8,1]{3,2,1,0:T(8,128)S(1)}, f32[3,17,8,1]{3,2,1,0:T(8,128)S(1)}, u32[]{:S(2)}, u32[]{:S(2)}) %collective-permute-start.12) | collective-permute-done | bytes 1664 | tf_op jit(solution)/shard_map/ppermute | solution.py:26
  194.4 1.2 copy-done.9
  195.5 1.7 reshape.38
  197.3 1.1 fusion.45
  199.4 4.5 %concatenate.102 = f32[24,12288]{1,0:T(8,128)S(1)} concatenate(f32[3,12288]{1,0:T(4,128)} %concatenate.91, f32[3,12288]{1,0:T(4,128)S(1)} %concatenate.94, f32[3,12288]{1,0:T(4,128)S(1)} %concatenate.96, f32[3,12288]{1,0:T(4,128)S(1)} %concatenate.97, f32[3,12288]{1,0:T(4,128)} %concatenate.98, f32[3,12288]{1,0:T(4,128)S(1)} %concatenate.99, f32[3,12288]{1,0:T(4,128)} %concatenate.100, ...), dimensions={0} | concatenate | bytes 2359296 | tf_op jit(solution)/shard_map/concatenate | solution.py:87
  (82 shorter events, 16.6 us)
Async XLA Ops:
  1.5 6.7 %collective-permute-start = (f32[16,1,128]{2,1,0:T(1,128)S(1)}, f32[16,1,128]{2,1,0:T(1,128)S(1)}, u32[]{:S(2)}, u32[]{:S(2)}) collective-permute-start(f32[16,1,128]{2,1,0:T(1,128)S(1)} %slice.292), channel_id=1, source_target_pairs={{0,4},{4,8},{8,12},{12,0},{1,5},{5,9},{9,13},{13,1},{2,6},{6,10},{... | collective-permute-start | bytes 24584 | tf_op jit(solution)/shard_map/ppermute | solution.py:35
  8.3 3.7 %collective-permute-start.1 = (f32[16,7,1]{2,1,0:T(8,128)S(1)}, f32[16,7,1]{2,1,0:T(8,128)S(1)}, u32[]{:S(2)}, u32[]{:S(2)}) collective-permute-start(f32[16,7,1]{2,1,0:T(8,128)S(1)} %pad_maximum_fusion.8), channel_id=1, source_target_pairs={{0,1},{1,2},{2,3},{3,0},{4,5},{5,6},{6,7},{7,4},{8,9},{9,10},{10,1... | collective-permute-start | bytes 1352 | tf_op jit(solution)/shard_map/ppermute | solution.py:35
  12.2 0.7 copy-start.7
  13.2 0.9 copy-start.2
  15.1 17.6 %copy-start.5 = (f32[3,17,6,128]{3,2,1,0:T(8,128)}, f32[3,17,6,128]{3,2,1,0:T(8,128)S(1)}, u32[]{:S(2)}) copy-start(f32[3,17,6,128]{3,2,1,0:T(8,128)S(1)} %get-tuple-element.15) | copy-start | bytes 470020
  15.9 5.7 %collective-permute-start.2 = (f32[3,17,1,128]{3,2,1,0:T(1,128)S(1)}, f32[3,17,1,128]{3,2,1,0:T(1,128)S(1)}, u32[]{:S(2)}, u32[]{:S(2)}) collective-permute-start(f32[3,17,1,128]{3,2,1,0:T(1,128)S(1)} %get-tuple-element.61), channel_id=1, source_target_pairs={{0,4},{4,8},{8,12},{12,0},{1,5},{5,9},{9,13},{13,1},{2,6},{6,10},{... | collective-permute-start | bytes 78344 | tf_op jit(solution)/shard_map/ppermute | solution.py:24
  15.9 5.6 %collective-permute-start.3 = (f32[3,17,1,128]{3,2,1,0:T(1,128)S(1)}, f32[3,17,1,128]{3,2,1,0:T(1,128)S(1)}, u32[]{:S(2)}, u32[]{:S(2)}) collective-permute-start(f32[3,17,1,128]{3,2,1,0:T(1,128)S(1)} %get-tuple-element.62), channel_id=1, source_target_pairs={{4,0},{8,4},{12,8},{0,12},{5,1},{9,5},{13,9},{1,13},{6,2},{10,6},{... | collective-permute-start | bytes 78344 | tf_op jit(solution)/shard_map/ppermute | solution.py:26
  21.8 4.4 %collective-permute-start.5 = (f32[3,17,8,1]{3,2,1,0:T(8,128)S(1)}, f32[3,17,8,1]{3,2,1,0:T(8,128)S(1)}, u32[]{:S(2)}, u32[]{:S(2)}) collective-permute-start(f32[3,17,8,1]{3,2,1,0:T(8,128)S(1)} %get-tuple-element.59), channel_id=1, source_target_pairs={{1,0},{2,1},{3,2},{0,3},{5,4},{6,5},{7,6},{4,7},{9,8},{10,9},{11,1... | collective-permute-start | bytes 4904 | tf_op jit(solution)/shard_map/ppermute | solution.py:26
  21.8 7.3 %collective-permute-start.4 = (f32[3,17,8,1]{3,2,1,0:T(8,128)S(1)}, f32[3,17,8,1]{3,2,1,0:T(8,128)S(1)}, u32[]{:S(2)}, u32[]{:S(2)}) collective-permute-start(f32[3,17,8,1]{3,2,1,0:T(8,128)S(1)} %get-tuple-element.60), channel_id=1, source_target_pairs={{0,1},{1,2},{2,3},{3,0},{4,5},{5,6},{6,7},{7,4},{8,9},{9,10},{10,1... | collective-permute-start | bytes 4904 | tf_op jit(solution)/shard_map/ppermute | solution.py:24
  34.3 4.5 %copy-start = (f32[24,24]{1,0:T(8,128)S(1)}, f32[24,24]{1,0:T(8,128)}, u32[]{:S(2)}) copy-start(f32[24,24]{1,0:T(8,128)} %constant.13.clone) | copy-start | bytes 6916
  46.7 0.9 copy-start.3
  47.0 35.6 %copy-start.6 = (f32[3,17,6,128]{3,2,1,0:T(8,128)S(1)}, f32[3,17,6,128]{3,2,1,0:T(8,128)}, u32[]{:S(2)}) copy-start(f32[3,17,6,128]{3,2,1,0:T(8,128)} %copy-done.5) | copy-start | bytes 470020
  115.4 5.7 %collective-permute-start.6 = (f32[3,17,1,128]{3,2,1,0:T(1,128)S(1)}, f32[3,17,1,128]{3,2,1,0:T(1,128)S(1)}, u32[]{:S(2)}, u32[]{:S(2)}) collective-permute-start(f32[3,17,1,128]{3,2,1,0:T(1,128)S(1)} %get-tuple-element.57), channel_id=1, source_target_pairs={{0,4},{4,8},{8,12},{12,0},{1,5},{5,9},{9,13},{13,1},{2,6},{6,10},{... | collective-permute-start | bytes 78344 | tf_op jit(solution)/shard_map/ppermute | solution.py:24
  115.5 5.6 %collective-permute-start.7 = (f32[3,17,1,128]{3,2,1,0:T(1,128)S(1)}, f32[3,17,1,128]{3,2,1,0:T(1,128)S(1)}, u32[]{:S(2)}, u32[]{:S(2)}) collective-permute-start(f32[3,17,1,128]{3,2,1,0:T(1,128)S(1)} %get-tuple-element.58), channel_id=1, source_target_pairs={{4,0},{8,4},{12,8},{0,12},{5,1},{9,5},{13,9},{1,13},{6,2},{10,6},{... | collective-permute-start | bytes 78344 | tf_op jit(solution)/shard_map/ppermute | solution.py:26
  121.3 5.4 %collective-permute-start.9 = (f32[3,17,8,1]{3,2,1,0:T(8,128)S(1)}, f32[3,17,8,1]{3,2,1,0:T(8,128)S(1)}, u32[]{:S(2)}, u32[]{:S(2)}) collective-permute-start(f32[3,17,8,1]{3,2,1,0:T(8,128)S(1)} %get-tuple-element.55), channel_id=1, source_target_pairs={{1,0},{2,1},{3,2},{0,3},{5,4},{6,5},{7,6},{4,7},{9,8},{10,9},{11,1... | collective-permute-start | bytes 4904 | tf_op jit(solution)/shard_map/ppermute | solution.py:26
  121.4 6.3 %collective-permute-start.8 = (f32[3,17,8,1]{3,2,1,0:T(8,128)S(1)}, f32[3,17,8,1]{3,2,1,0:T(8,128)S(1)}, u32[]{:S(2)}, u32[]{:S(2)}) collective-permute-start(f32[3,17,8,1]{3,2,1,0:T(8,128)S(1)} %get-tuple-element.56), channel_id=1, source_target_pairs={{0,1},{1,2},{2,3},{3,0},{4,5},{5,6},{6,7},{7,4},{8,9},{9,10},{10,1... | collective-permute-start | bytes 4904 | tf_op jit(solution)/shard_map/ppermute | solution.py:24
  137.3 6.8 %copy-start.8 = (f32[16,7,129]{2,1,0:T(8,128)S(1)}, f32[16,7,129]{2,1,0:T(8,128)}, u32[]{:S(2)}) copy-start(f32[16,7,129]{2,1,0:T(8,128)} %copy-done.7) | copy-start | bytes 173380
  144.3 0.9 copy-start.10
  144.5 37.3 %copy-start.4 = (f32[3,17,6,128]{3,2,1,0:T(8,128)S(1)}, f32[3,17,6,128]{3,2,1,0:T(8,128)}, u32[]{:S(2)}) copy-start(f32[3,17,6,128]{3,2,1,0:T(8,128)} %get-tuple-element.17) | copy-start | bytes 470020
  181.9 11.4 %copy-start.1 = (f32[3,17,6,128]{3,2,1,0:T(8,128)}, f32[3,17,6,128]{3,2,1,0:T(8,128)S(1)}, u32[]{:S(2)}) copy-start(f32[3,17,6,128]{3,2,1,0:T(8,128)S(1)} %multiply_add_fusion) | copy-start | bytes 470020
  181.9 5.7 %collective-permute-start.10 = (f32[3,17,1,128]{3,2,1,0:T(1,128)S(1)}, f32[3,17,1,128]{3,2,1,0:T(1,128)S(1)}, u32[]{:S(2)}, u32[]{:S(2)}) collective-permute-start(f32[3,17,1,128]{3,2,1,0:T(1,128)S(1)} %get-tuple-element.53), channel_id=1, source_target_pairs={{0,4},{4,8},{8,12},{12,0},{1,5},{5,9},{9,13},{13,1},{2,6},{6,10},{... | collective-permute-start | bytes 78344 | tf_op jit(solution)/shard_map/ppermute | solution.py:24
  182.0 5.6 %collective-permute-start.11 = (f32[3,17,1,128]{3,2,1,0:T(1,128)S(1)}, f32[3,17,1,128]{3,2,1,0:T(1,128)S(1)}, u32[]{:S(2)}, u32[]{:S(2)}) collective-permute-start(f32[3,17,1,128]{3,2,1,0:T(1,128)S(1)} %get-tuple-element.54), channel_id=1, source_target_pairs={{4,0},{8,4},{12,8},{0,12},{5,1},{9,5},{13,9},{1,13},{6,2},{10,6},{... | collective-permute-start | bytes 78344 | tf_op jit(solution)/shard_map/ppermute | solution.py:26
  187.7 3.4 %collective-permute-start.12 = (f32[3,17,8,1]{3,2,1,0:T(8,128)S(1)}, f32[3,17,8,1]{3,2,1,0:T(8,128)S(1)}, u32[]{:S(2)}, u32[]{:S(2)}) collective-permute-start(f32[3,17,8,1]{3,2,1,0:T(8,128)S(1)} %pad_maximum_fusion.3), channel_id=1, source_target_pairs={{1,0},{2,1},{3,2},{0,3},{5,4},{6,5},{7,6},{4,7},{9,8},{10,9},{11,1... | collective-permute-start | bytes 4904 | tf_op jit(solution)/shard_map/ppermute | solution.py:26
  194.4 1.2 copy-start.9
  199.1 5.0 %copy-start.11 = (s32[16,6,128]{2,0,1:T(8,128)S(1)}, s32[16,6,128]{2,0,1:T(8,128)}, u32[]{:S(2)}) copy-start(s32[16,6,128]{2,0,1:T(8,128)} %param.5) | copy-start | bytes 147460
where the time goes:
time: 206 us; the launch traced here: 205 us
  blocking collectives  97.1 us (47%)
  local copies, waits for them, and re-layouts  44.5 us (22%)
  waiting for transfers between devices  25.4 us (12%)
  starting transfers between devices  15.9 us (8%)
  other arithmetic  11.1 us (5%)
  matrix products  5.77 us (3%)
  between operations  5 us (2%)
    psum x2, blocking collectives, residual_norm(): return lax.psum(jnp.sum(current * current / diag), ('gx', 'gy'))  62.7 us
    psum x1, blocking collectives, body(): alpha = norm_now / lax.psum(jnp.sum(direction * image), ('gx', 'gy'))  34.4 us
    unnamed x44, local copies, waits for them, and re-layouts  15.8 us
    ppermute x6, waiting for transfers between devices, padded(): lax.ppermute(head, axis, [((i + 1) % count, i) for i in range(count)])  12 us
    ppermute x6, starting transfers between devices, padded(): lax.ppermute(head, axis, [((i + 1) % count, i) for i in range(count)])  11.6 us
    concatenate x12, local copies, waits for them, and re-layouts, stack_corners(): jnp.concatenate([wide[:, a:a + layers, b:b + span_x, c:c + span_y] for a,...  9.72 us
    ppermute x5, waiting for transfers between devices, padded(): lax.ppermute(tail, axis, [(i, (i + 1) % count) for i in range(count)])  9.43 us
    reshape x2, local copies, waits for them, and re-layouts, element_forces(): return flat.reshape(stacked.shape)  8.85 us
  transfers between devices with their start and end apart: 13, of which 10 were waited for; matrix products, arithmetic and copies ran while one was open for 2% of the time, Pallas kernels for 0%

commit v1 on v0

v1 whole, which is shorter than its diff:
```python
import functools

import jax
import jax.numpy as jnp
import numpy as np
from jax import lax
from jax.experimental import pallas as pl
from jax.experimental.pallas import tpu as pltpu
from jax.sharding import PartitionSpec as P

PHASE_STIFFNESS = (0.125, 0.343, 0.614, 1.0)
PHASE_SLOPE = (0.75, 1.47, 2.17, 3.0)
POISSON = 0.3
LAME = POISSON / ((1.0 + POISSON) * (1.0 - 2.0 * POISSON))
SHEAR = 1.0 / (2.0 * (1.0 + POISSON))
KE_DIAGONAL = (LAME + 4.0 * SHEAR) / 9.0

SLOT = 24
LANES = 128
FULL = 168
CORNERS = 152

VMEM = pl.BlockSpec(memory_space=pltpu.VMEM)
PARAMS = pltpu.CompilerParams(vmem_limit_bytes=32 * 1024 * 1024)


def lanes():
    return lax.broadcasted_iota(jnp.int32, (8, LANES), 1)


def sublanes():
    return lax.broadcasted_iota(jnp.int32, (8, LANES), 0)


def table(phase, values):
    out = jnp.full(phase.shape, values[3], jnp.float32)
    for index in (2, 1, 0):
        out = jnp.where(phase == index, jnp.float32(values[index]), out)
    return out


def lane_roll(x, by):
    if isinstance(by, int):
        by = by % LANES
        return x if by == 0 else pltpu.roll(x, by, 1)
    return pltpu.roll(x, lax.rem(by + LANES, LANES), 1)


def is_even(axis):
    return lax.rem(lax.axis_index(axis), 2) == 0


def pack_kernel(paired_x, paired_y, force, phase, fixed, col1, col2, row1, row2, pad):
    comps, nodes, rows, width = force.shape
    layers = nodes - 1
    lane = lanes()
    even_x = is_even("gx") if paired_x else True
    even_y = is_even("gy") if paired_y else True
    zero = jnp.zeros((8, LANES), jnp.float32)
    low = [zero, zero]
    high = [zero, zero]
    pad[...] = jnp.zeros(pad.shape, jnp.float32)

    def place(planes, tile, column, plane, slot, k):
        target = slot * SLOT + k
        planes[plane] = jnp.where(lane == target, lane_roll(tile, target - column), planes[plane])

    def put(at_low, at_high, value_low, value_high):
        if paired_x:
            if value_high is None:
                value_high = jnp.zeros((1, LANES), jnp.float32)
            row1[at_low : at_low + 1, :] = jnp.where(even_x, value_high, value_low)
            row2[at_low : at_low + 1, :] = jnp.where(even_x, value_low, value_high)
        else:
            row1[at_low : at_low + 1, :] = value_low
            row2[at_low : at_low + 1, :] = jnp.zeros((1, LANES), jnp.float32) if value_high is None else value_high

    for k in range(nodes):
        free = (1 - fixed[k]).astype(jnp.float32)
        for c in range(comps):
            q = c * nodes + k
            r0 = free * force[c, k]
            pad[q, 0:rows, :] = r0
            tile = pad[q]
            place(low, tile, 0, 0, c, k)
            place(low, tile, 1, 1, c, k)
            place(high, tile, width - 1, 0, c, k)
            put(q, q, r0[0:1], r0[rows - 1 : rows])
            put(comps * nodes + 2 * layers + q, None, r0[1:2], None)
        pad[comps * nodes, 0:rows, :] = free
        place(low, pad[comps * nodes], 0, 0, 3, k)
        put(2 * comps * nodes + 2 * layers + k, None, free[0:1], None)
        if k < layers:
            scale = table(phase[k], PHASE_STIFFNESS)
            pad[comps * nodes + 1, 0:rows, :] = scale
            tile = pad[comps * nodes + 1]
            place(low, tile, 0, 1, 3, k)
            place(low, tile, 1, 1, 4, k)
            place(high, tile, width - 2, 0, 3, k)
            place(high, tile, width - 1, 0, 4, k)
            put(comps * nodes + k, None, scale[0:1], scale[rows - 2 : rows - 1])
            put(comps * nodes + layers + k, None, scale[1:2], scale[rows - 1 : rows])
    used = 2 * comps * nodes + 2 * layers + nodes
    row1[used:, :] = jnp.zeros((FULL - used, LANES), jnp.float32)
    row2[used:, :] = jnp.zeros((FULL - used, LANES), jnp.float32)
    for plane in range(2):
        if paired_y:
            col1[plane] = jnp.where(even_y, high[plane], low[plane])
            col2[plane] = jnp.where(even_y, low[plane], high[plane])
        else:
            col1[plane] = low[plane]
            col2[plane] = high[plane]


def strip_kernel(paired_x, paired_y, own1, own2, got1, got2, row1, row2, strip, out1, out2):
    lane = lanes()
    even_x = is_even("gx") if paired_x else True
    even_y = is_even("gy") if paired_y else True
    if paired_y:
        own_low = [jnp.where(even_y, own2[p], own1[p]) for p in range(2)]
        own_high = [jnp.where(even_y, own1[p], own2[p]) for p in range(2)]
        from_low = [jnp.where(even_y, got2[p], got1[p]) for p in range(2)]
        from_high = [jnp.where(even_y, got1[p], got2[p]) for p in range(2)]
    else:
        own_low, own_high = [own1[p] for p in range(2)], [own2[p] for p in range(2)]
        from_low, from_high = [got2[p] for p in range(2)], [got1[p] for p in range(2)]

    def build(*items):
        out = jnp.zeros((8, LANES), jnp.float32)
        for planes, plane, source, slot in items:
            inside = (lane >= slot * SLOT) & (lane < slot * SLOT + SLOT)
            out = jnp.where(inside, lane_roll(planes[plane], (slot - source) * SLOT), out)
        return out

    planes = [
        build(
            (from_low, 0, c, 0),
            (own_low, 0, c, 1),
            (own_high, 0, c, 2),
            (from_high, 0, c, 3),
            (from_high, 1, c, 4),
        )
        for c in range(3)
    ]
    planes.append(
        build((from_low, 0, 3, 0), (from_low, 0, 4, 1), (own_high, 0, 3, 2), (own_high, 0, 4, 3), (from_high, 1, 3, 4))
    )
    planes.append(
        build((from_low, 0, 4, 0), (own_low, 1, 3, 1), (own_high, 0, 4, 2), (from_high, 1, 3, 3), (from_high, 1, 4, 4))
    )
    planes.append(build((from_high, 0, 3, 3)))
    rows = 6
    out1[...] = row1[...]
    out2[...] = row2[...]
    for p, plane in enumerate(planes):
        strip[p] = plane
        for which in range(2):
            at = CORNERS + 2 * p + which
            low_row = plane[which : which + 1]
            high_row = plane[rows - 2 + which : rows - 1 + which]
            if paired_x:
                out1[at : at + 1, :] = jnp.where(even_x, high_row, low_row)
                out2[at : at + 1, :] = jnp.where(even_x, low_row, high_row)
            else:
                out1[at : at + 1, :] = low_row
                out2[at : at + 1, :] = high_row


PLANE = ("", "1", "2", "12")


def split_layers(lo, hi):
    sums = [{m: lo[c][m] + hi[c][m] for m in ("1", "2", "12")} for c in range(3)]
    diffs = [{m: hi[c][m] - lo[c][m] for m in PLANE} for c in range(3)]
    u, v, w = range(3)
    return (
        diffs[u][""], sums[v]["1"], sums[w]["2"],
        sums[u]["1"] + diffs[v][""], sums[u]["2"] + diffs[w][""], sums[v]["2"] + sums[w]["1"],
        diffs[u]["1"], sums[w]["12"], diffs[u]["2"], sums[v]["12"], diffs[v]["1"], diffs[w]["2"],
        sums[u]["12"], diffs[v]["2"], diffs[w]["1"],
        diffs[u]["12"], diffs[v]["12"], diffs[w]["12"],
    )


def stress(m):
    one, two, three = 1.0 / 16.0, 1.0 / 48.0, 1.0 / 144.0
    trace = (LAME * one) * (m[0] + m[1] + m[2])
    out = [trace + (2.0 * SHEAR * one) * m[i] for i in range(3)]
    out += [(SHEAR * one) * m[i] for i in (3, 4, 5)]
    own, other = (LAME + 3.0 * SHEAR) * two, LAME * two
    for i in (6, 8, 10):
        out += [own * m[i] + other * m[i + 1], own * m[i + 1] + other * m[i]]
    total = m[12] + m[13] + m[14]
    out += [(SHEAR * two) * (m[i] + total) for i in (12, 13, 14)]
    out += [((LAME + 4.0 * SHEAR) * three) * m[i] for i in (15, 16, 17)]
    return out


def inner(g, m):
    parts = [g[i] * m[i] for i in range(18)]
    while len(parts) > 1:
        parts = [parts[i] + parts[i + 1] if i + 1 < len(parts) else parts[i] for i in range(0, len(parts), 2)]
    return parts[0]


def join_layers(g):
    sums = [
        {"1": g[3], "2": g[4], "12": g[12]},
        {"1": g[1], "2": g[5], "12": g[9]},
        {"1": g[5], "2": g[2], "12": g[7]},
    ]
    diffs = [
        {"": g[0], "1": g[6], "2": g[8], "12": g[15]},
        {"": g[3], "1": g[10], "2": g[13], "12": g[16]},
        {"": g[4], "1": g[14], "2": g[11], "12": g[17]},
    ]
    lower = [{m: (sums[c][m] - diffs[c][m] if m else -diffs[c][m]) for m in PLANE} for c in range(3)]
    upper = [{m: (sums[c][m] + diffs[c][m] if m else diffs[c][m]) for m in PLANE} for c in range(3)]
    return lower, upper


def in_plane(x, right, up):
    y = right(x)
    near, far = x + y, y - x
    near_up, far_up = up(near), up(far)
    return {"": near + near_up, "1": near_up - near, "2": far + far_up, "12": far_up - far}


def out_of_plane(f, right, up):
    plain = (f[""] - f["2"]) + right(f[""] + f["2"])
    steep = (f["1"] - f["12"]) + right(f["1"] + f["12"])
    return (plain - steep) + up(plain + steep)


def operator_kernel(
    paired_x, force, phase, fixed, strip, got1, got2,
    base, second, energy, sums,
    lo, hi, held, modes, residual, inverse,
):
    comps, nodes, rows, width = force.shape
    layers = nodes - 1
    lane, row = lanes(), sublanes()
    last_row, below = row == 6, row == 7
    cn = comps * nodes
    if paired_x:
        even_x = is_even("gx")
        lo[...] = jnp.where(even_x, got2[...], got1[...])
        hi[...] = jnp.where(even_x, got1[...], got2[...])
    else:
        lo[...] = got2[...]
        hi[...] = got1[...]

    def spread(ref, at):
        return jnp.broadcast_to(ref[pl.ds(at, 1), :], (8, LANES))

    def roll_up(x):
        return pltpu.roll(x, 7, 0)

    def roll_down(x):
        return pltpu.roll(x, 1, 0)

    def corner(ref, p, which):
        return spread(ref, CORNERS + 2 * p + which)

    tiles = [
        jnp.where(row < 6, strip[p], jnp.where(last_row, corner(hi, p, 0), corner(lo, p, 1))) for p in range(6)
    ]
    sevens = [corner(hi, p, 1) for p in range(5)]
    left, right = tiles[3], tiles[4]
    around = left + right
    around_7 = sevens[3] + sevens[4]
    around_m2 = corner(lo, 3, 0) + corner(lo, 4, 0)

    def node_rows(x, x_m2):
        return x + jnp.where(below, x_m2, roll_down(x))

    def node_row_7(x, x_7):
        return jnp.broadcast_to(x[6:7], (8, LANES)) + x_7

    def strip_diagonal(x):
        return KE_DIAGONAL * (x + lane_roll(x, 1))

    strip_diag = strip_diagonal(node_rows(around, around_m2))
    strip_diag_7 = strip_diagonal(node_row_7(around, around_7))
    strip_inv = jnp.where(strip_diag > 0.0, 1.0 / strip_diag, 0.0)
    strip_inv_7 = jnp.where(strip_diag_7 > 0.0, 1.0 / strip_diag_7, 0.0)
    strip_base = [tiles[c] * strip_inv for c in range(3)]
    strip_base_7 = [sevens[c] * strip_inv_7 for c in range(3)]
    edge_rows = node_rows(right, corner(lo, 4, 0))
    edge_rows_7 = node_row_7(right, sevens[4])

    slot = lane // SLOT
    live = (slot == 0) | (slot == 2) | (slot == 3)
    strip_scale = jnp.where(live, right, 0.0)

    def strip_modes(c):
        x, x_7 = strip_base[c], strip_base_7[c]
        near, near_7 = x + lane_roll(x, -SLOT), x_7 + lane_roll(x_7, -SLOT)
        far, far_7 = lane_roll(x, -SLOT) - x, lane_roll(x_7, -SLOT) - x_7
        near_up = jnp.where(last_row, near_7, roll_up(near))
        far_up = jnp.where(last_row, far_7, roll_up(far))
        return {"": near + near_up, "1": near_up - near, "2": far + far_up, "12": far_up - far}

    lower = [strip_modes(c) for c in range(3)]
    upper = [{m: lane_roll(lower[c][m], -1) for m in PLANE} for c in range(3)]
    g = [strip_scale * x for x in stress(split_layers(lower, upper))]
    f_low, f_up = join_layers(g)
    f_strip = []
    for c in range(3):
        f = {m: f_low[c][m] + lane_roll(f_up[c][m], 1) for m in PLANE}
        f_strip.append(out_of_plane(f, lambda x: lane_roll(x, SLOT), roll_down))
    strip_second = [jnp.where(tiles[5] > 0.0, (f_strip[c] - tiles[c]) * strip_inv, 0.0) for c in range(3)]

    def scale_of(k):
        held[0, 0:rows, :] = table(phase[k], PHASE_STIFFNESS)
        held[0, 6:7, :] = hi[pl.ds(cn + k, 1), :]
        held[0, 7:8, :] = lo[pl.ds(cn + layers + k, 1), :]
        return held[0], spread(hi, cn + layers + k), spread(lo, cn + k)

    def box(k):
        x, x_7, x_m2 = scale_of(k)
        r, r_7 = node_rows(x, x_m2), node_row_7(x, x_7)
        r = r + jnp.where(lane == 0, lane_roll(edge_rows, -k), lane_roll(r, 1))
        r_7 = r_7 + jnp.where(lane == 0, lane_roll(edge_rows_7, -k), lane_roll(r_7, 1))
        return x, r, r_7

    def first_layer(k, around_node, around_node_7):
        inv = 1.0 / (KE_DIAGONAL * around_node)
        inv_7 = 1.0 / (KE_DIAGONAL * around_node_7)
        inverse[k] = inv
        out = []
        free = (1 - fixed[k]).astype(jnp.float32)
        for c in range(3):
            q = c * nodes + k
            residual[q, 0:rows, :] = free * force[c, k]
            residual[q, 6:7, :] = hi[pl.ds(q, 1), :]
            residual[q, 7:8, :] = lo[pl.ds(q, 1), :]
            x = residual[q] * inv
            x_7 = spread(hi, cn + 2 * layers + q) * inv_7
            base[c, k] = x[0:rows]
            shift = LANES - 1 - (3 * SLOT + k)
            at_end = lane == LANES - 1
            y = jnp.where(at_end, lane_roll(strip_base[c], shift), lane_roll(x, -1))
            y_7 = jnp.where(at_end, lane_roll(strip_base_7[c], shift), lane_roll(x_7, -1))
            near, far, near_7, far_7 = x + y, y - x, x_7 + y_7, y_7 - x_7
            near_up = jnp.where(last_row, near_7, roll_up(near))
            far_up = jnp.where(last_row, far_7, roll_up(far))
            out.append({"": near + near_up, "1": near_up - near, "2": far + far_up, "12": far_up - far})
        return out

    def finish_layer(k, f, totals):
        inv = inverse[k]
        held[1, 0:rows, :] = 1.0 - fixed[k].astype(jnp.float32)
        held[1, 6:7, :] = hi[pl.ds(2 * cn + 2 * layers + k, 1), :]
        free = held[1] > 0.0
        a, b, d = totals
        for c in range(3):
            q = c * nodes + k
            r0 = residual[q]
            image = out_of_plane(f[c], lambda x: jnp.where(lane == 0, 0.0, lane_roll(x, 1)), roll_down)
            image = image + jnp.where(lane == 0, lane_roll(f_strip[c], -(SLOT + k)), 0.0)
            d0 = jnp.where(free, r0 * inv, r0)
            s = jnp.where(free, image, d0) - r0
            v = jnp.where(free, s * inv, s)
            second[c, k] = v[0:rows]
            residual[q] = v
            a, b, d = a + r0 * d0, b + d0 * s, d + s * v
        return a, b, d

    def store_energy(which, k, value):
        energy[which, k] = -table(phase[k], PHASE_SLOPE) * value[0:rows]

    def flat(x):
        return tuple(x[c][m] for c in range(3) for m in PLANE)

    def unflat(x):
        return [{m: x[4 * c + i] for i, m in enumerate(PLANE)} for c in range(3)]

    zero = jnp.zeros((8, LANES), jnp.float32)
    held[1] = zero
    scale_0, box_0, box_0_7 = box(0)
    start = first_layer(0, box_0, box_0_7)

    def element(k, low_modes, high_modes, scale, pending, totals):
        m = split_layers(low_modes, high_modes)
        g = stress(m)
        store_energy(0, k, inner(g, m))
        for i in range(18):
            modes[k, i] = m[i]
        f_lower, f_upper = join_layers([scale * x for x in g])
        done = [{m: pending[c][m] + f_lower[c][m] for m in PLANE} for c in range(3)]
        return f_upper, finish_layer(k, done, totals)

    def forward(k, carry):
        low_modes, pending, totals, scale, b, b_7 = carry
        next_scale, next_b, next_b_7 = box(k + 1)
        high = first_layer(k + 1, b + next_b, b_7 + next_b_7)
        f_upper, totals = element(k, unflat(low_modes), high, scale, unflat(pending), totals)
        return flat(high), flat(f_upper), totals, next_scale, next_b, next_b_7

    carry = (flat(start), (zero,) * 12, (zero,) * 3, scale_0, box_0, box_0_7)
    low_modes, pending, totals, scale, b, b_7 = lax.fori_loop(0, layers - 1, forward, carry)
    high = first_layer(layers, b, b_7)
    f_upper, totals = element(layers - 1, unflat(low_modes), high, scale, unflat(pending), totals)
    totals = finish_layer(layers, f_upper, totals)

    def second_layer(k):
        out = []
        for c in range(3):
            fill = lane_roll(strip_second[c], LANES - 1 - (3 * SLOT + k))
            x = residual[c * nodes + k]
            out.append(in_plane(x, lambda t: jnp.where(lane == LANES - 1, fill, lane_roll(t, -1)), roll_up))
        return out

    def again(k, carry):
        low_modes, total = carry
        high = second_layer(k + 1)
        m = split_layers(unflat(low_modes), high)
        g = stress(m)
        own = inner(g, m)
        store_energy(2, k, own)
        store_energy(1, k, inner(g, [modes[k, i] for i in range(18)]))
        scale = table(phase[k], PHASE_STIFFNESS)
        held[2, 0:rows, :] = scale * own[0:rows]
        return flat(high), total + held[2]

    held[2] = zero
    _, total = lax.fori_loop(0, layers, again, (flat(second_layer(0)), zero))
    for i, x in enumerate(totals + (total,)):
        x = jnp.where(row < rows, x, 0.0)
        x = jnp.sum(jnp.sum(x, axis=0, keepdims=True), axis=1, keepdims=True)
        sums[i : i + 1, :] = jnp.broadcast_to(x, (1, LANES))
    sums[4:, :] = jnp.zeros((4, LANES), jnp.float32)


def combine_kernel(base, second, energy, sums, displacement, sensitivity):
    a, b, d, e = (sums[i : i + 1, :] for i in range(4))
    ratio = b / a
    curve = a + b
    alpha = a / curve
    rest = d - b * ratio
    bend = e - 2.0 * ratio * (b + d) + ratio * ratio * curve
    alpha_next = rest / (bend - rest * rest / curve)
    beta = alpha * alpha * rest / a
    first = alpha + alpha_next * beta + alpha * alpha_next * ratio
    other = -alpha * alpha_next
    displacement[...] = first * base[...] + other * second[...]
    sensitivity[...] = (first * first) * energy[0] + (2.0 * first * other) * energy[1] + (other * other) * energy[2]


def exchange(one, two, axis):
    count = lax.axis_size(axis)
    if count % 2 == 0:
        far = lax.ppermute(two, axis, [(i, (i - 1) % count if i % 2 == 0 else (i + 1) % count) for i in range(count)])
        near = lax.ppermute(one, axis, [(i, i ^ 1) for i in range(count)])
        return near, far
    high = lax.ppermute(one, axis, [((i + 1) % count, i) for i in range(count)])
    low = lax.ppermute(two, axis, [(i, (i + 1) % count) for i in range(count)])
    return high, low


def total_over(x, axis):
    count = lax.axis_size(axis)
    if count & (count - 1):
        return lax.psum(x, axis)
    step = 1
    while step < count:
        x = x + lax.ppermute(x, axis, [(i, i ^ step) for i in range(count)])
        step *= 2
    return x


def body(force, phase, fixed):
    comps, nodes, rows, width = force.shape
    layers = nodes - 1
    f32 = jnp.float32
    paired_x = lax.axis_size("gx") % 2 == 0
    paired_y = lax.axis_size("gy") % 2 == 0
    column = jax.ShapeDtypeStruct((2, 8, LANES), f32)
    message = jax.ShapeDtypeStruct((FULL, LANES), f32)

    def call(kernel, out_shape, scratch=()):
        return pl.pallas_call(
            kernel,
            out_shape=out_shape,
            scratch_shapes=scratch,
            compiler_params=PARAMS,
        )

    col1, col2, row1, row2 = call(
        functools.partial(pack_kernel, paired_x, paired_y),
        (column, column, message, message),
        [pltpu.VMEM((comps * nodes + 2, 8, LANES), f32)],
    )(force, phase, fixed)
    near, far = exchange(col1, col2, "gy")
    strip, row1, row2 = call(
        functools.partial(strip_kernel, paired_x, paired_y),
        (jax.ShapeDtypeStruct((6, 8, LANES), f32), message, message),
    )(col1, col2, near, far, row1, row2)
    near, far = exchange(row1, row2, "gx")
    base, second, energy, sums = call(
        functools.partial(operator_kernel, paired_x),
        (
            jax.ShapeDtypeStruct(force.shape, f32),
            jax.ShapeDtypeStruct(force.shape, f32),
            jax.ShapeDtypeStruct((3,) + phase.shape, f32),
            jax.ShapeDtypeStruct((8, LANES), f32),
        ),
        [
            pltpu.VMEM((FULL, LANES), f32),
            pltpu.VMEM((FULL, LANES), f32),
            pltpu.VMEM((3, 8, LANES), f32),
            pltpu.VMEM((layers, 18, 8, LANES), f32),
            pltpu.VMEM((comps * nodes, 8, LANES), f32),
            pltpu.VMEM((nodes, 8, LANES), f32),
        ],
    )(force, phase, fixed, strip, near, far)
    sums = total_over(total_over(sums, "gy"), "gx")
    return call(
        combine_kernel,
        (jax.ShapeDtypeStruct(force.shape, f32), jax.ShapeDtypeStruct(phase.shape, f32)),
    )(base, second, energy, sums)


def solution(mesh):
    return jax.shard_map(
        body,
        mesh=mesh,
        in_specs=(
            P(None, None, ("parts", "gx"), "gy"),
            P(None, ("parts", "gx"), "gy"),
            P(None, ("parts", "gx"), "gy"),
        ),
        out_specs=(P(None, None, ("parts", "gx"), "gy"), P(None, ("parts", "gx"), "gy")),
        check_vma=False,
    )
```

time: 206 us -> 37.4 us (0.18)
  blocking collectives: 97.1 us -> 0 us
  local copies, waits for them, and re-layouts: 44.5 us -> 2.44 us
  other arithmetic: 11.1 us -> 0.01 us
  waiting for transfers between devices: 25.4 us -> 15.2 us
  Pallas kernels: 0 us -> 7.63 us
  matrix products: 5.77 us -> 0 us
  starting transfers between devices: 15.9 us -> 11.2 us
  between operations: 5 us -> 0.67 us
    psum x3 -> x0, blocking collectives: 97.1 us -> none  [the longest x2 62.7 us: residual_norm(): return lax.psum(jnp.sum(current * current / diag), ('gx', 'gy'))]
    reshape x5 -> x0, local copies, waits for them, and re-layouts: 16.3 us -> none  [the longest x2 8.85 us: element_forces(): return flat.reshape(stacked.shape)]
    unnamed x44 -> x7, local copies, waits for them, and re-layouts: 15.8 us -> 1.81 us
    ppermute x13 -> x8, waiting for transfers between devices: 25.4 us -> 15.2 us  [the longest x4 9.07 us: total_over(): x = x + lax.ppermute(x, axis, [(i, i ^ step) for i in range(count)])]
    concatenate x12 -> x0, local copies, waits for them, and re-layouts: 9.72 us -> none  [stack_corners(): jnp.concatenate([wide[:, a:a + layers, b:b + span_x, c:c + span_y] for a,...]
    pallas_call x0 -> x4, Pallas kernels: none -> 7.63 us  [the longest x1 6.42 us: body(): call(functools.partial(operator_kernel, paired_x), (jax.ShapeDtypeStruct(...]
    dot_general x3 -> x0, matrix products: 5.77 us -> none  [element_forces(): jnp.dot(stiff, stacked.reshape(24, -1), precision=lax.Precision.HIGHEST)]
    ppermute x13 -> x8, starting transfers between devices: 15.9 us -> 11.2 us  [the longest x2 5.09 us: exchange(): lax.ppermute(two, axis, [(i, (i - 1) % count if i % 2 == 0 else (i + 1) %...]
  transfers between devices with their start and end apart: 13 -> 8, of which waited for: 10 -> 7; matrix products, arithmetic and copies ran while one was open for 2% -> 0% of each run, Pallas kernels for 0% -> 0%
where the time goes in v1:
time: 37.4 us; the launch traced here: 37.2 us
  waiting for transfers between devices  15.2 us (41%)
  starting transfers between devices  11.2 us (30%)
  Pallas kernels  7.63 us (20%)
  local copies, waits for them, and re-layouts  2.44 us (7%)
  between operations  0.67 us (2%)
    ppermute x4, waiting for transfers between devices, total_over(): x = x + lax.ppermute(x, axis, [(i, i ^ step) for i in range(count)])  9.07 us
    pallas_call x1, Pallas kernels, body(): call(functools.partial(operator_kernel, paired_x), (jax.ShapeDtypeStruct(...  6.42 us
    ppermute x2, waiting for transfers between devices, exchange(): lax.ppermute(two, axis, [(i, (i - 1) % count if i % 2 == 0 else (i + 1) %...  5.5 us
    ppermute x2, starting transfers between devices, exchange(): lax.ppermute(two, axis, [(i, (i - 1) % count if i % 2 == 0 else (i + 1) %...  5.09 us
    ppermute x4, starting transfers between devices, total_over(): x = x + lax.ppermute(x, axis, [(i, i ^ step) for i in range(count)])  3.83 us
    ppermute x2, starting transfers between devices, exchange(): near = lax.ppermute(one, axis, [(i, i ^ 1) for i in range(count)])  2.33 us
    unnamed x7, local copies, waits for them, and re-layouts  1.81 us
  transfers between devices with their start and end apart: 8, of which 7 were waited for; matrix products, arithmetic and copies ran while one was open for 0% of the time, Pallas kernels for 0%

profile of v1, /device:TPU:0, one launch (start us, length us, event | category | flops | bytes accessed | tf_op | source)
XLA Modules:
  0.0 37.2 jit_solution(3432369922578249585)
XLA Ops:
  0.6 0.0 copy-start.2
  0.6 0.8 %copy.6.phase = s32[16,6,128]{2,1,0:T(8,128)S(1)} copy(s32[16,6,128]{2,0,1:T(8,128)} %param.4) | data formatting | bytes 98304 | tf_op args[1]
  1.5 0.0 copy-done.2
  1.5 0.0 copy-start
  1.5 0.9 %copy-done = f32[3,17,6,128]{3,2,1,0:T(8,128)S(1)} copy-done((f32[3,17,6,128]{3,2,1,0:T(8,128)S(1)}, f32[3,17,6,128]{3,2,1,0:T(8,128)}, u32[]{:S(2)}) %copy-start) | copy-done | bytes 156696
  2.4 0.0 copy-start.1
  2.4 0.4 %shard_map.50 = (f32[2,8,128]{2,1,0:T(8,128)S(1)}, f32[2,8,128]{2,1,0:T(8,128)S(1)}, f32[168,128]{1,0:T(8,128)S(1)}, f32[168,128]{1,0:T(8,128)S(1)}) custom-call(f32[3,17,6,128]{3,2,1,0:T(8,128)S(1)} %copy-done, s32[16,6,128]{2,1,0:T(8,128)S(1)} %copy.6.phase, s32[17,6,128]{2,1,0:T(8,128)S(1)} %copy-done.2), custom_call_target="tpu_custom_call" | custom-call | tf_op jit(solution)/shard_map/pallas_call | solution.py:490
  2.8 0.5 %collective-permute-start = (f32[2,8,128]{2,1,0:T(8,128)S(1)}, f32[2,8,128]{2,1,0:T(8,128)S(1)}, u32[]{:S(2)}, u32[]{:S(2)}) collective-permute-start(f32[2,8,128]{2,1,0:T(8,128)S(1)} %get-tuple-element.13.own1), channel_id=1, source_target_pairs={{0,1},{1,0},{2,3},{3,2},{4,5},{5,4},{6,7},{7,6},{8,9},{9,8},{10,11... | collective-permute-start | bytes 24584 | tf_op jit(solution)/shard_map/ppermute | solution.py:455
  3.3 2.6 %collective-permute-start.1 = (f32[2,8,128]{2,1,0:T(8,128)S(1)}, f32[2,8,128]{2,1,0:T(8,128)S(1)}, u32[]{:S(2)}, u32[]{:S(2)}) collective-permute-start(f32[2,8,128]{2,1,0:T(8,128)S(1)} %get-tuple-element.14.own2), channel_id=1, source_target_pairs={{0,3},{1,2},{2,1},{3,0},{4,7},{5,6},{6,5},{7,4},{8,11},{9,10},{10,... | collective-permute-start | bytes 24584 | tf_op jit(solution)/shard_map/ppermute | solution.py:454
  6.0 0.0 collective-permute-done.got1
  6.0 1.4 %collective-permute-done.1.got2 = f32[2,8,128]{2,1,0:T(8,128)S(1)} collective-permute-done((f32[2,8,128]{2,1,0:T(8,128)S(1)}, f32[2,8,128]{2,1,0:T(8,128)S(1)}, u32[]{:S(2)}, u32[]{:S(2)}) %collective-permute-start.1) | collective-permute-done | bytes 8224 | tf_op jit(solution)/shard_map/ppermute | solution.py:454
  7.3 0.1 shard_map.51
  7.4 1.8 %collective-permute-start.2 = (f32[168,128]{1,0:T(8,128)S(1)}, f32[168,128]{1,0:T(8,128)S(1)}, u32[]{:S(2)}, u32[]{:S(2)}) collective-permute-start(f32[168,128]{1,0:T(8,128)S(1)} %get-tuple-element.18), channel_id=1, source_target_pairs={{0,4},{4,0},{8,12},{12,8},{1,5},{5,1},{9,13},{13,9},{2,6},{6,2},{1... | collective-permute-start | bytes 258056 | tf_op jit(solution)/shard_map/ppermute | solution.py:455
  9.2 2.5 %collective-permute-start.3 = (f32[168,128]{1,0:T(8,128)S(1)}, f32[168,128]{1,0:T(8,128)S(1)}, u32[]{:S(2)}, u32[]{:S(2)}) collective-permute-start(f32[168,128]{1,0:T(8,128)S(1)} %get-tuple-element.19), channel_id=1, source_target_pairs={{0,12},{4,8},{8,4},{12,0},{1,13},{5,9},{9,5},{13,1},{2,14},{6,10},... | collective-permute-start | bytes 258056 | tf_op jit(solution)/shard_map/ppermute | solution.py:454
  11.7 0.7 %collective-permute-done.2.got1 = f32[168,128]{1,0:T(8,128)S(1)} collective-permute-done((f32[168,128]{1,0:T(8,128)S(1)}, f32[168,128]{1,0:T(8,128)S(1)}, u32[]{:S(2)}, u32[]{:S(2)}) %collective-permute-start.2) | collective-permute-done | bytes 86048 | tf_op jit(solution)/shard_map/ppermute | solution.py:455
  12.4 4.1 %collective-permute-done.3.got2 = f32[168,128]{1,0:T(8,128)S(1)} collective-permute-done((f32[168,128]{1,0:T(8,128)S(1)}, f32[168,128]{1,0:T(8,128)S(1)}, u32[]{:S(2)}, u32[]{:S(2)}) %collective-permute-start.3) | collective-permute-done | bytes 86048 | tf_op jit(solution)/shard_map/ppermute | solution.py:454
  16.5 0.0 copy-done.1
  16.5 6.4 %shard_map.52 = (f32[3,17,6,128]{3,2,1,0:T(8,128)S(1)}, f32[3,17,6,128]{3,2,1,0:T(8,128)S(1)}, f32[3,16,6,128]{3,2,1,0:T(8,128)S(1)}, f32[8,128]{1,0:T(8,128)S(1)}) custom-call(f32[3,17,6,128]{3,2,1,0:T(8,128)S(1)} %copy-done.1, s32[16,6,128]{2,1,0:T(8,128)S(1)} %copy.6.phase, s32[17,6,128]{2,1,0:T(8,128)S(1)} %copy-done.2, ...), custom_call_target="tpu_custom_call" | custom-call | tf_op jit(solution)/shard_map/pallas_call | solution.py:501
  23.0 0.0 collective-permute-start.4
  23.0 1.2 %collective-permute-done.4 = f32[8,128]{1,0:T(8,128)S(1)} collective-permute-done((f32[8,128]{1,0:T(8,128)S(1)}, f32[8,128]{1,0:T(8,128)S(1)}, u32[]{:S(2)}, u32[]{:S(2)}) %collective-permute-start.4) | collective-permute-done | bytes 4128 | tf_op jit(solution)/shard_map/ppermute | solution.py:468
  24.1 1.5 %collective-permute-start.5 = (f32[8,128]{1,0:T(8,128)S(1)}, f32[8,128]{1,0:T(8,128)S(1)}, u32[]{:S(2)}, u32[]{:S(2)}) collective-permute-start(f32[8,128]{1,0:T(8,128)S(1)} %add.12), channel_id=1, source_target_pairs={{0,2},{1,3},{2,0},{3,1},{4,6},{5,7},{6,4},{7,5},{8,10},{9,11},{10,... | collective-permute-start | bytes 12296 | tf_op jit(solution)/shard_map/ppermute | solution.py:468
  25.6 2.1 %collective-permute-done.5 = f32[8,128]{1,0:T(8,128)S(1)} collective-permute-done((f32[8,128]{1,0:T(8,128)S(1)}, f32[8,128]{1,0:T(8,128)S(1)}, u32[]{:S(2)}, u32[]{:S(2)}) %collective-permute-start.5) | collective-permute-done | bytes 4128 | tf_op jit(solution)/shard_map/ppermute | solution.py:468
  27.7 0.6 %collective-permute-start.6 = (f32[8,128]{1,0:T(8,128)S(1)}, f32[8,128]{1,0:T(8,128)S(1)}, u32[]{:S(2)}, u32[]{:S(2)}) collective-permute-start(f32[8,128]{1,0:T(8,128)S(1)} %add.13), channel_id=1, source_target_pairs={{0,4},{4,0},{8,12},{12,8},{1,5},{5,1},{9,13},{13,9},{2,6},{6,2},{1... | collective-permute-start | bytes 12296 | tf_op jit(solution)/shard_map/ppermute | solution.py:468
  28.3 3.0 %collective-permute-done.6 = f32[8,128]{1,0:T(8,128)S(1)} collective-permute-done((f32[8,128]{1,0:T(8,128)S(1)}, f32[8,128]{1,0:T(8,128)S(1)}, u32[]{:S(2)}, u32[]{:S(2)}) %collective-permute-start.6) | collective-permute-done | bytes 4128 | tf_op jit(solution)/shard_map/ppermute | solution.py:468
  31.4 1.8 %collective-permute-start.7 = (f32[8,128]{1,0:T(8,128)S(1)}, f32[8,128]{1,0:T(8,128)S(1)}, u32[]{:S(2)}, u32[]{:S(2)}) collective-permute-start(f32[8,128]{1,0:T(8,128)S(1)} %add.14), channel_id=1, source_target_pairs={{0,8},{4,12},{8,0},{12,4},{1,9},{5,13},{9,1},{13,5},{2,10},{6,14},... | collective-permute-start | bytes 12296 | tf_op jit(solution)/shard_map/ppermute | solution.py:468
  33.1 2.8 %collective-permute-done.7 = f32[8,128]{1,0:T(8,128)S(1)} collective-permute-done((f32[8,128]{1,0:T(8,128)S(1)}, f32[8,128]{1,0:T(8,128)S(1)}, u32[]{:S(2)}, u32[]{:S(2)}) %collective-permute-start.7) | collective-permute-done | bytes 4128 | tf_op jit(solution)/shard_map/ppermute | solution.py:468
  35.9 0.7 %shard_map.53 = (f32[3,17,6,128]{3,2,1,0:T(8,128)}, f32[16,6,128]{2,1,0:T(8,128)S(1)}) custom-call(f32[3,17,6,128]{3,2,1,0:T(8,128)S(1)} %get-tuple-element.20.base, f32[3,17,6,128]{3,2,1,0:T(8,128)S(1)} %get-tuple-element.21.second, f32[3,16,6,128]{3,2,1,0:T(8,128)S(1)} %get-tuple-element.22.energy, f32[8,128]{1,0:T(8,128)S(1)} %add.15.sums), custom_call_target="tpu_custom_call" | custom-call | tf_op jit(solution)/shard_map/pallas_call | solution.py:519
  36.6 0.6 %copy.7 = f32[16,6,128]{2,0,1:T(8,128)} copy(f32[16,6,128]{2,1,0:T(8,128)S(1)} %get-tuple-element.25) | data formatting | bytes 98304 | tf_op jit(solution)/shard_map/pallas_call | solution.py:519
  (4 shorter events, 0.0 us)
Async XLA Ops:
  0.6 0.9 %copy-start.2 = (s32[17,6,128]{2,1,0:T(8,128)S(1)}, s32[17,6,128]{2,1,0:T(8,128)}, u32[]{:S(2)}) copy-start(s32[17,6,128]{2,1,0:T(8,128)} %fixed.3) | copy-start | bytes 156676
  1.5 0.9 %copy-start = (f32[3,17,6,128]{3,2,1,0:T(8,128)S(1)}, f32[3,17,6,128]{3,2,1,0:T(8,128)}, u32[]{:S(2)}) copy-start(f32[3,17,6,128]{3,2,1,0:T(8,128)} %force.3) | copy-start | bytes 470020
  2.4 14.1 %copy-start.1 = (f32[3,17,6,128]{3,2,1,0:T(8,128)S(1)}, f32[3,17,6,128]{3,2,1,0:T(8,128)}, u32[]{:S(2)}) copy-start(f32[3,17,6,128]{3,2,1,0:T(8,128)} %force.3) | copy-start | bytes 470020
  2.8 3.1 %collective-permute-start = (f32[2,8,128]{2,1,0:T(8,128)S(1)}, f32[2,8,128]{2,1,0:T(8,128)S(1)}, u32[]{:S(2)}, u32[]{:S(2)}) collective-permute-start(f32[2,8,128]{2,1,0:T(8,128)S(1)} %get-tuple-element.13.own1), channel_id=1, source_target_pairs={{0,1},{1,0},{2,3},{3,2},{4,5},{5,4},{6,7},{7,6},{8,9},{9,8},{10,11... | collective-permute-start | bytes 24584 | tf_op jit(solution)/shard_map/ppermute | solution.py:455
  3.3 4.0 %collective-permute-start.1 = (f32[2,8,128]{2,1,0:T(8,128)S(1)}, f32[2,8,128]{2,1,0:T(8,128)S(1)}, u32[]{:S(2)}, u32[]{:S(2)}) collective-permute-start(f32[2,8,128]{2,1,0:T(8,128)S(1)} %get-tuple-element.14.own2), channel_id=1, source_target_pairs={{0,3},{1,2},{2,1},{3,0},{4,7},{5,6},{6,5},{7,4},{8,11},{9,10},{10,... | collective-permute-start | bytes 24584 | tf_op jit(solution)/shard_map/ppermute | solution.py:454
  7.4 5.0 %collective-permute-start.2 = (f32[168,128]{1,0:T(8,128)S(1)}, f32[168,128]{1,0:T(8,128)S(1)}, u32[]{:S(2)}, u32[]{:S(2)}) collective-permute-start(f32[168,128]{1,0:T(8,128)S(1)} %get-tuple-element.18), channel_id=1, source_target_pairs={{0,4},{4,0},{8,12},{12,8},{1,5},{5,1},{9,13},{13,9},{2,6},{6,2},{1... | collective-permute-start | bytes 258056 | tf_op jit(solution)/shard_map/ppermute | solution.py:455
  9.2 7.3 %collective-permute-start.3 = (f32[168,128]{1,0:T(8,128)S(1)}, f32[168,128]{1,0:T(8,128)S(1)}, u32[]{:S(2)}, u32[]{:S(2)}) collective-permute-start(f32[168,128]{1,0:T(8,128)S(1)} %get-tuple-element.19), channel_id=1, source_target_pairs={{0,12},{4,8},{8,4},{12,0},{1,13},{5,9},{9,5},{13,1},{2,14},{6,10},... | collective-permute-start | bytes 258056 | tf_op jit(solution)/shard_map/ppermute | solution.py:454
  23.0 1.2 %collective-permute-start.4 = (f32[8,128]{1,0:T(8,128)S(1)}, f32[8,128]{1,0:T(8,128)S(1)}, u32[]{:S(2)}, u32[]{:S(2)}) collective-permute-start(f32[8,128]{1,0:T(8,128)S(1)} %get-tuple-element.23), channel_id=1, source_target_pairs={{0,1},{1,0},{2,3},{3,2},{4,5},{5,4},{6,7},{7,6},{8,9},{9,8},{10,11... | collective-permute-start | bytes 12296 | tf_op jit(solution)/shard_map/ppermute | solution.py:468
  24.1 3.6 %collective-permute-start.5 = (f32[8,128]{1,0:T(8,128)S(1)}, f32[8,128]{1,0:T(8,128)S(1)}, u32[]{:S(2)}, u32[]{:S(2)}) collective-permute-start(f32[8,128]{1,0:T(8,128)S(1)} %add.12), channel_id=1, source_target_pairs={{0,2},{1,3},{2,0},{3,1},{4,6},{5,7},{6,4},{7,5},{8,10},{9,11},{10,... | collective-permute-start | bytes 12296 | tf_op jit(solution)/shard_map/ppermute | solution.py:468
  27.7 3.6 %collective-permute-start.6 = (f32[8,128]{1,0:T(8,128)S(1)}, f32[8,128]{1,0:T(8,128)S(1)}, u32[]{:S(2)}, u32[]{:S(2)}) collective-permute-start(f32[8,128]{1,0:T(8,128)S(1)} %add.13), channel_id=1, source_target_pairs={{0,4},{4,0},{8,12},{12,8},{1,5},{5,1},{9,13},{13,9},{2,6},{6,2},{1... | collective-permute-start | bytes 12296 | tf_op jit(solution)/shard_map/ppermute | solution.py:468
  31.4 4.5 %collective-permute-start.7 = (f32[8,128]{1,0:T(8,128)S(1)}, f32[8,128]{1,0:T(8,128)S(1)}, u32[]{:S(2)}, u32[]{:S(2)}) collective-permute-start(f32[8,128]{1,0:T(8,128)S(1)} %add.14), channel_id=1, source_target_pairs={{0,8},{4,12},{8,0},{12,4},{1,9},{5,13},{9,1},{13,5},{2,10},{6,14},... | collective-permute-start | bytes 12296 | tf_op jit(solution)/shard_map/ppermute | solution.py:468

commit v2 on v1

--- a/solution.py
+++ b/solution.py
@@ -37,6 +37,10 @@
     for index in (2, 1, 0):
         out = jnp.where(phase == index, jnp.float32(values[index]), out)
     return out
+
+
+def element_rows(ref, k, layers):
+    return ref[pl.ds(k, ref.shape[0] // layers, stride=layers), :]
 
 
 def lane_roll(x, by):
@@ -91,7 +95,7 @@
         place(low, pad[comps * nodes], 0, 0, 3, k)
         put(2 * comps * nodes + 2 * layers + k, None, free[0:1], None)
         if k < layers:
-            scale = table(phase[k], PHASE_STIFFNESS)
+            scale = table(element_rows(phase, k, layers), PHASE_STIFFNESS)
             pad[comps * nodes + 1, 0:rows, :] = scale
             tile = pad[comps * nodes + 1]
             place(low, tile, 0, 1, 3, k)
@@ -312,7 +316,7 @@
     strip_second = [jnp.where(tiles[5] > 0.0, (f_strip[c] - tiles[c]) * strip_inv, 0.0) for c in range(3)]
 
     def scale_of(k):
-        held[0, 0:rows, :] = table(phase[k], PHASE_STIFFNESS)
+        held[0, 0:rows, :] = table(element_rows(phase, k, layers), PHASE_STIFFNESS)
         held[0, 6:7, :] = hi[pl.ds(cn + k, 1), :]
         held[0, 7:8, :] = lo[pl.ds(cn + layers + k, 1), :]
         return held[0], spread(hi, cn + layers + k), spread(lo, cn + k)
@@ -368,7 +372,8 @@
         return a, b, d
 
     def store_energy(which, k, value):
-        energy[which, k] = -table(phase[k], PHASE_SLOPE) * value[0:rows]
+        slope = table(element_rows(phase, k, layers), PHASE_SLOPE)
+        energy[which, pl.ds(k, rows, stride=layers), :] = -slope * value[0:rows]
 
     def flat(x):
         return tuple(x[c][m] for c in range(3) for m in PLANE)
@@ -399,7 +404,7 @@
         return flat(high), flat(f_upper), totals, next_scale, next_b, next_b_7
 
     carry = (flat(start), (zero,) * 12, (zero,) * 3, scale_0, box_0, box_0_7)
-    low_modes, pending, totals, scale, b, b_7 = lax.fori_loop(0, layers - 1, forward, carry)
+    low_modes, pending, totals, scale, b, b_7 = lax.fori_loop(0, layers - 1, forward, carry, unroll=True)
     high = first_layer(layers, b, b_7)
     f_upper, totals = element(layers - 1, unflat(low_modes), high, scale, unflat(pending), totals)
     totals = finish_layer(layers, f_upper, totals)
@@ -420,12 +425,12 @@
         own = inner(g, m)
         store_energy(2, k, own)
         store_energy(1, k, inner(g, [modes[k, i] for i in range(18)]))
-        scale = table(phase[k], PHASE_STIFFNESS)
+        scale = table(element_rows(phase, k, layers), PHASE_STIFFNESS)
         held[2, 0:rows, :] = scale * own[0:rows]
         return flat(high), total + held[2]
 
     held[2] = zero
-    _, total = lax.fori_loop(0, layers, again, (flat(second_layer(0)), zero))
+    _, total = lax.fori_loop(0, layers, again, (flat(second_layer(0)), zero), unroll=True)
     for i, x in enumerate(totals + (total,)):
         x = jnp.where(row < rows, x, 0.0)
         x = jnp.sum(jnp.sum(x, axis=0, keepdims=True), axis=1, keepdims=True)
@@ -465,14 +470,19 @@
         return lax.psum(x, axis)
     step = 1
     while step < count:
-        x = x + lax.ppermute(x, axis, [(i, i ^ step) for i in range(count)])
-        step *= 2
+        width = 4 if count // step >= 4 else 2
+        group = [
+            lax.ppermute(x, axis, [(i, i ^ (step * by)) for i in range(count)]) for by in range(1, width)
+        ]
+        x = functools.reduce(jnp.add, group, x)
+        step *= width
     return x
 
 
 def body(force, phase, fixed):
     comps, nodes, rows, width = force.shape
     layers = nodes - 1
+    phase = phase.transpose(1, 0, 2).reshape(rows * layers, width)
     f32 = jnp.float32
     paired_x = lax.axis_size("gx") % 2 == 0
     paired_y = lax.axis_size("gy") % 2 == 0
@@ -516,10 +526,11 @@
         ],
     )(force, phase, fixed, strip, near, far)
     sums = total_over(total_over(sums, "gy"), "gx")
-    return call(
+    displacement, sensitivity = call(
         combine_kernel,
         (jax.ShapeDtypeStruct(force.shape, f32), jax.ShapeDtypeStruct(phase.shape, f32)),
     )(base, second, energy, sums)
+    return displacement, sensitivity.reshape(rows, layers, width).transpose(1, 0, 2)
 
 
 def solution(mesh):

time: 37.4 us -> 30.8 us (0.82)
  waiting for transfers between devices: 15.2 us -> 10.2 us
  Pallas kernels: 7.63 us -> 3.32 us
  starting transfers between devices: 11.2 us -> 13.7 us
    ppermute x4 -> x6, waiting for transfers between devices: 9.07 us -> 4.01 us  [total_over(): lax.ppermute(x, axis, [(i, i ^ step * by) for i in range(count)])]
    pallas_call x1, Pallas kernels: 6.42 us -> 2.11 us  [body(): call(functools.partial(operator_kernel, paired_x), (jax.ShapeDtypeStruct(...]
    ppermute x4 -> x6, starting transfers between devices: 3.83 us -> 6.32 us  [total_over(): lax.ppermute(x, axis, [(i, i ^ step * by) for i in range(count)])]
    unnamed x7 -> x12, local copies, waits for them, and re-layouts: 1.81 us -> 2.62 us
    pallas_call x1 -> x0, local copies, waits for them, and re-layouts: 0.63 us -> none  [body(): call(combine_kernel, (jax.ShapeDtypeStruct(force.shape, f32), jax.ShapeDt...]
  transfers between devices with their start and end apart: 8 -> 10, of which waited for: 7 -> 8; matrix products, arithmetic and copies ran while one was open for 0% -> 0% of each run, Pallas kernels for 0% -> 0%
where the time goes in v2:
time: 30.8 us; the launch traced here: 30.5 us
  starting transfers between devices  13.7 us (44%)
  waiting for transfers between devices  10.2 us (33%)
  Pallas kernels  3.32 us (11%)
  local copies, waits for them, and re-layouts  2.62 us (9%)
  between operations  0.67 us (2%)
    ppermute x6, starting transfers between devices, total_over(): lax.ppermute(x, axis, [(i, i ^ step * by) for i in range(count)])  6.32 us
    ppermute x2, waiting for transfers between devices, exchange(): lax.ppermute(two, axis, [(i, (i - 1) % count if i % 2 == 0 else (i + 1) %...  5.5 us
    ppermute x2, starting transfers between devices, exchange(): lax.ppermute(two, axis, [(i, (i - 1) % count if i % 2 == 0 else (i + 1) %...  5.09 us
    ppermute x6, waiting for transfers between devices, total_over(): lax.ppermute(x, axis, [(i, i ^ step * by) for i in range(count)])  4.01 us
    unnamed x12, local copies, waits for them, and re-layouts  2.62 us
    ppermute x2, starting transfers between devices, exchange(): near = lax.ppermute(one, axis, [(i, i ^ 1) for i in range(count)])  2.33 us
    pallas_call x1, Pallas kernels, body(): call(functools.partial(operator_kernel, paired_x), (jax.ShapeDtypeStruct(...  2.11 us
    pallas_call x1, Pallas kernels, body(): call(combine_kernel, (jax.ShapeDtypeStruct(force.shape, f32), jax.ShapeDt...  0.74 us
  transfers between devices with their start and end apart: 10, of which 8 were waited for; matrix products, arithmetic and copies ran while one was open for 0% of the time, Pallas kernels for 0%

profile of v2, /device:TPU:0, one launch (start us, length us, event | category | flops | bytes accessed | tf_op | source)
XLA Modules:
  0.0 30.5 jit_solution(9641463220464492044)
XLA Ops:
  0.6 0.0 copy-start
  0.6 0.9 %copy-done = f32[3,17,6,128]{3,2,1,0:T(8,128)S(1)} copy-done((f32[3,17,6,128]{3,2,1,0:T(8,128)S(1)}, f32[3,17,6,128]{3,2,1,0:T(8,128)}, u32[]{:S(2)}) %copy-start) | copy-done | bytes 156696
  1.6 0.0 copy-start.2
  1.6 0.9 %copy-done.2 = s32[17,6,128]{2,1,0:T(8,128)S(1)} copy-done((s32[17,6,128]{2,1,0:T(8,128)S(1)}, s32[17,6,128]{2,1,0:T(8,128)}, u32[]{:S(2)}) %copy-start.2) | copy-done | bytes 52248
  2.4 0.0 copy-start.4
  2.4 0.8 %copy-done.4 = s32[16,6,128]{2,0,1:T(8,128)S(1)} copy-done((s32[16,6,128]{2,0,1:T(8,128)S(1)}, s32[16,6,128]{2,0,1:T(8,128)}, u32[]{:S(2)}) %copy-start.4) | copy-done | bytes 49176
  3.2 0.0 copy-start.1
  3.2 0.4 %shard_map.50 = (f32[2,8,128]{2,1,0:T(8,128)S(1)}, f32[2,8,128]{2,1,0:T(8,128)S(1)}, f32[168,128]{1,0:T(8,128)S(1)}, f32[168,128]{1,0:T(8,128)S(1)}) custom-call(f32[3,17,6,128]{3,2,1,0:T(8,128)S(1)} %copy-done, s32[96,128]{1,0:T(8,128)S(1)} %bitcast.6, s32[17,6,128]{2,1,0:T(8,128)S(1)} %copy-done.2), custom_call_target="tpu_custom_call" | custom-call | tf_op jit(solution)/shard_map/pallas_call | solution.py:500
  3.6 0.5 %collective-permute-start = (f32[2,8,128]{2,1,0:T(8,128)S(1)}, f32[2,8,128]{2,1,0:T(8,128)S(1)}, u32[]{:S(2)}, u32[]{:S(2)}) collective-permute-start(f32[2,8,128]{2,1,0:T(8,128)S(1)} %get-tuple-element.15.own1), channel_id=1, source_target_pairs={{0,1},{1,0},{2,3},{3,2},{4,5},{5,4},{6,7},{7,6},{8,9},{9,8},{10,11... | collective-permute-start | bytes 24584 | tf_op jit(solution)/shard_map/ppermute | solution.py:460
  4.2 2.6 %collective-permute-start.1 = (f32[2,8,128]{2,1,0:T(8,128)S(1)}, f32[2,8,128]{2,1,0:T(8,128)S(1)}, u32[]{:S(2)}, u32[]{:S(2)}) collective-permute-start(f32[2,8,128]{2,1,0:T(8,128)S(1)} %get-tuple-element.16.own2), channel_id=1, source_target_pairs={{0,3},{1,2},{2,1},{3,0},{4,7},{5,6},{6,5},{7,4},{8,11},{9,10},{10,... | collective-permute-start | bytes 24584 | tf_op jit(solution)/shard_map/ppermute | solution.py:459
  6.8 0.0 collective-permute-done.got1
  6.8 1.4 %collective-permute-done.1.got2 = f32[2,8,128]{2,1,0:T(8,128)S(1)} collective-permute-done((f32[2,8,128]{2,1,0:T(8,128)S(1)}, f32[2,8,128]{2,1,0:T(8,128)S(1)}, u32[]{:S(2)}, u32[]{:S(2)}) %collective-permute-start.1) | collective-permute-done | bytes 8224 | tf_op jit(solution)/shard_map/ppermute | solution.py:459
  8.1 0.0 copy-start.3
  8.1 0.0 copy-start.5
  8.1 0.1 shard_map.51
  8.2 1.8 %collective-permute-start.2 = (f32[168,128]{1,0:T(8,128)S(1)}, f32[168,128]{1,0:T(8,128)S(1)}, u32[]{:S(2)}, u32[]{:S(2)}) collective-permute-start(f32[168,128]{1,0:T(8,128)S(1)} %get-tuple-element.20), channel_id=1, source_target_pairs={{0,4},{4,0},{8,12},{12,8},{1,5},{5,1},{9,13},{13,9},{2,6},{6,2},{1... | collective-permute-start | bytes 258056 | tf_op jit(solution)/shard_map/ppermute | solution.py:460
  10.1 2.5 %collective-permute-start.3 = (f32[168,128]{1,0:T(8,128)S(1)}, f32[168,128]{1,0:T(8,128)S(1)}, u32[]{:S(2)}, u32[]{:S(2)}) collective-permute-start(f32[168,128]{1,0:T(8,128)S(1)} %get-tuple-element.21), channel_id=1, source_target_pairs={{0,12},{4,8},{8,4},{12,0},{1,13},{5,9},{9,5},{13,1},{2,14},{6,10},... | collective-permute-start | bytes 258056 | tf_op jit(solution)/shard_map/ppermute | solution.py:459
  12.5 0.7 %collective-permute-done.2.got1 = f32[168,128]{1,0:T(8,128)S(1)} collective-permute-done((f32[168,128]{1,0:T(8,128)S(1)}, f32[168,128]{1,0:T(8,128)S(1)}, u32[]{:S(2)}, u32[]{:S(2)}) %collective-permute-start.2) | collective-permute-done | bytes 86048 | tf_op jit(solution)/shard_map/ppermute | solution.py:460
  13.2 4.1 %collective-permute-done.3.got2 = f32[168,128]{1,0:T(8,128)S(1)} collective-permute-done((f32[168,128]{1,0:T(8,128)S(1)}, f32[168,128]{1,0:T(8,128)S(1)}, u32[]{:S(2)}, u32[]{:S(2)}) %collective-permute-start.3) | collective-permute-done | bytes 86048 | tf_op jit(solution)/shard_map/ppermute | solution.py:459
  17.3 0.0 copy-done.1
  17.3 0.0 copy-done.3
  17.3 0.0 copy-done.5
  17.3 2.1 %shard_map.52 = (f32[3,17,6,128]{3,2,1,0:T(8,128)S(1)}, f32[3,17,6,128]{3,2,1,0:T(8,128)S(1)}, f32[3,96,128]{2,1,0:T(8,128)S(1)}, f32[8,128]{1,0:T(8,128)S(1)}) custom-call(f32[3,17,6,128]{3,2,1,0:T(8,128)S(1)} %copy-done.1, s32[96,128]{1,0:T(8,128)S(1)} %bitcast.7, s32[17,6,128]{2,1,0:T(8,128)S(1)} %copy-done.3, f32[6,8,128]{2,1,0:T(8,128)S(1)} %get-tuple-element.19.strip, ...), custom_call_target="tpu_custom_call" | custom-call | tf_op jit(solution)/shard_map/pallas_call | solution.py:511
  19.5 0.7 %collective-permute-start.6 = (f32[8,128]{1,0:T(8,128)S(1)}, f32[8,128]{1,0:T(8,128)S(1)}, u32[]{:S(2)}, u32[]{:S(2)}) collective-permute-start(f32[8,128]{1,0:T(8,128)S(1)} %get-tuple-element.25), channel_id=1, source_target_pairs={{0,3},{1,2},{2,1},{3,0},{4,7},{5,6},{6,5},{7,4},{8,11},{9,10},{10,... | collective-permute-start | bytes 12296 | tf_op jit(solution)/shard_map/ppermute | solution.py:475
  20.1 0.9 %collective-permute-start.5 = (f32[8,128]{1,0:T(8,128)S(1)}, f32[8,128]{1,0:T(8,128)S(1)}, u32[]{:S(2)}, u32[]{:S(2)}) collective-permute-start(f32[8,128]{1,0:T(8,128)S(1)} %get-tuple-element.25), channel_id=1, source_target_pairs={{0,2},{1,3},{2,0},{3,1},{4,6},{5,7},{6,4},{7,5},{8,10},{9,11},{10,... | collective-permute-start | bytes 12296 | tf_op jit(solution)/shard_map/ppermute | solution.py:475
  21.0 0.3 collective-permute-start.4
  21.3 1.2 %collective-permute-done.6 = f32[8,128]{1,0:T(8,128)S(1)} collective-permute-done((f32[8,128]{1,0:T(8,128)S(1)}, f32[8,128]{1,0:T(8,128)S(1)}, u32[]{:S(2)}, u32[]{:S(2)}) %collective-permute-start.6) | collective-permute-done | bytes 4128 | tf_op jit(solution)/shard_map/ppermute | solution.py:475
  22.5 1.3 %collective-permute-done.5 = f32[8,128]{1,0:T(8,128)S(1)} collective-permute-done((f32[8,128]{1,0:T(8,128)S(1)}, f32[8,128]{1,0:T(8,128)S(1)}, u32[]{:S(2)}, u32[]{:S(2)}) %collective-permute-start.5) | collective-permute-done | bytes 4128 | tf_op jit(solution)/shard_map/ppermute | solution.py:475
  23.7 0.0 collective-permute-done.4
  23.8 1.5 %collective-permute-start.9 = (f32[8,128]{1,0:T(8,128)S(1)}, f32[8,128]{1,0:T(8,128)S(1)}, u32[]{:S(2)}, u32[]{:S(2)}) collective-permute-start(f32[8,128]{1,0:T(8,128)S(1)} %add_add_fusion.1), channel_id=1, source_target_pairs={{0,12},{4,8},{8,4},{12,0},{1,13},{5,9},{9,5},{13,1},{2,14},{6,10},... | collective-permute-start | bytes 12296 | tf_op jit(solution)/shard_map/ppermute | solution.py:475
  25.2 0.2 collective-permute-start.8
  25.4 2.8 %collective-permute-start.7 = (f32[8,128]{1,0:T(8,128)S(1)}, f32[8,128]{1,0:T(8,128)S(1)}, u32[]{:S(2)}, u32[]{:S(2)}) collective-permute-start(f32[8,128]{1,0:T(8,128)S(1)} %add_add_fusion.1), channel_id=1, source_target_pairs={{0,4},{4,0},{8,12},{12,8},{1,5},{5,1},{9,13},{13,9},{2,6},{6,2},{1... | collective-permute-start | bytes 12296 | tf_op jit(solution)/shard_map/ppermute | solution.py:475
  28.2 1.0 %collective-permute-done.9 = f32[8,128]{1,0:T(8,128)S(1)} collective-permute-done((f32[8,128]{1,0:T(8,128)S(1)}, f32[8,128]{1,0:T(8,128)S(1)}, u32[]{:S(2)}, u32[]{:S(2)}) %collective-permute-start.9) | collective-permute-done | bytes 4128 | tf_op jit(solution)/shard_map/ppermute | solution.py:475
  29.2 0.5 %collective-permute-done.8 = f32[8,128]{1,0:T(8,128)S(1)} collective-permute-done((f32[8,128]{1,0:T(8,128)S(1)}, f32[8,128]{1,0:T(8,128)S(1)}, u32[]{:S(2)}, u32[]{:S(2)}) %collective-permute-start.8) | collective-permute-done | bytes 4128 | tf_op jit(solution)/shard_map/ppermute | solution.py:475
  29.7 0.1 collective-permute-done.7
  29.8 0.7 %shard_map.53 = (f32[3,17,6,128]{3,2,1,0:T(8,128)}, f32[96,128]{1,0:T(8,128)}) custom-call(f32[3,17,6,128]{3,2,1,0:T(8,128)S(1)} %get-tuple-element.22.base, f32[3,17,6,128]{3,2,1,0:T(8,128)S(1)} %get-tuple-element.23.second, f32[3,96,128]{2,1,0:T(8,128)S(1)} %get-tuple-element.24.energy, f32[8,128]{1,0:T(8,128)S(1)} %add_add_fusion.sums), custom_call_target="tpu_custom_call" | custom-call | tf_op jit(solution)/shard_map/pallas_call | solution.py:529
  (2 shorter events, 0.0 us)
Async XLA Ops:
  0.6 0.9 %copy-start = (f32[3,17,6,128]{3,2,1,0:T(8,128)S(1)}, f32[3,17,6,128]{3,2,1,0:T(8,128)}, u32[]{:S(2)}) copy-start(f32[3,17,6,128]{3,2,1,0:T(8,128)} %force.3) | copy-start | bytes 470020
  1.6 0.9 %copy-start.2 = (s32[17,6,128]{2,1,0:T(8,128)S(1)}, s32[17,6,128]{2,1,0:T(8,128)}, u32[]{:S(2)}) copy-start(s32[17,6,128]{2,1,0:T(8,128)} %fixed.3) | copy-start | bytes 156676
  2.4 0.8 %copy-start.4 = (s32[16,6,128]{2,0,1:T(8,128)S(1)}, s32[16,6,128]{2,0,1:T(8,128)}, u32[]{:S(2)}) copy-start(s32[16,6,128]{2,0,1:T(8,128)} %param.4) | copy-start | bytes 147460
  3.2 14.1 %copy-start.1 = (f32[3,17,6,128]{3,2,1,0:T(8,128)S(1)}, f32[3,17,6,128]{3,2,1,0:T(8,128)}, u32[]{:S(2)}) copy-start(f32[3,17,6,128]{3,2,1,0:T(8,128)} %force.3) | copy-start | bytes 470020
  3.6 3.1 %collective-permute-start = (f32[2,8,128]{2,1,0:T(8,128)S(1)}, f32[2,8,128]{2,1,0:T(8,128)S(1)}, u32[]{:S(2)}, u32[]{:S(2)}) collective-permute-start(f32[2,8,128]{2,1,0:T(8,128)S(1)} %get-tuple-element.15.own1), channel_id=1, source_target_pairs={{0,1},{1,0},{2,3},{3,2},{4,5},{5,4},{6,7},{7,6},{8,9},{9,8},{10,11... | collective-permute-start | bytes 24584 | tf_op jit(solution)/shard_map/ppermute | solution.py:460
  4.2 4.0 %collective-permute-start.1 = (f32[2,8,128]{2,1,0:T(8,128)S(1)}, f32[2,8,128]{2,1,0:T(8,128)S(1)}, u32[]{:S(2)}, u32[]{:S(2)}) collective-permute-start(f32[2,8,128]{2,1,0:T(8,128)S(1)} %get-tuple-element.16.own2), channel_id=1, source_target_pairs={{0,3},{1,2},{2,1},{3,0},{4,7},{5,6},{6,5},{7,4},{8,11},{9,10},{10,... | collective-permute-start | bytes 24584 | tf_op jit(solution)/shard_map/ppermute | solution.py:459
  8.1 9.2 %copy-start.3 = (s32[17,6,128]{2,1,0:T(8,128)S(1)}, s32[17,6,128]{2,1,0:T(8,128)}, u32[]{:S(2)}) copy-start(s32[17,6,128]{2,1,0:T(8,128)} %fixed.3) | copy-start | bytes 156676
  8.1 9.2 %copy-start.5 = (s32[16,6,128]{2,0,1:T(8,128)S(1)}, s32[16,6,128]{2,0,1:T(8,128)}, u32[]{:S(2)}) copy-start(s32[16,6,128]{2,0,1:T(8,128)} %param.4) | copy-start | bytes 147460
  8.2 5.0 %collective-permute-start.2 = (f32[168,128]{1,0:T(8,128)S(1)}, f32[168,128]{1,0:T(8,128)S(1)}, u32[]{:S(2)}, u32[]{:S(2)}) collective-permute-start(f32[168,128]{1,0:T(8,128)S(1)} %get-tuple-element.20), channel_id=1, source_target_pairs={{0,4},{4,0},{8,12},{12,8},{1,5},{5,1},{9,13},{13,9},{2,6},{6,2},{1... | collective-permute-start | bytes 258056 | tf_op jit(solution)/shard_map/ppermute | solution.py:460
  10.1 7.3 %collective-permute-start.3 = (f32[168,128]{1,0:T(8,128)S(1)}, f32[168,128]{1,0:T(8,128)S(1)}, u32[]{:S(2)}, u32[]{:S(2)}) collective-permute-start(f32[168,128]{1,0:T(8,128)S(1)} %get-tuple-element.21), channel_id=1, source_target_pairs={{0,12},{4,8},{8,4},{12,0},{1,13},{5,9},{9,5},{13,1},{2,14},{6,10},... | collective-permute-start | bytes 258056 | tf_op jit(solution)/shard_map/ppermute | solution.py:459
  19.5 3.0 %collective-permute-start.6 = (f32[8,128]{1,0:T(8,128)S(1)}, f32[8,128]{1,0:T(8,128)S(1)}, u32[]{:S(2)}, u32[]{:S(2)}) collective-permute-start(f32[8,128]{1,0:T(8,128)S(1)} %get-tuple-element.25), channel_id=1, source_target_pairs={{0,3},{1,2},{2,1},{3,0},{4,7},{5,6},{6,5},{7,4},{8,11},{9,10},{10,... | collective-permute-start | bytes 12296 | tf_op jit(solution)/shard_map/ppermute | solution.py:475
  20.1 3.6 %collective-permute-start.5 = (f32[8,128]{1,0:T(8,128)S(1)}, f32[8,128]{1,0:T(8,128)S(1)}, u32[]{:S(2)}, u32[]{:S(2)}) collective-permute-start(f32[8,128]{1,0:T(8,128)S(1)} %get-tuple-element.25), channel_id=1, source_target_pairs={{0,2},{1,3},{2,0},{3,1},{4,6},{5,7},{6,4},{7,5},{8,10},{9,11},{10,... | collective-permute-start | bytes 12296 | tf_op jit(solution)/shard_map/ppermute | solution.py:475
  21.0 2.7 %collective-permute-start.4 = (f32[8,128]{1,0:T(8,128)S(1)}, f32[8,128]{1,0:T(8,128)S(1)}, u32[]{:S(2)}, u32[]{:S(2)}) collective-permute-start(f32[8,128]{1,0:T(8,128)S(1)} %get-tuple-element.25), channel_id=1, source_target_pairs={{0,1},{1,0},{2,3},{3,2},{4,5},{5,4},{6,7},{7,6},{8,9},{9,8},{10,11... | collective-permute-start | bytes 12296 | tf_op jit(solution)/shard_map/ppermute | solution.py:475
  23.8 5.5 %collective-permute-start.9 = (f32[8,128]{1,0:T(8,128)S(1)}, f32[8,128]{1,0:T(8,128)S(1)}, u32[]{:S(2)}, u32[]{:S(2)}) collective-permute-start(f32[8,128]{1,0:T(8,128)S(1)} %add_add_fusion.1), channel_id=1, source_target_pairs={{0,12},{4,8},{8,4},{12,0},{1,13},{5,9},{9,5},{13,1},{2,14},{6,10},... | collective-permute-start | bytes 12296 | tf_op jit(solution)/shard_map/ppermute | solution.py:475
  25.2 4.5 %collective-permute-start.8 = (f32[8,128]{1,0:T(8,128)S(1)}, f32[8,128]{1,0:T(8,128)S(1)}, u32[]{:S(2)}, u32[]{:S(2)}) collective-permute-start(f32[8,128]{1,0:T(8,128)S(1)} %add_add_fusion.1), channel_id=1, source_target_pairs={{0,8},{4,12},{8,0},{12,4},{1,9},{5,13},{9,1},{13,5},{2,10},{6,14},... | collective-permute-start | bytes 12296 | tf_op jit(solution)/shard_map/ppermute | solution.py:475
  25.4 4.4 %collective-permute-start.7 = (f32[8,128]{1,0:T(8,128)S(1)}, f32[8,128]{1,0:T(8,128)S(1)}, u32[]{:S(2)}, u32[]{:S(2)}) collective-permute-start(f32[8,128]{1,0:T(8,128)S(1)} %add_add_fusion.1), channel_id=1, source_target_pairs={{0,4},{4,0},{8,12},{12,8},{1,5},{5,1},{9,13},{13,9},{2,6},{6,2},{1... | collective-permute-start | bytes 12296 | tf_op jit(solution)/shard_map/ppermute | solution.py:475

commit v3 on v2

--- a/solution.py
+++ b/solution.py
@@ -54,8 +54,9 @@
     return lax.rem(lax.axis_index(axis), 2) == 0
 
 
-def pack_kernel(paired_x, paired_y, force, phase, fixed, col1, col2, row1, row2, pad):
-    comps, nodes, rows, width = force.shape
+def pack_kernel(paired_x, paired_y, rhs_0, rhs_1, rhs_2, phase, fixed, col1, col2, row1, row2, pad):
+    rhs, comps = (rhs_0, rhs_1, rhs_2), 3
+    nodes, rows, width = rhs_0.shape
     layers = nodes - 1
     lane = lanes()
     even_x = is_even("gx") if paired_x else True
@@ -83,7 +84,7 @@
         free = (1 - fixed[k]).astype(jnp.float32)
         for c in range(comps):
             q = c * nodes + k
-            r0 = free * force[c, k]
+            r0 = rhs[c][k]
             pad[q, 0:rows, :] = r0
             tile = pad[q]
             place(low, tile, 0, 0, c, k)
@@ -237,11 +238,12 @@
 
 
 def operator_kernel(
-    paired_x, force, phase, fixed, strip, got1, got2,
+    paired_x, rhs_0, rhs_1, rhs_2, phase, fixed, strip, got1, got2,
     base, second, energy, sums,
     lo, hi, held, modes, residual, inverse,
 ):
-    comps, nodes, rows, width = force.shape
+    rhs, comps = (rhs_0, rhs_1, rhs_2), 3
+    nodes, rows, width = rhs_0.shape
     layers = nodes - 1
     lane, row = lanes(), sublanes()
     last_row, below = row == 6, row == 7
@@ -333,10 +335,9 @@
         inv_7 = 1.0 / (KE_DIAGONAL * around_node_7)
         inverse[k] = inv
         out = []
-        free = (1 - fixed[k]).astype(jnp.float32)
         for c in range(3):
             q = c * nodes + k
-            residual[q, 0:rows, :] = free * force[c, k]
+            residual[q, 0:rows, :] = rhs[c][k]
             residual[q, 6:7, :] = hi[pl.ds(q, 1), :]
             residual[q, 7:8, :] = lo[pl.ds(q, 1), :]
             x = residual[q] * inv
@@ -483,6 +484,7 @@
     comps, nodes, rows, width = force.shape
     layers = nodes - 1
     phase = phase.transpose(1, 0, 2).reshape(rows * layers, width)
+    rhs = [(1 - fixed).astype(jnp.float32) * force[c] for c in range(comps)]
     f32 = jnp.float32
     paired_x = lax.axis_size("gx") % 2 == 0
     paired_y = lax.axis_size("gy") % 2 == 0
@@ -501,7 +503,7 @@
         functools.partial(pack_kernel, paired_x, paired_y),
         (column, column, message, message),
         [pltpu.VMEM((comps * nodes + 2, 8, LANES), f32)],
-    )(force, phase, fixed)
+    )(*rhs, phase, fixed)
     near, far = exchange(col1, col2, "gy")
     strip, row1, row2 = call(
         functools.partial(strip_kernel, paired_x, paired_y),
@@ -524,7 +526,7 @@
             pltpu.VMEM((comps * nodes, 8, LANES), f32),
             pltpu.VMEM((nodes, 8, LANES), f32),
         ],
-    )(force, phase, fixed, strip, near, far)
+    )(*rhs, phase, fixed, strip, near, far)
     sums = total_over(total_over(sums, "gy"), "gx")
     displacement, sensitivity = call(
         combine_kernel,

time: 30.8 us -> 29.1 us (0.945)
  local copies, waits for them, and re-layouts: 2.62 us -> 0.01 us
  other arithmetic: 0.01 us -> 1.05 us
    unnamed x12 -> x4, local copies, waits for them, and re-layouts: 2.62 us -> 0.01 us
    mul x0 -> x1, other arithmetic: none -> 1.04 us  [body(): rhs = [(1 - fixed).astype(jnp.float32) * force[c] for c in range(comps)]]
where the time goes in v3:
time: 29.1 us; the launch traced here: 29 us
  starting transfers between devices  13.7 us (47%)
  waiting for transfers between devices  10.2 us (35%)
  Pallas kernels  3.31 us (11%)
  other arithmetic  1.05 us (4%)
  between operations  0.69 us (2%)
    ppermute x6, starting transfers between devices, total_over(): lax.ppermute(x, axis, [(i, i ^ step * by) for i in range(count)])  6.32 us
    ppermute x2, waiting for transfers between devices, exchange(): lax.ppermute(two, axis, [(i, (i - 1) % count if i % 2 == 0 else (i + 1) %...  5.5 us
    ppermute x2, starting transfers between devices, exchange(): lax.ppermute(two, axis, [(i, (i - 1) % count if i % 2 == 0 else (i + 1) %...  5.09 us
    ppermute x6, waiting for transfers between devices, total_over(): lax.ppermute(x, axis, [(i, i ^ step * by) for i in range(count)])  4.01 us
    ppermute x2, starting transfers between devices, exchange(): near = lax.ppermute(one, axis, [(i, i ^ 1) for i in range(count)])  2.33 us
    pallas_call x1, Pallas kernels, body(): call(functools.partial(operator_kernel, paired_x), (jax.ShapeDtypeStruct(...  2.09 us
    mul x1, other arithmetic, body(): rhs = [(1 - fixed).astype(jnp.float32) * force[c] for c in range(comps)]  1.04 us
    pallas_call x1, Pallas kernels, body(): call(combine_kernel, (jax.ShapeDtypeStruct(force.shape, f32), jax.ShapeDt...  0.74 us
  transfers between devices with their start and end apart: 10, of which 8 were waited for; matrix products, arithmetic and copies ran while one was open for 0% of the time, Pallas kernels for 0%

profile of v3, /device:TPU:0, one launch (start us, length us, event | category | flops | bytes accessed | tf_op | source)
XLA Modules:
  0.0 29.0 jit_solution(17486974871166520357)
XLA Ops:
  0.6 0.0 copy-start
  0.6 0.0 copy-start.1
  0.6 1.0 %bitcast_multiply_fusion = (f32[17,6,128]{2,1,0:T(8,128)S(1)}, f32[17,6,128]{2,1,0:T(8,128)S(1)}, f32[17,6,128]{2,1,0:T(8,128)S(1)}) fusion(f32[3,17,6,128]{3,2,1,0:T(8,128)} %param.3, s32[17,6,128]{2,1,0:T(8,128)} %fixed.3), kind=kLoop, calls=%fused_computation | loop fusion | flops 65280 | bytes 365568 | tf_op jit(solution)/shard_map/mul | solution.py:487
  1.7 0.0 copy-done
  1.7 0.0 copy-done.1
  1.7 0.4 %shard_map.50 = (f32[2,8,128]{2,1,0:T(8,128)S(1)}, f32[2,8,128]{2,1,0:T(8,128)S(1)}, f32[168,128]{1,0:T(8,128)S(1)}, f32[168,128]{1,0:T(8,128)S(1)}) custom-call(f32[17,6,128]{2,1,0:T(8,128)S(1)} %get-tuple-element.29.rhs_0, f32[17,6,128]{2,1,0:T(8,128)S(1)} %get-tuple-element.30.rhs_1, f32[17,6,128]{2,1,0:T(8,128)S(1)} %get-tuple-element.28.rhs_2, ...), custom_call_target="tpu_custom_call" | custom-call | tf_op jit(solution)/shard_map/pallas_call | solution.py:502
  2.1 0.5 %collective-permute-start = (f32[2,8,128]{2,1,0:T(8,128)S(1)}, f32[2,8,128]{2,1,0:T(8,128)S(1)}, u32[]{:S(2)}, u32[]{:S(2)}) collective-permute-start(f32[2,8,128]{2,1,0:T(8,128)S(1)} %get-tuple-element.15.own1), channel_id=1, source_target_pairs={{0,1},{1,0},{2,3},{3,2},{4,5},{5,4},{6,7},{7,6},{8,9},{9,8},{10,11... | collective-permute-start | bytes 24584 | tf_op jit(solution)/shard_map/ppermute | solution.py:461
  2.6 2.6 %collective-permute-start.1 = (f32[2,8,128]{2,1,0:T(8,128)S(1)}, f32[2,8,128]{2,1,0:T(8,128)S(1)}, u32[]{:S(2)}, u32[]{:S(2)}) collective-permute-start(f32[2,8,128]{2,1,0:T(8,128)S(1)} %get-tuple-element.16.own2), channel_id=1, source_target_pairs={{0,3},{1,2},{2,1},{3,0},{4,7},{5,6},{6,5},{7,4},{8,11},{9,10},{10,... | collective-permute-start | bytes 24584 | tf_op jit(solution)/shard_map/ppermute | solution.py:460
  5.2 0.0 collective-permute-done.got1
  5.2 1.4 %collective-permute-done.1.got2 = f32[2,8,128]{2,1,0:T(8,128)S(1)} collective-permute-done((f32[2,8,128]{2,1,0:T(8,128)S(1)}, f32[2,8,128]{2,1,0:T(8,128)S(1)}, u32[]{:S(2)}, u32[]{:S(2)}) %collective-permute-start.1) | collective-permute-done | bytes 8224 | tf_op jit(solution)/shard_map/ppermute | solution.py:460
  6.6 0.1 shard_map.51
  6.7 1.8 %collective-permute-start.2 = (f32[168,128]{1,0:T(8,128)S(1)}, f32[168,128]{1,0:T(8,128)S(1)}, u32[]{:S(2)}, u32[]{:S(2)}) collective-permute-start(f32[168,128]{1,0:T(8,128)S(1)} %get-tuple-element.20), channel_id=1, source_target_pairs={{0,4},{4,0},{8,12},{12,8},{1,5},{5,1},{9,13},{13,9},{2,6},{6,2},{1... | collective-permute-start | bytes 258056 | tf_op jit(solution)/shard_map/ppermute | solution.py:461
  8.5 2.5 %collective-permute-start.3 = (f32[168,128]{1,0:T(8,128)S(1)}, f32[168,128]{1,0:T(8,128)S(1)}, u32[]{:S(2)}, u32[]{:S(2)}) collective-permute-start(f32[168,128]{1,0:T(8,128)S(1)} %get-tuple-element.21), channel_id=1, source_target_pairs={{0,12},{4,8},{8,4},{12,0},{1,13},{5,9},{9,5},{13,1},{2,14},{6,10},... | collective-permute-start | bytes 258056 | tf_op jit(solution)/shard_map/ppermute | solution.py:460
  11.0 0.7 %collective-permute-done.2.got1 = f32[168,128]{1,0:T(8,128)S(1)} collective-permute-done((f32[168,128]{1,0:T(8,128)S(1)}, f32[168,128]{1,0:T(8,128)S(1)}, u32[]{:S(2)}, u32[]{:S(2)}) %collective-permute-start.2) | collective-permute-done | bytes 86048 | tf_op jit(solution)/shard_map/ppermute | solution.py:461
  11.7 4.1 %collective-permute-done.3.got2 = f32[168,128]{1,0:T(8,128)S(1)} collective-permute-done((f32[168,128]{1,0:T(8,128)S(1)}, f32[168,128]{1,0:T(8,128)S(1)}, u32[]{:S(2)}, u32[]{:S(2)}) %collective-permute-start.3) | collective-permute-done | bytes 86048 | tf_op jit(solution)/shard_map/ppermute | solution.py:460
  15.8 2.1 %shard_map.52 = (f32[3,17,6,128]{3,2,1,0:T(8,128)S(1)}, f32[3,17,6,128]{3,2,1,0:T(8,128)S(1)}, f32[3,96,128]{2,1,0:T(8,128)S(1)}, f32[8,128]{1,0:T(8,128)S(1)}) custom-call(f32[17,6,128]{2,1,0:T(8,128)S(1)} %get-tuple-element.29.rhs_0, f32[17,6,128]{2,1,0:T(8,128)S(1)} %get-tuple-element.30.rhs_1, f32[17,6,128]{2,1,0:T(8,128)S(1)} %get-tuple-element.28.rhs_2, ...), custom_call_target="tpu_custom_call" | custom-call | tf_op jit(solution)/shard_map/pallas_call | solution.py:513
  17.9 0.7 %collective-permute-start.6 = (f32[8,128]{1,0:T(8,128)S(1)}, f32[8,128]{1,0:T(8,128)S(1)}, u32[]{:S(2)}, u32[]{:S(2)}) collective-permute-start(f32[8,128]{1,0:T(8,128)S(1)} %get-tuple-element.25), channel_id=1, source_target_pairs={{0,3},{1,2},{2,1},{3,0},{4,7},{5,6},{6,5},{7,4},{8,11},{9,10},{10,... | collective-permute-start | bytes 12296 | tf_op jit(solution)/shard_map/ppermute | solution.py:476
  18.5 0.9 %collective-permute-start.5 = (f32[8,128]{1,0:T(8,128)S(1)}, f32[8,128]{1,0:T(8,128)S(1)}, u32[]{:S(2)}, u32[]{:S(2)}) collective-permute-start(f32[8,128]{1,0:T(8,128)S(1)} %get-tuple-element.25), channel_id=1, source_target_pairs={{0,2},{1,3},{2,0},{3,1},{4,6},{5,7},{6,4},{7,5},{8,10},{9,11},{10,... | collective-permute-start | bytes 12296 | tf_op jit(solution)/shard_map/ppermute | solution.py:476
  19.4 0.3 %collective-permute-start.4 = (f32[8,128]{1,0:T(8,128)S(1)}, f32[8,128]{1,0:T(8,128)S(1)}, u32[]{:S(2)}, u32[]{:S(2)}) collective-permute-start(f32[8,128]{1,0:T(8,128)S(1)} %get-tuple-element.25), channel_id=1, source_target_pairs={{0,1},{1,0},{2,3},{3,2},{4,5},{5,4},{6,7},{7,6},{8,9},{9,8},{10,11... | collective-permute-start | bytes 12296 | tf_op jit(solution)/shard_map/ppermute | solution.py:476
  19.8 1.2 %collective-permute-done.6 = f32[8,128]{1,0:T(8,128)S(1)} collective-permute-done((f32[8,128]{1,0:T(8,128)S(1)}, f32[8,128]{1,0:T(8,128)S(1)}, u32[]{:S(2)}, u32[]{:S(2)}) %collective-permute-start.6) | collective-permute-done | bytes 4128 | tf_op jit(solution)/shard_map/ppermute | solution.py:476
  20.9 1.3 %collective-permute-done.5 = f32[8,128]{1,0:T(8,128)S(1)} collective-permute-done((f32[8,128]{1,0:T(8,128)S(1)}, f32[8,128]{1,0:T(8,128)S(1)}, u32[]{:S(2)}, u32[]{:S(2)}) %collective-permute-start.5) | collective-permute-done | bytes 4128 | tf_op jit(solution)/shard_map/ppermute | solution.py:476
  22.2 0.0 collective-permute-done.4
  22.2 1.5 %collective-permute-start.9 = (f32[8,128]{1,0:T(8,128)S(1)}, f32[8,128]{1,0:T(8,128)S(1)}, u32[]{:S(2)}, u32[]{:S(2)}) collective-permute-start(f32[8,128]{1,0:T(8,128)S(1)} %add_add_fusion.1), channel_id=1, source_target_pairs={{0,12},{4,8},{8,4},{12,0},{1,13},{5,9},{9,5},{13,1},{2,14},{6,10},... | collective-permute-start | bytes 12296 | tf_op jit(solution)/shard_map/ppermute | solution.py:476
  23.7 0.2 collective-permute-start.8
  23.9 2.8 %collective-permute-start.7 = (f32[8,128]{1,0:T(8,128)S(1)}, f32[8,128]{1,0:T(8,128)S(1)}, u32[]{:S(2)}, u32[]{:S(2)}) collective-permute-start(f32[8,128]{1,0:T(8,128)S(1)} %add_add_fusion.1), channel_id=1, source_target_pairs={{0,4},{4,0},{8,12},{12,8},{1,5},{5,1},{9,13},{13,9},{2,6},{6,2},{1... | collective-permute-start | bytes 12296 | tf_op jit(solution)/shard_map/ppermute | solution.py:476
  26.6 1.0 %collective-permute-done.9 = f32[8,128]{1,0:T(8,128)S(1)} collective-permute-done((f32[8,128]{1,0:T(8,128)S(1)}, f32[8,128]{1,0:T(8,128)S(1)}, u32[]{:S(2)}, u32[]{:S(2)}) %collective-permute-start.9) | collective-permute-done | bytes 4128 | tf_op jit(solution)/shard_map/ppermute | solution.py:476
  27.7 0.5 %collective-permute-done.8 = f32[8,128]{1,0:T(8,128)S(1)} collective-permute-done((f32[8,128]{1,0:T(8,128)S(1)}, f32[8,128]{1,0:T(8,128)S(1)}, u32[]{:S(2)}, u32[]{:S(2)}) %collective-permute-start.8) | collective-permute-done | bytes 4128 | tf_op jit(solution)/shard_map/ppermute | solution.py:476
  28.2 0.1 collective-permute-done.7
  28.2 0.7 %shard_map.53 = (f32[3,17,6,128]{3,2,1,0:T(8,128)}, f32[96,128]{1,0:T(8,128)}) custom-call(f32[3,17,6,128]{3,2,1,0:T(8,128)S(1)} %get-tuple-element.22.base, f32[3,17,6,128]{3,2,1,0:T(8,128)S(1)} %get-tuple-element.23.second, f32[3,96,128]{2,1,0:T(8,128)S(1)} %get-tuple-element.24.energy, f32[8,128]{1,0:T(8,128)S(1)} %add_add_fusion.sums), custom_call_target="tpu_custom_call" | custom-call | tf_op jit(solution)/shard_map/pallas_call | solution.py:531
  (2 shorter events, 0.0 us)
Async XLA Ops:
  0.6 1.1 %copy-start = (s32[17,6,128]{2,1,0:T(8,128)S(1)}, s32[17,6,128]{2,1,0:T(8,128)}, u32[]{:S(2)}) copy-start(s32[17,6,128]{2,1,0:T(8,128)} %fixed.3) | copy-start | bytes 156676
  0.6 1.1 %copy-start.1 = (s32[16,6,128]{2,0,1:T(8,128)S(1)}, s32[16,6,128]{2,0,1:T(8,128)}, u32[]{:S(2)}) copy-start(s32[16,6,128]{2,0,1:T(8,128)} %param.4) | copy-start | bytes 147460
  2.1 3.1 %collective-permute-start = (f32[2,8,128]{2,1,0:T(8,128)S(1)}, f32[2,8,128]{2,1,0:T(8,128)S(1)}, u32[]{:S(2)}, u32[]{:S(2)}) collective-permute-start(f32[2,8,128]{2,1,0:T(8,128)S(1)} %get-tuple-element.15.own1), channel_id=1, source_target_pairs={{0,1},{1,0},{2,3},{3,2},{4,5},{5,4},{6,7},{7,6},{8,9},{9,8},{10,11... | collective-permute-start | bytes 24584 | tf_op jit(solution)/shard_map/ppermute | solution.py:461
  2.6 4.0 %collective-permute-start.1 = (f32[2,8,128]{2,1,0:T(8,128)S(1)}, f32[2,8,128]{2,1,0:T(8,128)S(1)}, u32[]{:S(2)}, u32[]{:S(2)}) collective-permute-start(f32[2,8,128]{2,1,0:T(8,128)S(1)} %get-tuple-element.16.own2), channel_id=1, source_target_pairs={{0,3},{1,2},{2,1},{3,0},{4,7},{5,6},{6,5},{7,4},{8,11},{9,10},{10,... | collective-permute-start | bytes 24584 | tf_op jit(solution)/shard_map/ppermute | solution.py:460
  6.7 5.0 %collective-permute-start.2 = (f32[168,128]{1,0:T(8,128)S(1)}, f32[168,128]{1,0:T(8,128)S(1)}, u32[]{:S(2)}, u32[]{:S(2)}) collective-permute-start(f32[168,128]{1,0:T(8,128)S(1)} %get-tuple-element.20), channel_id=1, source_target_pairs={{0,4},{4,0},{8,12},{12,8},{1,5},{5,1},{9,13},{13,9},{2,6},{6,2},{1... | collective-permute-start | bytes 258056 | tf_op jit(solution)/shard_map/ppermute | solution.py:461
  8.5 7.3 %collective-permute-start.3 = (f32[168,128]{1,0:T(8,128)S(1)}, f32[168,128]{1,0:T(8,128)S(1)}, u32[]{:S(2)}, u32[]{:S(2)}) collective-permute-start(f32[168,128]{1,0:T(8,128)S(1)} %get-tuple-element.21), channel_id=1, source_target_pairs={{0,12},{4,8},{8,4},{12,0},{1,13},{5,9},{9,5},{13,1},{2,14},{6,10},... | collective-permute-start | bytes 258056 | tf_op jit(solution)/shard_map/ppermute | solution.py:460
  17.9 3.0 %collective-permute-start.6 = (f32[8,128]{1,0:T(8,128)S(1)}, f32[8,128]{1,0:T(8,128)S(1)}, u32[]{:S(2)}, u32[]{:S(2)}) collective-permute-start(f32[8,128]{1,0:T(8,128)S(1)} %get-tuple-element.25), channel_id=1, source_target_pairs={{0,3},{1,2},{2,1},{3,0},{4,7},{5,6},{6,5},{7,4},{8,11},{9,10},{10,... | collective-permute-start | bytes 12296 | tf_op jit(solution)/shard_map/ppermute | solution.py:476
  18.5 3.6 %collective-permute-start.5 = (f32[8,128]{1,0:T(8,128)S(1)}, f32[8,128]{1,0:T(8,128)S(1)}, u32[]{:S(2)}, u32[]{:S(2)}) collective-permute-start(f32[8,128]{1,0:T(8,128)S(1)} %get-tuple-element.25), channel_id=1, source_target_pairs={{0,2},{1,3},{2,0},{3,1},{4,6},{5,7},{6,4},{7,5},{8,10},{9,11},{10,... | collective-permute-start | bytes 12296 | tf_op jit(solution)/shard_map/ppermute | solution.py:476
  19.4 2.7 %collective-permute-start.4 = (f32[8,128]{1,0:T(8,128)S(1)}, f32[8,128]{1,0:T(8,128)S(1)}, u32[]{:S(2)}, u32[]{:S(2)}) collective-permute-start(f32[8,128]{1,0:T(8,128)S(1)} %get-tuple-element.25), channel_id=1, source_target_pairs={{0,1},{1,0},{2,3},{3,2},{4,5},{5,4},{6,7},{7,6},{8,9},{9,8},{10,11... | collective-permute-start | bytes 12296 | tf_op jit(solution)/shard_map/ppermute | solution.py:476
  22.2 5.5 %collective-permute-start.9 = (f32[8,128]{1,0:T(8,128)S(1)}, f32[8,128]{1,0:T(8,128)S(1)}, u32[]{:S(2)}, u32[]{:S(2)}) collective-permute-start(f32[8,128]{1,0:T(8,128)S(1)} %add_add_fusion.1), channel_id=1, source_target_pairs={{0,12},{4,8},{8,4},{12,0},{1,13},{5,9},{9,5},{13,1},{2,14},{6,10},... | collective-permute-start | bytes 12296 | tf_op jit(solution)/shard_map/ppermute | solution.py:476
  23.7 4.5 %collective-permute-start.8 = (f32[8,128]{1,0:T(8,128)S(1)}, f32[8,128]{1,0:T(8,128)S(1)}, u32[]{:S(2)}, u32[]{:S(2)}) collective-permute-start(f32[8,128]{1,0:T(8,128)S(1)} %add_add_fusion.1), channel_id=1, source_target_pairs={{0,8},{4,12},{8,0},{12,4},{1,9},{5,13},{9,1},{13,5},{2,10},{6,14},... | collective-permute-start | bytes 12296 | tf_op jit(solution)/shard_map/ppermute | solution.py:476
  23.9 4.4 %collective-permute-start.7 = (f32[8,128]{1,0:T(8,128)S(1)}, f32[8,128]{1,0:T(8,128)S(1)}, u32[]{:S(2)}, u32[]{:S(2)}) collective-permute-start(f32[8,128]{1,0:T(8,128)S(1)} %add_add_fusion.1), channel_id=1, source_target_pairs={{0,4},{4,0},{8,12},{12,8},{1,5},{5,1},{9,13},{13,9},{2,6},{6,2},{1... | collective-permute-start | bytes 12296 | tf_op jit(solution)/shard_map/ppermute | solution.py:476

commit v4 on v3

v4 whole, which is shorter than its diff:
```python
import functools

import jax
import jax.numpy as jnp
import numpy as np
from jax import lax
from jax.experimental import pallas as pl
from jax.experimental.pallas import tpu as pltpu
from jax.sharding import PartitionSpec as P

PHASE_STIFFNESS = (0.125, 0.343, 0.614, 1.0)
PHASE_SLOPE = (0.75, 1.47, 2.17, 3.0)
POISSON = 0.3
LAME = POISSON / ((1.0 + POISSON) * (1.0 - 2.0 * POISSON))
SHEAR = 1.0 / (2.0 * (1.0 + POISSON))
KE_DIAGONAL = (LAME + 4.0 * SHEAR) / 9.0

SLOTS = 7
LANES = 128
FULL = 168
CORNERS = 152

VMEM = pl.BlockSpec(memory_space=pltpu.VMEM)
PARAMS = pltpu.CompilerParams(vmem_limit_bytes=32 * 1024 * 1024)


def lanes():
    return lax.broadcasted_iota(jnp.int32, (8, LANES), 1)


def sublanes():
    return lax.broadcasted_iota(jnp.int32, (8, LANES), 0)


def table(phase, values):
    out = jnp.full(phase.shape, values[3], jnp.float32)
    for index in (2, 1, 0):
        out = jnp.where(phase == index, jnp.float32(values[index]), out)
    return out


def element_rows(ref, k, layers):
    return ref[pl.ds(k, ref.shape[0] // layers, stride=layers), :]


def lane_roll(x, by):
    if isinstance(by, int):
        by = by % LANES
        return x if by == 0 else pltpu.roll(x, by, 1)
    return pltpu.roll(x, lax.rem(by + LANES, LANES), 1)


def is_even(axis):
    return lax.rem(lax.axis_index(axis), 2) == 0


def gather(nodes, *items):
    lane = lanes()
    slot = jnp.where(lane < nodes * SLOTS, lax.rem(lane, SLOTS), SLOTS)
    out = jnp.zeros((8, LANES), jnp.float32)
    for plane, by, first, count in items:
        out = jnp.where((slot >= first) & (slot < first + count), lane_roll(plane, by), out)
    return out


def column_kernel(paired, rhs_0, rhs_1, rhs_2, phase, fixed, own, col1, col2, pad):
    rhs = (rhs_0, rhs_1, rhs_2)
    nodes, rows, width = rhs_0.shape
    layers = nodes - 1
    lane = lanes()
    even = is_even("gy") if paired else True
    pad[...] = jnp.zeros(pad.shape, jnp.float32)
    planes = [jnp.zeros((8, LANES), jnp.float32)] * 5
    for k in range(nodes):
        here = (lane >= k * SLOTS) & (lane < k * SLOTS + 5)
        values = [rhs[c][k] for c in range(3)]
        values.append(table(element_rows(phase, k, layers), PHASE_STIFFNESS) if k < layers else None)
        values.append((1 - fixed[k]).astype(jnp.float32))
        for p, value in enumerate(values):
            if value is not None:
                pad[5 * k + p, 0:rows, :] = value
                planes[p] = jnp.where(here, lane_roll(pad[5 * k + p], k * SLOTS + 3), planes[p])
    for p in range(5):
        own[p] = planes[p]
    high = [
        gather(nodes, (planes[0], -2, 0, 1), (planes[1], -1, 1, 1), (planes[2], 0, 2, 1), (planes[3], 2, 3, 2)),
        jnp.zeros((8, LANES), jnp.float32),
    ]
    low = [
        gather(nodes, (planes[0], -3, 0, 2), (planes[1], -1, 2, 2), (planes[2], 1, 4, 2), (planes[4], 3, 6, 1)),
        planes[3],
    ]
    for p in range(2):
        if paired:
            col1[p] = jnp.where(even, high[p], low[p])
            col2[p] = jnp.where(even, low[p], high[p])
        else:
            col1[p] = low[p]
            col2[p] = high[p]


def row_kernel(paired, rhs_0, rhs_1, rhs_2, phase, fixed, row1, row2):
    rhs = (rhs_0, rhs_1, rhs_2)
    nodes, rows, width = rhs_0.shape
    layers, cn = nodes - 1, 3 * nodes
    even = is_even("gx") if paired else True
    nothing = jnp.zeros((1, LANES), jnp.float32)

    def put(at, low, high):
        if paired:
            row1[at : at + 1, :] = jnp.where(even, high, low)
            row2[at : at + 1, :] = jnp.where(even, low, high)
        else:
            row1[at : at + 1, :] = low
            row2[at : at + 1, :] = high

    for k in range(nodes):
        for c in range(3):
            q = c * nodes + k
            put(q, rhs[c][k, 0:1], rhs[c][k, rows - 1 : rows])
            put(cn + 2 * layers + q, rhs[c][k, 1:2], nothing)
        put(2 * cn + 2 * layers + k, (1 - fixed[k, 0:1]).astype(jnp.float32), nothing)
    scale = [table(phase[i * layers : (i + 1) * layers], PHASE_STIFFNESS) for i in (0, 1, rows - 2, rows - 1)]
    for i in range(2):
        at = cn + i * layers
        if paired:
            row1[at : at + layers, :] = jnp.where(even, scale[2 + i], scale[i])
            row2[at : at + layers, :] = jnp.where(even, scale[i], scale[2 + i])
        else:
            row1[at : at + layers, :] = scale[i]
            row2[at : at + layers, :] = scale[2 + i]
    used = 2 * cn + 2 * layers + nodes
    row1[used:, :] = jnp.zeros((FULL - used, LANES), jnp.float32)
    row2[used:, :] = jnp.zeros((FULL - used, LANES), jnp.float32)


def strip_kernel(nodes, paired_x, paired_y, own, got1, got2, row1, row2, strip, out1, out2):
    even_x = is_even("gx") if paired_x else True
    even_y = is_even("gy") if paired_y else True
    if paired_y:
        from_low = jnp.where(even_y, got2[0], got1[0])
        from_high = [jnp.where(even_y, got1[p], got2[p]) for p in range(2)]
    else:
        from_low, from_high = got2[0], [got1[p] for p in range(2)]
    planes = [
        gather(nodes, (from_low, -c, 0, 1), (own[c], -2, 1, 2), (own[c], 2, 3, 2), (from_high[0], 5 - 2 * c, 5, 2))
        for c in range(3)
    ]
    scale = own[3]
    planes.append(gather(nodes, (from_low, -3, 0, 2), (scale, -1, 2, 1), (scale, 3, 3, 3), (from_high[1], 3, 6, 1)))
    planes.append(gather(nodes, (from_low, -4, 0, 1), (scale, -2, 1, 2), (scale, 2, 3, 2), (from_high[1], 2, 5, 2)))
    planes.append(gather(nodes, (own[4], -2, 1, 1), (own[4], 2, 4, 1), (from_high[0], -1, 5, 1)))
    rows = 6
    out1[...] = row1[...]
    out2[...] = row2[...]
    for p, plane in enumerate(planes):
        strip[p] = plane
        for which in range(2):
            at = CORNERS + 2 * p + which
            low_row = plane[which : which + 1]
            high_row = plane[rows - 2 + which : rows - 1 + which]
            if paired_x:
                out1[at : at + 1, :] = jnp.where(even_x, high_row, low_row)
                out2[at : at + 1, :] = jnp.where(even_x, low_row, high_row)
            else:
                out1[at : at + 1, :] = low_row
                out2[at : at + 1, :] = high_row


PLANE = ("", "1", "2", "12")


def split_layers(lo, hi):
    sums = [{m: lo[c][m] + hi[c][m] for m in ("1", "2", "12")} for c in range(3)]
    diffs = [{m: hi[c][m] - lo[c][m] for m in PLANE} for c in range(3)]
    u, v, w = range(3)
    return (
        diffs[u][""], sums[v]["1"], sums[w]["2"],
        sums[u]["1"] + diffs[v][""], sums[u]["2"] + diffs[w][""], sums[v]["2"] + sums[w]["1"],
        diffs[u]["1"], sums[w]["12"], diffs[u]["2"], sums[v]["12"], diffs[v]["1"], diffs[w]["2"],
        sums[u]["12"], diffs[v]["2"], diffs[w]["1"],
        diffs[u]["12"], diffs[v]["12"], diffs[w]["12"],
    )


def stress(m):
    one, two, three = 1.0 / 16.0, 1.0 / 48.0, 1.0 / 144.0
    trace = (LAME * one) * (m[0] + m[1] + m[2])
    out = [trace + (2.0 * SHEAR * one) * m[i] for i in range(3)]
    out += [(SHEAR * one) * m[i] for i in (3, 4, 5)]
    own, other = (LAME + 3.0 * SHEAR) * two, LAME * two
    for i in (6, 8, 10):
        out += [own * m[i] + other * m[i + 1], own * m[i + 1] + other * m[i]]
    total = m[12] + m[13] + m[14]
    out += [(SHEAR * two) * (m[i] + total) for i in (12, 13, 14)]
    out += [((LAME + 4.0 * SHEAR) * three) * m[i] for i in (15, 16, 17)]
    return out


def inner(g, m):
    parts = [g[i] * m[i] for i in range(18)]
    while len(parts) > 1:
        parts = [parts[i] + parts[i + 1] if i + 1 < len(parts) else parts[i] for i in range(0, len(parts), 2)]
    return parts[0]


def join_layers(g):
    sums = [
        {"1": g[3], "2": g[4], "12": g[12]},
        {"1": g[1], "2": g[5], "12": g[9]},
        {"1": g[5], "2": g[2], "12": g[7]},
    ]
    diffs = [
        {"": g[0], "1": g[6], "2": g[8], "12": g[15]},
        {"": g[3], "1": g[10], "2": g[13], "12": g[16]},
        {"": g[4], "1": g[14], "2": g[11], "12": g[17]},
    ]
    lower = [{m: (sums[c][m] - diffs[c][m] if m else -diffs[c][m]) for m in PLANE} for c in range(3)]
    upper = [{m: (sums[c][m] + diffs[c][m] if m else diffs[c][m]) for m in PLANE} for c in range(3)]
    return lower, upper


def in_plane(x, right, up):
    y = right(x)
    near, far = x + y, y - x
    near_up, far_up = up(near), up(far)
    return {"": near + near_up, "1": near_up - near, "2": far + far_up, "12": far_up - far}


def out_of_plane(f, right, up):
    plain = (f[""] - f["2"]) + right(f[""] + f["2"])
    steep = (f["1"] - f["12"]) + right(f["1"] + f["12"])
    return (plain - steep) + up(plain + steep)


def operator_kernel(
    paired_x, rhs_0, rhs_1, rhs_2, phase, fixed, strip, got1, got2,
    base, second, edges, sums,
    lo, hi, held, residual, inverse, dense, far_base,
):
    rhs, comps = (rhs_0, rhs_1, rhs_2), 3
    nodes, rows, width = rhs_0.shape
    layers = nodes - 1
    lane, row = lanes(), sublanes()
    last_row, below = row == 6, row == 7
    cn = comps * nodes
    if paired_x:
        even_x = is_even("gx")
        lo[...] = jnp.where(even_x, got2[...], got1[...])
        hi[...] = jnp.where(even_x, got1[...], got2[...])
    else:
        lo[...] = got2[...]
        hi[...] = got1[...]

    def spread(ref, at):
        return jnp.broadcast_to(ref[pl.ds(at, 1), :], (8, LANES))

    def roll_up(x):
        return pltpu.roll(x, 7, 0)

    def roll_down(x):
        return pltpu.roll(x, 1, 0)

    def node_rows(x, x_m2):
        return x + jnp.where(below, x_m2, roll_down(x))

    def node_row_7(x, x_7):
        return jnp.broadcast_to(x[6:7], (8, LANES)) + x_7

    def plane_modes(x, y, x_up, y_up):
        near, far, near_up, far_up = x + y, y - x, x_up + y_up, y_up - x_up
        return {"": near + near_up, "1": near_up - near, "2": far + far_up, "12": far_up - far}

    def node_forces(f, by):
        sides = []
        for sign in (-1, 1):
            plain = f[""] + f["2"] if sign > 0 else f[""] - f["2"]
            steep = f["1"] + f["12"] if sign > 0 else f["1"] - f["12"]
            sides.append((plain - steep) + roll_down(plain + steep))
        return sides[0] + lane_roll(sides[1], by)

    def products(totals, d0, image, z, s, v):
        return tuple(t + x for t, x in zip(totals, (d0 * image, image * z, s * v, v * image)))

    def corner(ref, p, which):
        return spread(ref, CORNERS + 2 * p + which)

    tiles = [
        jnp.where(row < 6, strip[p], jnp.where(last_row, corner(hi, p, 0), corner(lo, p, 1))) for p in range(6)
    ]
    sevens = [corner(hi, p, 1) for p in range(5)]
    left, right = tiles[3], tiles[4]
    edge_rows = node_rows(right, corner(lo, 4, 0))
    edge_rows_7 = node_row_7(right, sevens[4])

    tall = lax.broadcasted_iota(jnp.int32, (layers, LANES), 0)
    wide = lax.broadcasted_iota(jnp.int32, (layers, LANES), 1)
    pair = hi[cn : cn + layers, :] + hi[cn + layers : cn + 2 * layers, :]
    edge = jnp.broadcast_to(edge_rows_7[0:1], (layers, LANES))
    edge = jnp.sum(jnp.where(wide == SLOTS * tall, edge, 0.0), axis=1, keepdims=True)
    dense[...] = jnp.zeros(dense.shape, jnp.float32)
    dense[1 : layers + 1, :] = pair + jnp.where(wide == 0, edge, pltpu.roll(pair, 1, 1))
    inv_7 = dense[0:24, :] + dense[1:25, :]
    inv_7 = jnp.where(inv_7 > 0.0, 1.0 / (KE_DIAGONAL * inv_7), 0.0)
    for c in range(3):
        x_7 = hi[cn + 2 * layers + c * nodes : cn + 2 * layers + c * nodes + 24, :] * inv_7
        far_base[c] = x_7
        far_base[3 + c] = pltpu.roll(x_7, LANES - 1, 1)

    def strip_diagonal(x):
        return KE_DIAGONAL * (x + lane_roll(x, SLOTS))

    strip_diag = strip_diagonal(node_rows(left + right, corner(lo, 3, 0) + corner(lo, 4, 0)))
    strip_diag_7 = strip_diagonal(node_row_7(left + right, sevens[3] + sevens[4]))
    strip_inv = jnp.where(strip_diag > 0.0, 1.0 / strip_diag, 0.0)
    strip_inv_7 = jnp.where(strip_diag_7 > 0.0, 1.0 / strip_diag_7, 0.0)
    slot = lax.rem(lane, SLOTS)
    strip_scale = jnp.where((slot == 2) | (slot == 6), 0.0, right)
    strip_base = [tiles[c] * strip_inv for c in range(3)]

    def strip_layers(modes):
        return [{m: lane_roll(modes[c][m], -SLOTS) for m in PLANE} for c in range(3)]

    lower = []
    for c in range(3):
        x, x_7 = strip_base[c], sevens[c] * strip_inv_7
        y, y_7 = lane_roll(x, -1), lane_roll(x_7, -1)
        lower.append(plane_modes(x, y, jnp.where(last_row, x_7, roll_up(x)), jnp.where(last_row, y_7, roll_up(y))))
    f_low, f_up = join_layers([strip_scale * x for x in stress(split_layers(lower, strip_layers(lower)))])
    strip_second, strip_sums = [], (0.0,) * 4
    for c in range(3):
        f = node_forces({m: f_low[c][m] + lane_roll(f_up[c][m], SLOTS) for m in PLANE}, 1)
        image = jnp.where(tiles[5] > 0.0, f, 0.0)
        s = jnp.where(tiles[5] > 0.0, f - tiles[c], 0.0)
        strip_second.append(s * strip_inv)
        strip_sums = products(strip_sums, strip_base[c], image, image * strip_inv, s, strip_second[c])
        edges[c] = strip_base[c]
        edges[3 + c] = strip_second[c]
    ends = [jnp.where(slot == 4, x, lane_roll(x, 4)) for x in strip_second]
    lower = [plane_modes(x, lane_roll(x, -1), roll_up(x), roll_up(lane_roll(x, -1))) for x in strip_second]
    m = split_layers(lower, strip_layers(lower))
    strip_e = strip_scale * inner(stress(m), m)

    def box(k):
        held[0, 0:rows, :] = table(element_rows(phase, k, layers), PHASE_STIFFNESS)
        held[0, 6:7, :] = hi[pl.ds(cn + k, 1), :]
        held[0, 7:8, :] = lo[pl.ds(cn + layers + k, 1), :]
        x = held[0]
        r = node_rows(x, spread(lo, cn + k))
        return x, r + jnp.where(lane == 0, lane_roll(edge_rows, -SLOTS * k), lane_roll(r, 1))

    def first_layer(k, around_node):
        inv = 1.0 / (KE_DIAGONAL * around_node)
        inverse[k] = inv
        out = []
        for c in range(3):
            q = c * nodes + k
            residual[q, 0:rows, :] = rhs[c][k]
            residual[q, 6:7, :] = hi[pl.ds(q, 1), :]
            residual[q, 7:8, :] = lo[pl.ds(q, 1), :]
            x = residual[q] * inv
            base[q] = x
            y = lane_roll(x, -1)
            x_up = jnp.where(last_row, spread(far_base.at[c], k), roll_up(x))
            y_up = jnp.where(last_row, spread(far_base.at[3 + c], k), roll_up(y))
            out.append(plane_modes(x, y, x_up, y_up))
        return out

    def finish_layer(k, f, totals):
        inv = inverse[k]
        held[1, 0:rows, :] = 1.0 - fixed[k].astype(jnp.float32)
        held[1, 6:7, :] = hi[pl.ds(2 * cn + 2 * layers + k, 1), :]
        free = held[1] > 0.0
        inv = jnp.where(free, inv, 1.0)
        a, rest = totals[0], totals[1:]
        for c in range(3):
            q = c * nodes + k
            r0 = residual[q]
            d0 = r0 * inv
            image = jnp.where(free, node_forces(f[c], 1), d0)
            s = image - r0
            v = s * inv
            ends_now = lane_roll(ends[c], LANES - 1 - (SLOTS * k + 4))
            second[q] = jnp.where((lane == 0) | (lane == LANES - 1), ends_now, v)
            a, rest = a + r0 * d0, products(rest, d0, image, image * inv, s, v)
        return (a,) + rest

    def flat(x):
        return tuple(x[c][m] for c in range(3) for m in PLANE)

    def unflat(x):
        return [{m: x[4 * c + i] for i, m in enumerate(PLANE)} for c in range(3)]

    zero = jnp.zeros((8, LANES), jnp.float32)
    held[1] = zero
    held[2] = zero

    def element(k, low_modes, high_modes, scale, pending, totals):
        g = stress(split_layers(low_modes, high_modes))
        f_lower, f_upper = join_layers([scale * x for x in g])
        done = [{m: pending[c][m] + f_lower[c][m] for m in PLANE} for c in range(3)]
        return f_upper, finish_layer(k, done, totals)

    def forward(k, carry):
        low_modes, pending, totals, scale, b = carry
        next_scale, next_b = box(k + 1)
        high = first_layer(k + 1, b + next_b)
        f_upper, totals = element(k, unflat(low_modes), high, scale, unflat(pending), totals)
        return flat(high), flat(f_upper), totals, next_scale, next_b

    scale, b = box(0)
    carry = (flat(first_layer(0, b)), (zero,) * 12, (zero,) * 5, scale, b)
    low_modes, pending, totals, scale, b = lax.fori_loop(0, layers - 1, forward, carry, unroll=True)
    high = first_layer(layers, b)
    f_upper, totals = element(layers - 1, unflat(low_modes), high, scale, unflat(pending), totals)
    totals = finish_layer(layers, f_upper, totals)

    def second_layer(k):
        out = []
        for c in range(3):
            x = second[c * nodes + k]
            y = lane_roll(x, -1)
            out.append(plane_modes(x, y, roll_up(x), roll_up(y)))
        return out

    def again(k, carry):
        low_modes, total = carry
        high = second_layer(k + 1)
        m = split_layers(unflat(low_modes), high)
        held[2, 0:rows, :] = table(element_rows(phase, k, layers), PHASE_STIFFNESS)
        return flat(high), total + held[2] * inner(stress(m), m)

    _, total = lax.fori_loop(0, layers, again, (flat(second_layer(0)), zero), unroll=True)
    mine = row < rows
    inside = mine & (lane > 0) & (lane < LANES - 1)
    at_ends = mine & ((slot == 1) | (slot == 4))
    totals = [jnp.where(mine, totals[0], 0.0)] + [
        jnp.where(inside, x, 0.0) + jnp.where(at_ends, y, 0.0) for x, y in zip(totals[1:], strip_sums)
    ]
    totals.append(
        jnp.where(mine & (lane < LANES - 1), total, 0.0) + jnp.where(mine & (slot == 4), strip_e, 0.0)
    )
    for i, x in enumerate(totals):
        x = jnp.sum(jnp.sum(x, axis=0, keepdims=True), axis=1, keepdims=True)
        sums[i : i + 1, :] = jnp.broadcast_to(x, (1, LANES))
    sums[6:, :] = jnp.zeros((2, LANES), jnp.float32)


def energy_kernel(base, second, edges, phase, energy):
    nodes = base.shape[0] // 3
    layers = nodes - 1
    rows = phase.shape[0] // layers
    lane = lanes()

    def layer(field, first_edge, k):
        out = []
        for c in range(3):
            fill = lane_roll(edges[first_edge + c], LANES - 1 - (SLOTS * k + 5))
            out.append(
                in_plane(
                    field[c * nodes + k],
                    lambda t: jnp.where(lane == LANES - 1, fill, lane_roll(t, -1)),
                    lambda t: pltpu.roll(t, 7, 0),
                )
            )
        return out

    low = layer(base, 0, 0), layer(second, 3, 0)
    for k in range(layers):
        high = layer(base, 0, k + 1), layer(second, 3, k + 1)
        m, n = split_layers(low[0], high[0]), split_layers(low[1], high[1])
        g, h = stress(m), stress(n)
        slope = -table(element_rows(phase, k, layers), PHASE_SLOPE)
        for which, value in enumerate((inner(g, m), inner(h, m), inner(h, n))):
            energy[which, pl.ds(k, rows, stride=layers), :] = slope * value[0:rows]
        low = high


def combine_kernel(base, second, energy, sums, displacement, sensitivity):
    a, curve, plain, shifted, cross, bend = (sums[i : i + 1, :] for i in range(6))
    slope = curve / a
    alpha = a / curve
    less = 1.0 - slope
    rest = jnp.where(slope < 0.5, plain - slope * curve, shifted - less * less * a)
    bend = bend + 2.0 * less * cross + less * less * curve
    alpha_next = rest / (bend - rest * rest / curve)
    beta = alpha * alpha * rest / a
    first = alpha + alpha_next * beta - alpha * alpha_next * less
    other = -alpha * alpha_next
    comps, nodes, rows, width = displacement.shape
    for c in range(comps):
        for k in range(nodes):
            q = c * nodes + k
            displacement[c, k] = (first * base[q] + other * second[q])[0:rows]
    sensitivity[...] = (first * first) * energy[0] + (2.0 * first * other) * energy[1] + (other * other) * energy[2]


def exchange(one, two, axis):
    count = lax.axis_size(axis)
    if count % 2 == 0:
        far = lax.ppermute(two, axis, [(i, (i - 1) % count if i % 2 == 0 else (i + 1) % count) for i in range(count)])
        near = lax.ppermute(one, axis, [(i, i ^ 1) for i in range(count)])
        return near, far
    high = lax.ppermute(one, axis, [((i + 1) % count, i) for i in range(count)])
    low = lax.ppermute(two, axis, [(i, (i + 1) % count) for i in range(count)])
    return high, low


def total_over(x, axis, order):
    count = lax.axis_size(axis)
    if count & (count - 1):
        return lax.psum(x, axis)
    step = 1
    while step < count:
        width = 4 if count // step >= 4 else 2
        group = [
            lax.ppermute(x, axis, [(i, i ^ (step * by)) for i in range(count)]) for by in order if by < width
        ]
        x = functools.reduce(jnp.add, group, x)
        step *= width
    return x


def body(force, phase, fixed):
    comps, nodes, rows, width = force.shape
    layers = nodes - 1
    phase = phase.transpose(1, 0, 2).reshape(rows * layers, width)
    rhs = [(1 - fixed).astype(jnp.float32) * force[c] for c in range(comps)]
    f32 = jnp.float32
    paired_x = lax.axis_size("gx") % 2 == 0
    paired_y = lax.axis_size("gy") % 2 == 0
    column = jax.ShapeDtypeStruct((2, 8, LANES), f32)
    message = jax.ShapeDtypeStruct((FULL, LANES), f32)

    def call(kernel, out_shape, scratch=()):
        return pl.pallas_call(
            kernel,
            out_shape=out_shape,
            scratch_shapes=scratch,
            compiler_params=PARAMS,
        )

    strips = jax.ShapeDtypeStruct((6, 8, LANES), f32)
    own, col1, col2 = call(
        functools.partial(column_kernel, paired_y),
        (jax.ShapeDtypeStruct((5, 8, LANES), f32), column, column),
        [pltpu.VMEM((5 * nodes, 8, LANES), f32)],
    )(*rhs, phase, fixed)
    row1, row2 = call(functools.partial(row_kernel, paired_x), (message, message))(*rhs, phase, fixed)
    near, far = exchange(col1, col2, "gy")
    strip, row1, row2 = call(
        functools.partial(strip_kernel, nodes, paired_x, paired_y),
        (strips, message, message),
    )(own, near, far, row1, row2)
    near, far = exchange(row1, row2, "gx")
    field = jax.ShapeDtypeStruct((comps * nodes, 8, LANES), f32)
    base, second, edges, sums = call(
        functools.partial(operator_kernel, paired_x),
        (
            field,
            field,
            strips,
            jax.ShapeDtypeStruct((8, LANES), f32),
        ),
        [
            pltpu.VMEM((FULL, LANES), f32),
            pltpu.VMEM((FULL, LANES), f32),
            pltpu.VMEM((3, 8, LANES), f32),
            pltpu.VMEM((comps * nodes, 8, LANES), f32),
            pltpu.VMEM((nodes, 8, LANES), f32),
            pltpu.VMEM((32, LANES), f32),
            pltpu.VMEM((6, 24, LANES), f32),
        ],
    )(*rhs, phase, fixed, strip, near, far)
    energy = call(energy_kernel, jax.ShapeDtypeStruct((3,) + phase.shape, f32))(base, second, edges, phase)
    sums = total_over(total_over(sums, "gy", (1, 2, 3)), "gx", (1, 2, 3))
    displacement, sensitivity = call(
        combine_kernel,
        (jax.ShapeDtypeStruct(force.shape, f32), jax.ShapeDtypeStruct(phase.shape, f32)),
    )(base, second, energy, sums)
    return displacement, sensitivity.reshape(rows, layers, width).transpose(1, 0, 2)


def solution(mesh):
    return jax.shard_map(
        body,
        mesh=mesh,
        in_specs=(
            P(None, None, ("parts", "gx"), "gy"),
            P(None, ("parts", "gx"), "gy"),
            P(None, ("parts", "gx"), "gy"),
        ),
        out_specs=(P(None, None, ("parts", "gx"), "gy"), P(None, ("parts", "gx"), "gy")),
        check_vma=False,
    )
```

time: 29.1 us -> 28.2 us (0.969)
  waiting for transfers between devices: 10.2 us -> 9.31 us
    ppermute x6, waiting for transfers between devices: 4.01 us -> 3.25 us  [total_over(): lax.ppermute(x, axis, [(i, i ^ step * by) for i in range(count)])]
    pallas_call x3 -> x5, Pallas kernels: 2.57 us -> 2.55 us  [the longest x1 1.34 us: body(): call(functools.partial(operator_kernel, paired_x), (field, field, strips,...]
  transfers between devices with their start and end apart: 10 -> 10, of which waited for: 8 -> 8; matrix products, arithmetic and copies ran while one was open for 0% -> 0% of each run, Pallas kernels for 0% -> 3%
where the time goes in v4:
time: 28.2 us; the launch traced here: 28.1 us
  starting transfers between devices  13.7 us (49%)
  waiting for transfers between devices  9.31 us (33%)
  Pallas kernels  3.29 us (12%)
  other arithmetic  1.05 us (4%)
  between operations  0.71 us (3%)
    ppermute x6, starting transfers between devices, total_over(): lax.ppermute(x, axis, [(i, i ^ step * by) for i in range(count)])  6.32 us
    ppermute x2, waiting for transfers between devices, exchange(): lax.ppermute(two, axis, [(i, (i - 1) % count if i % 2 == 0 else (i + 1) %...  5.39 us
    ppermute x2, starting transfers between devices, exchange(): lax.ppermute(two, axis, [(i, (i - 1) % count if i % 2 == 0 else (i + 1) %...  5.09 us
    ppermute x6, waiting for transfers between devices, total_over(): lax.ppermute(x, axis, [(i, i ^ step * by) for i in range(count)])  3.25 us
    ppermute x2, starting transfers between devices, exchange(): near = lax.ppermute(one, axis, [(i, i ^ 1) for i in range(count)])  2.3 us
    pallas_call x1, Pallas kernels, body(): call(functools.partial(operator_kernel, paired_x), (field, field, strips,...  1.34 us
    mul x1, other arithmetic, body(): rhs = [(1 - fixed).astype(jnp.float32) * force[c] for c in range(comps)]  1.04 us
    pallas_call x1, Pallas kernels, body(): call(energy_kernel, jax.ShapeDtypeStruct((3,) + phase.shape, f32))  0.75 us
  transfers between devices with their start and end apart: 10, of which 8 were waited for; matrix products, arithmetic and copies ran while one was open for 0% of the time, Pallas kernels for 3%

profile of v4, /device:TPU:0, one launch (start us, length us, event | category | flops | bytes accessed | tf_op | source)
XLA Modules:
  0.0 28.1 jit_solution(2526132229805036946)
XLA Ops:
  0.6 0.0 copy-start
  0.6 0.0 copy-start.1
  0.6 1.0 %bitcast_multiply_fusion = (f32[17,6,128]{2,1,0:T(8,128)S(1)}, f32[17,6,128]{2,1,0:T(8,128)S(1)}, f32[17,6,128]{2,1,0:T(8,128)S(1)}) fusion(f32[3,17,6,128]{3,2,1,0:T(8,128)} %param.3, s32[17,6,128]{2,1,0:T(8,128)} %fixed.5), kind=kLoop, calls=%fused_computation | loop fusion | flops 65280 | bytes 365568 | tf_op jit(solution)/shard_map/mul | solution.py:528
  1.7 0.0 copy-done
  1.7 0.0 copy-done.1
  1.7 0.3 shard_map.50
  2.0 0.5 %collective-permute-start = (f32[2,8,128]{2,1,0:T(8,128)S(1)}, f32[2,8,128]{2,1,0:T(8,128)S(1)}, u32[]{:S(2)}, u32[]{:S(2)}) collective-permute-start(f32[2,8,128]{2,1,0:T(8,128)S(1)} %get-tuple-element.17), channel_id=1, source_target_pairs={{0,1},{1,0},{2,3},{3,2},{4,5},{5,4},{6,7},{7,6},{8,9},{9,8},{10,11... | collective-permute-start | bytes 24584 | tf_op jit(solution)/shard_map/ppermute | solution.py:502
  2.5 2.6 %collective-permute-start.1 = (f32[2,8,128]{2,1,0:T(8,128)S(1)}, f32[2,8,128]{2,1,0:T(8,128)S(1)}, u32[]{:S(2)}, u32[]{:S(2)}) collective-permute-start(f32[2,8,128]{2,1,0:T(8,128)S(1)} %get-tuple-element.18), channel_id=1, source_target_pairs={{0,3},{1,2},{2,1},{3,0},{4,7},{5,6},{6,5},{7,4},{8,11},{9,10},{10,... | collective-permute-start | bytes 24584 | tf_op jit(solution)/shard_map/ppermute | solution.py:501
  5.1 0.1 shard_map.51
  5.2 0.0 collective-permute-done.got1
  5.2 1.3 %collective-permute-done.1.got2 = f32[2,8,128]{2,1,0:T(8,128)S(1)} collective-permute-done((f32[2,8,128]{2,1,0:T(8,128)S(1)}, f32[2,8,128]{2,1,0:T(8,128)S(1)}, u32[]{:S(2)}, u32[]{:S(2)}) %collective-permute-start.1) | collective-permute-done | bytes 8224 | tf_op jit(solution)/shard_map/ppermute | solution.py:501
  6.4 0.1 shard_map.52
  6.5 1.8 %collective-permute-start.2 = (f32[168,128]{1,0:T(8,128)S(1)}, f32[168,128]{1,0:T(8,128)S(1)}, u32[]{:S(2)}, u32[]{:S(2)}) collective-permute-start(f32[168,128]{1,0:T(8,128)S(1)} %get-tuple-element.22), channel_id=1, source_target_pairs={{0,4},{4,0},{8,12},{12,8},{1,5},{5,1},{9,13},{13,9},{2,6},{6,2},{1... | collective-permute-start | bytes 258056 | tf_op jit(solution)/shard_map/ppermute | solution.py:502
  8.4 2.5 %collective-permute-start.3 = (f32[168,128]{1,0:T(8,128)S(1)}, f32[168,128]{1,0:T(8,128)S(1)}, u32[]{:S(2)}, u32[]{:S(2)}) collective-permute-start(f32[168,128]{1,0:T(8,128)S(1)} %get-tuple-element.23), channel_id=1, source_target_pairs={{0,12},{4,8},{8,4},{12,0},{1,13},{5,9},{9,5},{13,1},{2,14},{6,10},... | collective-permute-start | bytes 258056 | tf_op jit(solution)/shard_map/ppermute | solution.py:501
  10.8 0.7 %collective-permute-done.2.got1 = f32[168,128]{1,0:T(8,128)S(1)} collective-permute-done((f32[168,128]{1,0:T(8,128)S(1)}, f32[168,128]{1,0:T(8,128)S(1)}, u32[]{:S(2)}, u32[]{:S(2)}) %collective-permute-start.2) | collective-permute-done | bytes 86048 | tf_op jit(solution)/shard_map/ppermute | solution.py:502
  11.5 4.1 %collective-permute-done.3.got2 = f32[168,128]{1,0:T(8,128)S(1)} collective-permute-done((f32[168,128]{1,0:T(8,128)S(1)}, f32[168,128]{1,0:T(8,128)S(1)}, u32[]{:S(2)}, u32[]{:S(2)}) %collective-permute-start.3) | collective-permute-done | bytes 86048 | tf_op jit(solution)/shard_map/ppermute | solution.py:501
  15.6 1.3 %shard_map.53 = (f32[51,8,128]{2,1,0:T(8,128)S(1)}, f32[51,8,128]{2,1,0:T(8,128)S(1)}, f32[6,8,128]{2,1,0:T(8,128)S(1)}, f32[8,128]{1,0:T(8,128)S(1)}) custom-call(f32[17,6,128]{2,1,0:T(8,128)S(1)} %get-tuple-element.31.rhs_0, f32[17,6,128]{2,1,0:T(8,128)S(1)} %get-tuple-element.32.rhs_1, f32[17,6,128]{2,1,0:T(8,128)S(1)} %get-tuple-element.30.rhs_2, ...), custom_call_target="tpu_custom_call" | custom-call | tf_op jit(solution)/shard_map/pallas_call | solution.py:557
  17.0 0.7 %collective-permute-start.6 = (f32[8,128]{1,0:T(8,128)S(1)}, f32[8,128]{1,0:T(8,128)S(1)}, u32[]{:S(2)}, u32[]{:S(2)}) collective-permute-start(f32[8,128]{1,0:T(8,128)S(1)} %get-tuple-element.27), channel_id=1, source_target_pairs={{0,3},{1,2},{2,1},{3,0},{4,7},{5,6},{6,5},{7,4},{8,11},{9,10},{10,... | collective-permute-start | bytes 12296 | tf_op jit(solution)/shard_map/ppermute | solution.py:517
  17.6 0.9 %collective-permute-start.5 = (f32[8,128]{1,0:T(8,128)S(1)}, f32[8,128]{1,0:T(8,128)S(1)}, u32[]{:S(2)}, u32[]{:S(2)}) collective-permute-start(f32[8,128]{1,0:T(8,128)S(1)} %get-tuple-element.27), channel_id=1, source_target_pairs={{0,2},{1,3},{2,0},{3,1},{4,6},{5,7},{6,4},{7,5},{8,10},{9,11},{10,... | collective-permute-start | bytes 12296 | tf_op jit(solution)/shard_map/ppermute | solution.py:517
  18.5 0.3 %collective-permute-start.4 = (f32[8,128]{1,0:T(8,128)S(1)}, f32[8,128]{1,0:T(8,128)S(1)}, u32[]{:S(2)}, u32[]{:S(2)}) collective-permute-start(f32[8,128]{1,0:T(8,128)S(1)} %get-tuple-element.27), channel_id=1, source_target_pairs={{0,1},{1,0},{2,3},{3,2},{4,5},{5,4},{6,7},{7,6},{8,9},{9,8},{10,11... | collective-permute-start | bytes 12296 | tf_op jit(solution)/shard_map/ppermute | solution.py:517
  18.8 1.2 %collective-permute-done.6 = f32[8,128]{1,0:T(8,128)S(1)} collective-permute-done((f32[8,128]{1,0:T(8,128)S(1)}, f32[8,128]{1,0:T(8,128)S(1)}, u32[]{:S(2)}, u32[]{:S(2)}) %collective-permute-start.6) | collective-permute-done | bytes 4128 | tf_op jit(solution)/shard_map/ppermute | solution.py:517
  20.0 1.3 %collective-permute-done.5 = f32[8,128]{1,0:T(8,128)S(1)} collective-permute-done((f32[8,128]{1,0:T(8,128)S(1)}, f32[8,128]{1,0:T(8,128)S(1)}, u32[]{:S(2)}, u32[]{:S(2)}) %collective-permute-start.5) | collective-permute-done | bytes 4128 | tf_op jit(solution)/shard_map/ppermute | solution.py:517
  21.3 0.0 collective-permute-done.4
  21.3 1.5 %collective-permute-start.9 = (f32[8,128]{1,0:T(8,128)S(1)}, f32[8,128]{1,0:T(8,128)S(1)}, u32[]{:S(2)}, u32[]{:S(2)}) collective-permute-start(f32[8,128]{1,0:T(8,128)S(1)} %add_add_fusion.1), channel_id=1, source_target_pairs={{0,12},{4,8},{8,4},{12,0},{1,13},{5,9},{9,5},{13,1},{2,14},{6,10},... | collective-permute-start | bytes 12296 | tf_op jit(solution)/shard_map/ppermute | solution.py:517
  22.7 0.2 collective-permute-start.8
  22.9 2.8 %collective-permute-start.7 = (f32[8,128]{1,0:T(8,128)S(1)}, f32[8,128]{1,0:T(8,128)S(1)}, u32[]{:S(2)}, u32[]{:S(2)}) collective-permute-start(f32[8,128]{1,0:T(8,128)S(1)} %add_add_fusion.1), channel_id=1, source_target_pairs={{0,4},{4,0},{8,12},{12,8},{1,5},{5,1},{9,13},{13,9},{2,6},{6,2},{1... | collective-permute-start | bytes 12296 | tf_op jit(solution)/shard_map/ppermute | solution.py:517
  25.7 0.8 %shard_map.54.energy = f32[3,96,128]{2,1,0:T(8,128)S(1)} custom-call(f32[51,8,128]{2,1,0:T(8,128)S(1)} %get-tuple-element.24.base, f32[51,8,128]{2,1,0:T(8,128)S(1)} %get-tuple-element.25.second, f32[6,8,128]{2,1,0:T(8,128)S(1)} %get-tuple-element.26.edges, s32[96,128]{1,0:T(8,128)S(1)} %bitcast.15), custom_call_target="tpu_custom_call" | custom-call | tf_op jit(solution)/shard_map/pallas_call | solution.py:575
  26.5 0.3 collective-permute-done.9
  26.7 0.5 %collective-permute-done.8 = f32[8,128]{1,0:T(8,128)S(1)} collective-permute-done((f32[8,128]{1,0:T(8,128)S(1)}, f32[8,128]{1,0:T(8,128)S(1)}, u32[]{:S(2)}, u32[]{:S(2)}) %collective-permute-start.8) | collective-permute-done | bytes 4128 | tf_op jit(solution)/shard_map/ppermute | solution.py:517
  27.2 0.1 collective-permute-done.7
  27.3 0.7 %shard_map.55 = (f32[3,17,6,128]{3,2,1,0:T(8,128)}, f32[96,128]{1,0:T(8,128)}) custom-call(f32[51,8,128]{2,1,0:T(8,128)S(1)} %get-tuple-element.24.base, f32[51,8,128]{2,1,0:T(8,128)S(1)} %get-tuple-element.25.second, f32[3,96,128]{2,1,0:T(8,128)S(1)} %shard_map.54.energy, f32[8,128]{1,0:T(8,128)S(1)} %add_add_fusion.sums), custom_call_target="tpu_custom_call" | custom-call | tf_op jit(solution)/shard_map/pallas_call | solution.py:577
  (2 shorter events, 0.0 us)
Async XLA Ops:
  0.6 1.1 %copy-start = (s32[17,6,128]{2,1,0:T(8,128)S(1)}, s32[17,6,128]{2,1,0:T(8,128)}, u32[]{:S(2)}) copy-start(s32[17,6,128]{2,1,0:T(8,128)} %fixed.5) | copy-start | bytes 156676
  0.6 1.1 %copy-start.1 = (s32[16,6,128]{2,0,1:T(8,128)S(1)}, s32[16,6,128]{2,0,1:T(8,128)}, u32[]{:S(2)}) copy-start(s32[16,6,128]{2,0,1:T(8,128)} %param.4) | copy-start | bytes 147460
  2.0 3.2 %collective-permute-start = (f32[2,8,128]{2,1,0:T(8,128)S(1)}, f32[2,8,128]{2,1,0:T(8,128)S(1)}, u32[]{:S(2)}, u32[]{:S(2)}) collective-permute-start(f32[2,8,128]{2,1,0:T(8,128)S(1)} %get-tuple-element.17), channel_id=1, source_target_pairs={{0,1},{1,0},{2,3},{3,2},{4,5},{5,4},{6,7},{7,6},{8,9},{9,8},{10,11... | collective-permute-start | bytes 24584 | tf_op jit(solution)/shard_map/ppermute | solution.py:502
  2.5 4.0 %collective-permute-start.1 = (f32[2,8,128]{2,1,0:T(8,128)S(1)}, f32[2,8,128]{2,1,0:T(8,128)S(1)}, u32[]{:S(2)}, u32[]{:S(2)}) collective-permute-start(f32[2,8,128]{2,1,0:T(8,128)S(1)} %get-tuple-element.18), channel_id=1, source_target_pairs={{0,3},{1,2},{2,1},{3,0},{4,7},{5,6},{6,5},{7,4},{8,11},{9,10},{10,... | collective-permute-start | bytes 24584 | tf_op jit(solution)/shard_map/ppermute | solution.py:501
  6.5 5.0 %collective-permute-start.2 = (f32[168,128]{1,0:T(8,128)S(1)}, f32[168,128]{1,0:T(8,128)S(1)}, u32[]{:S(2)}, u32[]{:S(2)}) collective-permute-start(f32[168,128]{1,0:T(8,128)S(1)} %get-tuple-element.22), channel_id=1, source_target_pairs={{0,4},{4,0},{8,12},{12,8},{1,5},{5,1},{9,13},{13,9},{2,6},{6,2},{1... | collective-permute-start | bytes 258056 | tf_op jit(solution)/shard_map/ppermute | solution.py:502
  8.4 7.3 %collective-permute-start.3 = (f32[168,128]{1,0:T(8,128)S(1)}, f32[168,128]{1,0:T(8,128)S(1)}, u32[]{:S(2)}, u32[]{:S(2)}) collective-permute-start(f32[168,128]{1,0:T(8,128)S(1)} %get-tuple-element.23), channel_id=1, source_target_pairs={{0,12},{4,8},{8,4},{12,0},{1,13},{5,9},{9,5},{13,1},{2,14},{6,10},... | collective-permute-start | bytes 258056 | tf_op jit(solution)/shard_map/ppermute | solution.py:501
  17.0 3.0 %collective-permute-start.6 = (f32[8,128]{1,0:T(8,128)S(1)}, f32[8,128]{1,0:T(8,128)S(1)}, u32[]{:S(2)}, u32[]{:S(2)}) collective-permute-start(f32[8,128]{1,0:T(8,128)S(1)} %get-tuple-element.27), channel_id=1, source_target_pairs={{0,3},{1,2},{2,1},{3,0},{4,7},{5,6},{6,5},{7,4},{8,11},{9,10},{10,... | collective-permute-start | bytes 12296 | tf_op jit(solution)/shard_map/ppermute | solution.py:517
  17.6 3.6 %collective-permute-start.5 = (f32[8,128]{1,0:T(8,128)S(1)}, f32[8,128]{1,0:T(8,128)S(1)}, u32[]{:S(2)}, u32[]{:S(2)}) collective-permute-start(f32[8,128]{1,0:T(8,128)S(1)} %get-tuple-element.27), channel_id=1, source_target_pairs={{0,2},{1,3},{2,0},{3,1},{4,6},{5,7},{6,4},{7,5},{8,10},{9,11},{10,... | collective-permute-start | bytes 12296 | tf_op jit(solution)/shard_map/ppermute | solution.py:517
  18.5 2.7 %collective-permute-start.4 = (f32[8,128]{1,0:T(8,128)S(1)}, f32[8,128]{1,0:T(8,128)S(1)}, u32[]{:S(2)}, u32[]{:S(2)}) collective-permute-start(f32[8,128]{1,0:T(8,128)S(1)} %get-tuple-element.27), channel_id=1, source_target_pairs={{0,1},{1,0},{2,3},{3,2},{4,5},{5,4},{6,7},{7,6},{8,9},{9,8},{10,11... | collective-permute-start | bytes 12296 | tf_op jit(solution)/shard_map/ppermute | solution.py:517
  21.3 5.5 %collective-permute-start.9 = (f32[8,128]{1,0:T(8,128)S(1)}, f32[8,128]{1,0:T(8,128)S(1)}, u32[]{:S(2)}, u32[]{:S(2)}) collective-permute-start(f32[8,128]{1,0:T(8,128)S(1)} %add_add_fusion.1), channel_id=1, source_target_pairs={{0,12},{4,8},{8,4},{12,0},{1,13},{5,9},{9,5},{13,1},{2,14},{6,10},... | collective-permute-start | bytes 12296 | tf_op jit(solution)/shard_map/ppermute | solution.py:517
  22.7 4.5 %collective-permute-start.8 = (f32[8,128]{1,0:T(8,128)S(1)}, f32[8,128]{1,0:T(8,128)S(1)}, u32[]{:S(2)}, u32[]{:S(2)}) collective-permute-start(f32[8,128]{1,0:T(8,128)S(1)} %add_add_fusion.1), channel_id=1, source_target_pairs={{0,8},{4,12},{8,0},{12,4},{1,9},{5,13},{9,1},{13,5},{2,10},{6,14},... | collective-permute-start | bytes 12296 | tf_op jit(solution)/shard_map/ppermute | solution.py:517
  22.9 4.4 %collective-permute-start.7 = (f32[8,128]{1,0:T(8,128)S(1)}, f32[8,128]{1,0:T(8,128)S(1)}, u32[]{:S(2)}, u32[]{:S(2)}) collective-permute-start(f32[8,128]{1,0:T(8,128)S(1)} %add_add_fusion.1), channel_id=1, source_target_pairs={{0,4},{4,0},{8,12},{12,8},{1,5},{5,1},{9,13},{13,9},{2,6},{6,2},{1... | collective-permute-start | bytes 12296 | tf_op jit(solution)/shard_map/ppermute | solution.py:517

commit v5 on v4

--- a/solution.py
+++ b/solution.py
@@ -17,8 +17,8 @@
 
 SLOTS = 7
 LANES = 128
-FULL = 168
-CORNERS = 152
+DOWN, DOWN_CORNERS = 168, 152
+UP, UP_CORNERS = 168, 83
 
 VMEM = pl.BlockSpec(memory_space=pltpu.VMEM)
 PARAMS = pltpu.CompilerParams(vmem_limit_bytes=32 * 1024 * 1024)
@@ -99,45 +99,30 @@
             col2[p] = high[p]
 
 
-def row_kernel(paired, rhs_0, rhs_1, rhs_2, phase, fixed, row1, row2):
+def row_kernel(rhs_0, rhs_1, rhs_2, phase, fixed, down, up):
     rhs = (rhs_0, rhs_1, rhs_2)
     nodes, rows, width = rhs_0.shape
     layers, cn = nodes - 1, 3 * nodes
-    even = is_even("gx") if paired else True
-    nothing = jnp.zeros((1, LANES), jnp.float32)
-
-    def put(at, low, high):
-        if paired:
-            row1[at : at + 1, :] = jnp.where(even, high, low)
-            row2[at : at + 1, :] = jnp.where(even, low, high)
-        else:
-            row1[at : at + 1, :] = low
-            row2[at : at + 1, :] = high
-
     for k in range(nodes):
         for c in range(3):
             q = c * nodes + k
-            put(q, rhs[c][k, 0:1], rhs[c][k, rows - 1 : rows])
-            put(cn + 2 * layers + q, rhs[c][k, 1:2], nothing)
-        put(2 * cn + 2 * layers + k, (1 - fixed[k, 0:1]).astype(jnp.float32), nothing)
-    scale = [table(phase[i * layers : (i + 1) * layers], PHASE_STIFFNESS) for i in (0, 1, rows - 2, rows - 1)]
+            down[q : q + 1, :] = rhs[c][k, 0:1]
+            down[cn + 2 * layers + q : cn + 2 * layers + q + 1, :] = rhs[c][k, 1:2]
+            up[q : q + 1, :] = rhs[c][k, rows - 1 : rows]
+        at = 2 * cn + 2 * layers + k
+        down[at : at + 1, :] = (1 - fixed[k, 0:1]).astype(jnp.float32)
     for i in range(2):
         at = cn + i * layers
-        if paired:
-            row1[at : at + layers, :] = jnp.where(even, scale[2 + i], scale[i])
-            row2[at : at + layers, :] = jnp.where(even, scale[i], scale[2 + i])
-        else:
-            row1[at : at + layers, :] = scale[i]
-            row2[at : at + layers, :] = scale[2 + i]
-    used = 2 * cn + 2 * layers + nodes
-    row1[used:, :] = jnp.zeros((FULL - used, LANES), jnp.float32)
-    row2[used:, :] = jnp.zeros((FULL - used, LANES), jnp.float32)
-
-
-def strip_kernel(nodes, paired_x, paired_y, own, got1, got2, row1, row2, strip, out1, out2):
-    even_x = is_even("gx") if paired_x else True
-    even_y = is_even("gy") if paired_y else True
-    if paired_y:
+        down[at : at + layers, :] = table(phase[i * layers : (i + 1) * layers], PHASE_STIFFNESS)
+        first = (rows - 2 + i) * layers
+        up[at : at + layers, :] = table(phase[first : first + layers], PHASE_STIFFNESS)
+    down[2 * cn + 2 * layers + nodes :, :] = jnp.zeros((DOWN - 2 * cn - 2 * layers - nodes, LANES), jnp.float32)
+    up[cn + 2 * layers :, :] = jnp.zeros((UP - cn - 2 * layers, LANES), jnp.float32)
+
+
+def strip_kernel(nodes, paired, own, got2, got1, down, up, strip, down_out, up_out):
+    even_y = is_even("gy") if paired else True
+    if paired:
         from_low = jnp.where(even_y, got2[0], got1[0])
         from_high = [jnp.where(even_y, got1[p], got2[p]) for p in range(2)]
     else:
@@ -151,20 +136,12 @@
     planes.append(gather(nodes, (from_low, -4, 0, 1), (scale, -2, 1, 2), (scale, 2, 3, 2), (from_high[1], 2, 5, 2)))
     planes.append(gather(nodes, (own[4], -2, 1, 1), (own[4], 2, 4, 1), (from_high[0], -1, 5, 1)))
     rows = 6
-    out1[...] = row1[...]
-    out2[...] = row2[...]
+    down_out[...] = down[...]
+    up_out[...] = up[...]
     for p, plane in enumerate(planes):
         strip[p] = plane
-        for which in range(2):
-            at = CORNERS + 2 * p + which
-            low_row = plane[which : which + 1]
-            high_row = plane[rows - 2 + which : rows - 1 + which]
-            if paired_x:
-                out1[at : at + 1, :] = jnp.where(even_x, high_row, low_row)
-                out2[at : at + 1, :] = jnp.where(even_x, low_row, high_row)
-            else:
-                out1[at : at + 1, :] = low_row
-                out2[at : at + 1, :] = high_row
+        down_out[DOWN_CORNERS + 2 * p : DOWN_CORNERS + 2 * p + 2, :] = plane[0:2]
+        up_out[UP_CORNERS + 2 * p : UP_CORNERS + 2 * p + 2, :] = plane[rows - 2 : rows]
 
 
 PLANE = ("", "1", "2", "12")
@@ -234,9 +211,9 @@
 
 
 def operator_kernel(
-    paired_x, rhs_0, rhs_1, rhs_2, phase, fixed, strip, got1, got2,
+    rhs_0, rhs_1, rhs_2, phase, fixed, strip, lo, hi,
     base, second, edges, sums,
-    lo, hi, held, residual, inverse, dense, far_base,
+    held, residual, inverse, dense, far_base,
 ):
     rhs, comps = (rhs_0, rhs_1, rhs_2), 3
     nodes, rows, width = rhs_0.shape
@@ -244,14 +221,6 @@
     lane, row = lanes(), sublanes()
     last_row, below = row == 6, row == 7
     cn = comps * nodes
-    if paired_x:
-        even_x = is_even("gx")
-        lo[...] = jnp.where(even_x, got2[...], got1[...])
-        hi[...] = jnp.where(even_x, got1[...], got2[...])
-    else:
-        lo[...] = got2[...]
-        hi[...] = got1[...]
-
     def spread(ref, at):
         return jnp.broadcast_to(ref[pl.ds(at, 1), :], (8, LANES))
 
@@ -283,7 +252,7 @@
         return tuple(t + x for t, x in zip(totals, (d0 * image, image * z, s * v, v * image)))
 
     def corner(ref, p, which):
-        return spread(ref, CORNERS + 2 * p + which)
+        return spread(ref, (UP_CORNERS if ref is lo else DOWN_CORNERS) + 2 * p + which)
 
     tiles = [
         jnp.where(row < 6, strip[p], jnp.where(last_row, corner(hi, p, 0), corner(lo, p, 1))) for p in range(6)
@@ -495,28 +464,32 @@
     sensitivity[...] = (first * first) * energy[0] + (2.0 * first * other) * energy[1] + (other * other) * energy[2]
 
 
-def exchange(one, two, axis):
+def exchange_pairs(one, two, axis):
     count = lax.axis_size(axis)
-    if count % 2 == 0:
-        far = lax.ppermute(two, axis, [(i, (i - 1) % count if i % 2 == 0 else (i + 1) % count) for i in range(count)])
-        near = lax.ppermute(one, axis, [(i, i ^ 1) for i in range(count)])
-        return near, far
-    high = lax.ppermute(one, axis, [((i + 1) % count, i) for i in range(count)])
-    low = lax.ppermute(two, axis, [(i, (i + 1) % count) for i in range(count)])
+    far = lax.ppermute(two, axis, [(i, (i - 1) % count if i % 2 == 0 else (i + 1) % count) for i in range(count)])
+    near = lax.ppermute(one, axis, [(i, i ^ 1) for i in range(count)])
+    return near, far
+
+
+def exchange(down, up, axis):
+    count = lax.axis_size(axis)
+    low = lax.ppermute(up, axis, [(i, (i + 1) % count) for i in range(count)])
+    high = lax.ppermute(down, axis, [((i + 1) % count, i) for i in range(count)])
     return high, low
 
 
-def total_over(x, axis, order):
+def total_over(x, axis):
     count = lax.axis_size(axis)
     if count & (count - 1):
         return lax.psum(x, axis)
     step = 1
     while step < count:
         width = 4 if count // step >= 4 else 2
-        group = [
-            lax.ppermute(x, axis, [(i, i ^ (step * by)) for i in range(count)]) for by in order if by < width
-        ]
-        x = functools.reduce(jnp.add, group, x)
+        if axis == "gx" and count == 4:
+            to = [[(i, (i + by) % 4) for i in range(4)] for by in (3, 2, 1)]
+        else:
+            to = [[(i, i ^ (step * by)) for i in range(count)] for by in range(1, width)]
+        x = functools.reduce(jnp.add, [lax.ppermute(x, axis, pairs) for pairs in to], x)
         step *= width
     return x
 
@@ -527,35 +500,29 @@
     phase = phase.transpose(1, 0, 2).reshape(rows * layers, width)
     rhs = [(1 - fixed).astype(jnp.float32) * force[c] for c in range(comps)]
     f32 = jnp.float32
-    paired_x = lax.axis_size("gx") % 2 == 0
-    paired_y = lax.axis_size("gy") % 2 == 0
+    paired = lax.axis_size("gy") % 2 == 0
     column = jax.ShapeDtypeStruct((2, 8, LANES), f32)
-    message = jax.ShapeDtypeStruct((FULL, LANES), f32)
+    messages = (jax.ShapeDtypeStruct((DOWN, LANES), f32), jax.ShapeDtypeStruct((UP, LANES), f32))
+    strips = jax.ShapeDtypeStruct((6, 8, LANES), f32)
 
     def call(kernel, out_shape, scratch=()):
-        return pl.pallas_call(
-            kernel,
-            out_shape=out_shape,
-            scratch_shapes=scratch,
-            compiler_params=PARAMS,
-        )
-
-    strips = jax.ShapeDtypeStruct((6, 8, LANES), f32)
+        return pl.pallas_call(kernel, out_shape=out_shape, scratch_shapes=scratch, compiler_params=PARAMS)
+
     own, col1, col2 = call(
-        functools.partial(column_kernel, paired_y),
+        functools.partial(column_kernel, paired),
         (jax.ShapeDtypeStruct((5, 8, LANES), f32), column, column),
         [pltpu.VMEM((5 * nodes, 8, LANES), f32)],
     )(*rhs, phase, fixed)
-    row1, row2 = call(functools.partial(row_kernel, paired_x), (message, message))(*rhs, phase, fixed)
-    near, far = exchange(col1, col2, "gy")
-    strip, row1, row2 = call(
-        functools.partial(strip_kernel, nodes, paired_x, paired_y),
-        (strips, message, message),
-    )(own, near, far, row1, row2)
-    near, far = exchange(row1, row2, "gx")
+    down, up = call(row_kernel, messages)(*rhs, phase, fixed)
+    near, far = (exchange_pairs if paired else exchange)(col1, col2, "gy")
+    strip, down, up = call(
+        functools.partial(strip_kernel, nodes, paired),
+        (strips,) + messages,
+    )(own, far, near, down, up)
+    high, low = exchange(down, up, "gx")
     field = jax.ShapeDtypeStruct((comps * nodes, 8, LANES), f32)
     base, second, edges, sums = call(
-        functools.partial(operator_kernel, paired_x),
+        operator_kernel,
         (
             field,
             field,
@@ -563,17 +530,15 @@
             jax.ShapeDtypeStruct((8, LANES), f32),
         ),
         [
-            pltpu.VMEM((FULL, LANES), f32),
-            pltpu.VMEM((FULL, LANES), f32),
             pltpu.VMEM((3, 8, LANES), f32),
             pltpu.VMEM((comps * nodes, 8, LANES), f32),
             pltpu.VMEM((nodes, 8, LANES), f32),
             pltpu.VMEM((32, LANES), f32),
             pltpu.VMEM((6, 24, LANES), f32),
         ],
-    )(*rhs, phase, fixed, strip, near, far)
+    )(*rhs, phase, fixed, strip, low, high)
     energy = call(energy_kernel, jax.ShapeDtypeStruct((3,) + phase.shape, f32))(base, second, edges, phase)
-    sums = total_over(total_over(sums, "gy", (1, 2, 3)), "gx", (1, 2, 3))
+    sums = total_over(total_over(sums, "gx"), "gy")
     displacement, sensitivity = call(
         combine_kernel,
         (jax.ShapeDtypeStruct(force.shape, f32), jax.ShapeDtypeStruct(phase.shape, f32)),

time: 28.2 us -> 27 us (0.957)
  waiting for transfers between devices: 9.31 us -> 8.27 us
  starting transfers between devices: 13.7 us -> 13.4 us
    ppermute x10, waiting for transfers between devices: 9.31 us -> 8.27 us  [the longest x6 3.5 us: total_over(): lax.ppermute(x, axis, pairs)]
    ppermute x10, starting transfers between devices: 13.7 us -> 13.4 us  [the longest x6 5.92 us: total_over(): lax.ppermute(x, axis, pairs)]
  transfers between devices with their start and end apart: 10 -> 10, of which waited for: 8 -> 9; matrix products, arithmetic and copies ran while one was open for 0% -> 0% of each run, Pallas kernels for 3% -> 3%
where the time goes in v5:
time: 27 us; the launch traced here: 26.7 us
  starting transfers between devices  13.4 us (50%)
  waiting for transfers between devices  8.27 us (31%)
  Pallas kernels  3.29 us (12%)
  other arithmetic  1.05 us (4%)
  between operations  0.7 us (3%)
    ppermute x6, starting transfers between devices, total_over(): lax.ppermute(x, axis, pairs)  5.92 us
    ppermute x6, waiting for transfers between devices, total_over(): lax.ppermute(x, axis, pairs)  3.5 us
    ppermute x1, waiting for transfers between devices, exchange(): low = lax.ppermute(up, axis, [(i, (i + 1) % count) for i in range(count)])  3.14 us
    ppermute x1, starting transfers between devices, exchange_pairs(): lax.ppermute(two, axis, [(i, (i - 1) % count if i % 2 == 0 else (i + 1) %...  2.41 us
    ppermute x1, starting transfers between devices, exchange(): low = lax.ppermute(up, axis, [(i, (i + 1) % count) for i in range(count)])  2.31 us
    ppermute x1, starting transfers between devices, exchange(): lax.ppermute(down, axis, [((i + 1) % count, i) for i in range(count)])  2.09 us
    pallas_call x1, Pallas kernels, body(): call(operator_kernel, (field, field, strips, jax.ShapeDtypeStruct((8, LAN...  1.37 us
    mul x1, other arithmetic, body(): rhs = [(1 - fixed).astype(jnp.float32) * force[c] for c in range(comps)]  1.04 us
  transfers between devices with their start and end apart: 10, of which 9 were waited for; matrix products, arithmetic and copies ran while one was open for 0% of the time, Pallas kernels for 3%

profile of v5, /device:TPU:0, one launch (start us, length us, event | category | flops | bytes accessed | tf_op | source)
XLA Modules:
  0.0 26.7 jit_solution(8056730104842217595)
XLA Ops:
  0.6 0.0 copy-start
  0.6 0.0 copy-start.1
  0.6 1.0 %bitcast_multiply_fusion = (f32[17,6,128]{2,1,0:T(8,128)S(1)}, f32[17,6,128]{2,1,0:T(8,128)S(1)}, f32[17,6,128]{2,1,0:T(8,128)S(1)}) fusion(f32[3,17,6,128]{3,2,1,0:T(8,128)} %param.3, s32[17,6,128]{2,1,0:T(8,128)} %fixed.5), kind=kLoop, calls=%fused_computation | loop fusion | flops 65280 | bytes 365568 | tf_op jit(solution)/shard_map/mul | solution.py:501
  1.7 0.0 copy-done
  1.7 0.0 copy-done.1
  1.7 0.3 shard_map.50
  2.0 2.4 %collective-permute-start = (f32[2,8,128]{2,1,0:T(8,128)S(1)}, f32[2,8,128]{2,1,0:T(8,128)S(1)}, u32[]{:S(2)}, u32[]{:S(2)}) collective-permute-start(f32[2,8,128]{2,1,0:T(8,128)S(1)} %get-tuple-element.17), channel_id=1, source_target_pairs={{0,3},{1,2},{2,1},{3,0},{4,7},{5,6},{6,5},{7,4},{8,11},{9,10},{10,... | collective-permute-start | bytes 24584 | tf_op jit(solution)/shard_map/ppermute | solution.py:469
  4.4 0.7 %collective-permute-start.1 = (f32[2,8,128]{2,1,0:T(8,128)S(1)}, f32[2,8,128]{2,1,0:T(8,128)S(1)}, u32[]{:S(2)}, u32[]{:S(2)}) collective-permute-start(f32[2,8,128]{2,1,0:T(8,128)S(1)} %get-tuple-element.18), channel_id=1, source_target_pairs={{0,1},{1,0},{2,3},{3,2},{4,5},{5,4},{6,7},{7,6},{8,9},{9,8},{10,11... | collective-permute-start | bytes 24584 | tf_op jit(solution)/shard_map/ppermute | solution.py:470
  5.1 0.1 shard_map.51
  5.1 0.6 %collective-permute-done.got2 = f32[2,8,128]{2,1,0:T(8,128)S(1)} collective-permute-done((f32[2,8,128]{2,1,0:T(8,128)S(1)}, f32[2,8,128]{2,1,0:T(8,128)S(1)}, u32[]{:S(2)}, u32[]{:S(2)}) %collective-permute-start) | collective-permute-done | bytes 8224 | tf_op jit(solution)/shard_map/ppermute | solution.py:469
  5.8 0.1 collective-permute-done.1.got1
  5.9 0.1 shard_map.52
  6.0 2.3 %collective-permute-start.2 = (f32[168,128]{1,0:T(8,128)S(1)}, f32[168,128]{1,0:T(8,128)S(1)}, u32[]{:S(2)}, u32[]{:S(2)}) collective-permute-start(f32[168,128]{1,0:T(8,128)S(1)} %get-tuple-element.22), channel_id=1, source_target_pairs={{0,4},{4,8},{8,12},{12,0},{1,5},{5,9},{9,13},{13,1},{2,6},{6,10},{... | collective-permute-start | bytes 258056 | tf_op jit(solution)/shard_map/ppermute | solution.py:476
  8.3 2.1 %collective-permute-start.3 = (f32[168,128]{1,0:T(8,128)S(1)}, f32[168,128]{1,0:T(8,128)S(1)}, u32[]{:S(2)}, u32[]{:S(2)}) collective-permute-start(f32[168,128]{1,0:T(8,128)S(1)} %get-tuple-element.23), channel_id=1, source_target_pairs={{4,0},{8,4},{12,8},{0,12},{5,1},{9,5},{13,9},{1,13},{6,2},{10,6},{... | collective-permute-start | bytes 258056 | tf_op jit(solution)/shard_map/ppermute | solution.py:477
  10.4 3.1 %collective-permute-done.2.lo = f32[168,128]{1,0:T(8,128)S(1)} collective-permute-done((f32[168,128]{1,0:T(8,128)S(1)}, f32[168,128]{1,0:T(8,128)S(1)}, u32[]{:S(2)}, u32[]{:S(2)}) %collective-permute-start.2) | collective-permute-done | bytes 86048 | tf_op jit(solution)/shard_map/ppermute | solution.py:476
  13.5 0.9 %collective-permute-done.3.hi = f32[168,128]{1,0:T(8,128)S(1)} collective-permute-done((f32[168,128]{1,0:T(8,128)S(1)}, f32[168,128]{1,0:T(8,128)S(1)}, u32[]{:S(2)}, u32[]{:S(2)}) %collective-permute-start.3) | collective-permute-done | bytes 86048 | tf_op jit(solution)/shard_map/ppermute | solution.py:477
  14.4 1.4 %shard_map.53 = (f32[51,8,128]{2,1,0:T(8,128)S(1)}, f32[51,8,128]{2,1,0:T(8,128)S(1)}, f32[6,8,128]{2,1,0:T(8,128)S(1)}, f32[8,128]{1,0:T(8,128)S(1)}) custom-call(f32[17,6,128]{2,1,0:T(8,128)S(1)} %get-tuple-element.31.rhs_0, f32[17,6,128]{2,1,0:T(8,128)S(1)} %get-tuple-element.32.rhs_1, f32[17,6,128]{2,1,0:T(8,128)S(1)} %get-tuple-element.30.rhs_2, ...), custom_call_target="tpu_custom_call" | custom-call | tf_op jit(solution)/shard_map/pallas_call | solution.py:524
  15.8 1.1 %collective-permute-start.6 = (f32[8,128]{1,0:T(8,128)S(1)}, f32[8,128]{1,0:T(8,128)S(1)}, u32[]{:S(2)}, u32[]{:S(2)}) collective-permute-start(f32[8,128]{1,0:T(8,128)S(1)} %get-tuple-element.27), channel_id=1, source_target_pairs={{0,4},{4,8},{8,12},{12,0},{1,5},{5,9},{9,13},{13,1},{2,6},{6,10},{... | collective-permute-start | bytes 12296 | tf_op jit(solution)/shard_map/ppermute | solution.py:492
  16.9 1.8 %collective-permute-start.5 = (f32[8,128]{1,0:T(8,128)S(1)}, f32[8,128]{1,0:T(8,128)S(1)}, u32[]{:S(2)}, u32[]{:S(2)}) collective-permute-start(f32[8,128]{1,0:T(8,128)S(1)} %get-tuple-element.27), channel_id=1, source_target_pairs={{0,8},{4,12},{8,0},{12,4},{1,9},{5,13},{9,1},{13,5},{2,10},{6,14},... | collective-permute-start | bytes 12296 | tf_op jit(solution)/shard_map/ppermute | solution.py:492
  18.7 1.2 %collective-permute-start.4 = (f32[8,128]{1,0:T(8,128)S(1)}, f32[8,128]{1,0:T(8,128)S(1)}, u32[]{:S(2)}, u32[]{:S(2)}) collective-permute-start(f32[8,128]{1,0:T(8,128)S(1)} %get-tuple-element.27), channel_id=1, source_target_pairs={{0,12},{4,0},{8,4},{12,8},{1,13},{5,1},{9,5},{13,9},{2,14},{6,2},{... | collective-permute-start | bytes 12296 | tf_op jit(solution)/shard_map/ppermute | solution.py:492
  19.9 1.4 %collective-permute-done.6 = f32[8,128]{1,0:T(8,128)S(1)} collective-permute-done((f32[8,128]{1,0:T(8,128)S(1)}, f32[8,128]{1,0:T(8,128)S(1)}, u32[]{:S(2)}, u32[]{:S(2)}) %collective-permute-start.6) | collective-permute-done | bytes 4128 | tf_op jit(solution)/shard_map/ppermute | solution.py:492
  21.2 0.3 %collective-permute-done.5 = f32[8,128]{1,0:T(8,128)S(1)} collective-permute-done((f32[8,128]{1,0:T(8,128)S(1)}, f32[8,128]{1,0:T(8,128)S(1)}, u32[]{:S(2)}, u32[]{:S(2)}) %collective-permute-start.5) | collective-permute-done | bytes 4128 | tf_op jit(solution)/shard_map/ppermute | solution.py:492
  21.5 0.8 %collective-permute-done.4 = f32[8,128]{1,0:T(8,128)S(1)} collective-permute-done((f32[8,128]{1,0:T(8,128)S(1)}, f32[8,128]{1,0:T(8,128)S(1)}, u32[]{:S(2)}, u32[]{:S(2)}) %collective-permute-start.4) | collective-permute-done | bytes 4128 | tf_op jit(solution)/shard_map/ppermute | solution.py:492
  22.3 0.0 collective-permute-start.9
  22.3 1.7 %collective-permute-start.8 = (f32[8,128]{1,0:T(8,128)S(1)}, f32[8,128]{1,0:T(8,128)S(1)}, u32[]{:S(2)}, u32[]{:S(2)}) collective-permute-start(f32[8,128]{1,0:T(8,128)S(1)} %add_add_fusion.1), channel_id=1, source_target_pairs={{0,2},{1,3},{2,0},{3,1},{4,6},{5,7},{6,4},{7,5},{8,10},{9,11},{10,... | collective-permute-start | bytes 12296 | tf_op jit(solution)/shard_map/ppermute | solution.py:492
  24.0 0.2 collective-permute-start.7
  24.2 0.8 %shard_map.54.energy = f32[3,96,128]{2,1,0:T(8,128)S(1)} custom-call(f32[51,8,128]{2,1,0:T(8,128)S(1)} %get-tuple-element.24.base, f32[51,8,128]{2,1,0:T(8,128)S(1)} %get-tuple-element.25.second, f32[6,8,128]{2,1,0:T(8,128)S(1)} %get-tuple-element.26.edges, s32[96,128]{1,0:T(8,128)S(1)} %bitcast.15), custom_call_target="tpu_custom_call" | custom-call | tf_op jit(solution)/shard_map/pallas_call | solution.py:540
  24.9 0.4 %collective-permute-done.9 = f32[8,128]{1,0:T(8,128)S(1)} collective-permute-done((f32[8,128]{1,0:T(8,128)S(1)}, f32[8,128]{1,0:T(8,128)S(1)}, u32[]{:S(2)}, u32[]{:S(2)}) %collective-permute-start.9) | collective-permute-done | bytes 4128 | tf_op jit(solution)/shard_map/ppermute | solution.py:492
  25.3 0.6 %collective-permute-done.8 = f32[8,128]{1,0:T(8,128)S(1)} collective-permute-done((f32[8,128]{1,0:T(8,128)S(1)}, f32[8,128]{1,0:T(8,128)S(1)}, u32[]{:S(2)}, u32[]{:S(2)}) %collective-permute-start.8) | collective-permute-done | bytes 4128 | tf_op jit(solution)/shard_map/ppermute | solution.py:492
  26.0 0.0 collective-permute-done.7
  26.0 0.7 %shard_map.55 = (f32[3,17,6,128]{3,2,1,0:T(8,128)}, f32[96,128]{1,0:T(8,128)}) custom-call(f32[51,8,128]{2,1,0:T(8,128)S(1)} %get-tuple-element.24.base, f32[51,8,128]{2,1,0:T(8,128)S(1)} %get-tuple-element.25.second, f32[3,96,128]{2,1,0:T(8,128)S(1)} %shard_map.54.energy, f32[8,128]{1,0:T(8,128)S(1)} %add_add_fusion.sums), custom_call_target="tpu_custom_call" | custom-call | tf_op jit(solution)/shard_map/pallas_call | solution.py:542
  (2 shorter events, 0.0 us)
Async XLA Ops:
  0.6 1.1 %copy-start = (s32[17,6,128]{2,1,0:T(8,128)S(1)}, s32[17,6,128]{2,1,0:T(8,128)}, u32[]{:S(2)}) copy-start(s32[17,6,128]{2,1,0:T(8,128)} %fixed.5) | copy-start | bytes 156676
  0.6 1.1 %copy-start.1 = (s32[16,6,128]{2,0,1:T(8,128)S(1)}, s32[16,6,128]{2,0,1:T(8,128)}, u32[]{:S(2)}) copy-start(s32[16,6,128]{2,0,1:T(8,128)} %param.4) | copy-start | bytes 147460
  2.0 3.8 %collective-permute-start = (f32[2,8,128]{2,1,0:T(8,128)S(1)}, f32[2,8,128]{2,1,0:T(8,128)S(1)}, u32[]{:S(2)}, u32[]{:S(2)}) collective-permute-start(f32[2,8,128]{2,1,0:T(8,128)S(1)} %get-tuple-element.17), channel_id=1, source_target_pairs={{0,3},{1,2},{2,1},{3,0},{4,7},{5,6},{6,5},{7,4},{8,11},{9,10},{10,... | collective-permute-start | bytes 24584 | tf_op jit(solution)/shard_map/ppermute | solution.py:469
  4.4 1.5 %collective-permute-start.1 = (f32[2,8,128]{2,1,0:T(8,128)S(1)}, f32[2,8,128]{2,1,0:T(8,128)S(1)}, u32[]{:S(2)}, u32[]{:S(2)}) collective-permute-start(f32[2,8,128]{2,1,0:T(8,128)S(1)} %get-tuple-element.18), channel_id=1, source_target_pairs={{0,1},{1,0},{2,3},{3,2},{4,5},{5,4},{6,7},{7,6},{8,9},{9,8},{10,11... | collective-permute-start | bytes 24584 | tf_op jit(solution)/shard_map/ppermute | solution.py:470
  6.0 7.5 %collective-permute-start.2 = (f32[168,128]{1,0:T(8,128)S(1)}, f32[168,128]{1,0:T(8,128)S(1)}, u32[]{:S(2)}, u32[]{:S(2)}) collective-permute-start(f32[168,128]{1,0:T(8,128)S(1)} %get-tuple-element.22), channel_id=1, source_target_pairs={{0,4},{4,8},{8,12},{12,0},{1,5},{5,9},{9,13},{13,1},{2,6},{6,10},{... | collective-permute-start | bytes 258056 | tf_op jit(solution)/shard_map/ppermute | solution.py:476
  8.3 6.1 %collective-permute-start.3 = (f32[168,128]{1,0:T(8,128)S(1)}, f32[168,128]{1,0:T(8,128)S(1)}, u32[]{:S(2)}, u32[]{:S(2)}) collective-permute-start(f32[168,128]{1,0:T(8,128)S(1)} %get-tuple-element.23), channel_id=1, source_target_pairs={{4,0},{8,4},{12,8},{0,12},{5,1},{9,5},{13,9},{1,13},{6,2},{10,6},{... | collective-permute-start | bytes 258056 | tf_op jit(solution)/shard_map/ppermute | solution.py:477
  15.8 5.4 %collective-permute-start.6 = (f32[8,128]{1,0:T(8,128)S(1)}, f32[8,128]{1,0:T(8,128)S(1)}, u32[]{:S(2)}, u32[]{:S(2)}) collective-permute-start(f32[8,128]{1,0:T(8,128)S(1)} %get-tuple-element.27), channel_id=1, source_target_pairs={{0,4},{4,8},{8,12},{12,0},{1,5},{5,9},{9,13},{13,1},{2,6},{6,10},{... | collective-permute-start | bytes 12296 | tf_op jit(solution)/shard_map/ppermute | solution.py:492
  16.9 4.5 %collective-permute-start.5 = (f32[8,128]{1,0:T(8,128)S(1)}, f32[8,128]{1,0:T(8,128)S(1)}, u32[]{:S(2)}, u32[]{:S(2)}) collective-permute-start(f32[8,128]{1,0:T(8,128)S(1)} %get-tuple-element.27), channel_id=1, source_target_pairs={{0,8},{4,12},{8,0},{12,4},{1,9},{5,13},{9,1},{13,5},{2,10},{6,14},... | collective-permute-start | bytes 12296 | tf_op jit(solution)/shard_map/ppermute | solution.py:492
  18.7 3.6 %collective-permute-start.4 = (f32[8,128]{1,0:T(8,128)S(1)}, f32[8,128]{1,0:T(8,128)S(1)}, u32[]{:S(2)}, u32[]{:S(2)}) collective-permute-start(f32[8,128]{1,0:T(8,128)S(1)} %get-tuple-element.27), channel_id=1, source_target_pairs={{0,12},{4,0},{8,4},{12,8},{1,13},{5,1},{9,5},{13,9},{2,14},{6,2},{... | collective-permute-start | bytes 12296 | tf_op jit(solution)/shard_map/ppermute | solution.py:492
  22.3 3.0 %collective-permute-start.9 = (f32[8,128]{1,0:T(8,128)S(1)}, f32[8,128]{1,0:T(8,128)S(1)}, u32[]{:S(2)}, u32[]{:S(2)}) collective-permute-start(f32[8,128]{1,0:T(8,128)S(1)} %add_add_fusion.1), channel_id=1, source_target_pairs={{0,3},{1,2},{2,1},{3,0},{4,7},{5,6},{6,5},{7,4},{8,11},{9,10},{10,... | collective-permute-start | bytes 12296 | tf_op jit(solution)/shard_map/ppermute | solution.py:492
  22.3 3.7 %collective-permute-start.8 = (f32[8,128]{1,0:T(8,128)S(1)}, f32[8,128]{1,0:T(8,128)S(1)}, u32[]{:S(2)}, u32[]{:S(2)}) collective-permute-start(f32[8,128]{1,0:T(8,128)S(1)} %add_add_fusion.1), channel_id=1, source_target_pairs={{0,2},{1,3},{2,0},{3,1},{4,6},{5,7},{6,4},{7,5},{8,10},{9,11},{10,... | collective-permute-start | bytes 12296 | tf_op jit(solution)/shard_map/ppermute | solution.py:492
  24.0 2.0 %collective-permute-start.7 = (f32[8,128]{1,0:T(8,128)S(1)}, f32[8,128]{1,0:T(8,128)S(1)}, u32[]{:S(2)}, u32[]{:S(2)}) collective-permute-start(f32[8,128]{1,0:T(8,128)S(1)} %add_add_fusion.1), channel_id=1, source_target_pairs={{0,1},{1,0},{2,3},{3,2},{4,5},{5,4},{6,7},{7,6},{8,9},{9,8},{10,11... | collective-permute-start | bytes 12296 | tf_op jit(solution)/shard_map/ppermute | solution.py:492

commit v6 on v5

--- a/solution.py
+++ b/solution.py
@@ -17,8 +17,8 @@
 
 SLOTS = 7
 LANES = 128
-DOWN, DOWN_CORNERS = 168, 152
-UP, UP_CORNERS = 168, 83
+DOWN, DOWN_CORNERS = 144, 135
+UP, UP_CORNERS = 144, 83
 
 VMEM = pl.BlockSpec(memory_space=pltpu.VMEM)
 PARAMS = pltpu.CompilerParams(vmem_limit_bytes=32 * 1024 * 1024)
@@ -67,10 +67,10 @@
     rhs = (rhs_0, rhs_1, rhs_2)
     nodes, rows, width = rhs_0.shape
     layers = nodes - 1
-    lane = lanes()
+    lane = lax.broadcasted_iota(jnp.int32, (rows, LANES), 1)
     even = is_even("gy") if paired else True
     pad[...] = jnp.zeros(pad.shape, jnp.float32)
-    planes = [jnp.zeros((8, LANES), jnp.float32)] * 5
+    planes = [jnp.zeros((rows, LANES), jnp.float32)] * 5
     for k in range(nodes):
         here = (lane >= k * SLOTS) & (lane < k * SLOTS + 5)
         values = [rhs[c][k] for c in range(3)]
@@ -78,9 +78,10 @@
         values.append((1 - fixed[k]).astype(jnp.float32))
         for p, value in enumerate(values):
             if value is not None:
-                pad[5 * k + p, 0:rows, :] = value
-                planes[p] = jnp.where(here, lane_roll(pad[5 * k + p], k * SLOTS + 3), planes[p])
+                planes[p] = jnp.where(here, lane_roll(value, k * SLOTS + 3), planes[p])
     for p in range(5):
+        pad[p, 0:rows, :] = planes[p]
+        planes[p] = pad[p]
         own[p] = planes[p]
     high = [
         gather(nodes, (planes[0], -2, 0, 1), (planes[1], -1, 1, 1), (planes[2], 0, 2, 1), (planes[3], 2, 3, 2)),
@@ -99,7 +100,7 @@
             col2[p] = high[p]
 
 
-def row_kernel(rhs_0, rhs_1, rhs_2, phase, fixed, down, up):
+def row_kernel(rhs_0, rhs_1, rhs_2, phase, fixed, down, up, pair):
     rhs = (rhs_0, rhs_1, rhs_2)
     nodes, rows, width = rhs_0.shape
     layers, cn = nodes - 1, 3 * nodes
@@ -107,20 +108,20 @@
         for c in range(3):
             q = c * nodes + k
             down[q : q + 1, :] = rhs[c][k, 0:1]
-            down[cn + 2 * layers + q : cn + 2 * layers + q + 1, :] = rhs[c][k, 1:2]
+            down[cn + layers + nodes + q : cn + layers + nodes + q + 1, :] = rhs[c][k, 1:2]
             up[q : q + 1, :] = rhs[c][k, rows - 1 : rows]
-        at = 2 * cn + 2 * layers + k
+        at = cn + layers + k
         down[at : at + 1, :] = (1 - fixed[k, 0:1]).astype(jnp.float32)
-    for i in range(2):
-        at = cn + i * layers
-        down[at : at + layers, :] = table(phase[i * layers : (i + 1) * layers], PHASE_STIFFNESS)
-        first = (rows - 2 + i) * layers
-        up[at : at + layers, :] = table(phase[first : first + layers], PHASE_STIFFNESS)
-    down[2 * cn + 2 * layers + nodes :, :] = jnp.zeros((DOWN - 2 * cn - 2 * layers - nodes, LANES), jnp.float32)
-    up[cn + 2 * layers :, :] = jnp.zeros((UP - cn - 2 * layers, LANES), jnp.float32)
-
-
-def strip_kernel(nodes, paired, own, got2, got1, down, up, strip, down_out, up_out):
+    scale = [table(phase[i * layers : (i + 1) * layers], PHASE_STIFFNESS) for i in (0, 1, rows - 2, rows - 1)]
+    down[cn : cn + layers, :] = scale[0]
+    up[cn : cn + layers, :] = scale[2]
+    up[cn + layers : cn + 2 * layers, :] = scale[3]
+    pair[...] = scale[0] + scale[1]
+    down[DOWN_CORNERS:, :] = jnp.zeros((DOWN - DOWN_CORNERS, LANES), jnp.float32)
+    up[UP_CORNERS:, :] = jnp.zeros((UP - UP_CORNERS, LANES), jnp.float32)
+
+
+def strip_kernel(nodes, paired, own, got2, got1, down, up, pair, strip, down_out, up_out, dense):
     even_y = is_even("gy") if paired else True
     if paired:
         from_low = jnp.where(even_y, got2[0], got1[0])
@@ -140,8 +141,27 @@
     up_out[...] = up[...]
     for p, plane in enumerate(planes):
         strip[p] = plane
-        down_out[DOWN_CORNERS + 2 * p : DOWN_CORNERS + 2 * p + 2, :] = plane[0:2]
         up_out[UP_CORNERS + 2 * p : UP_CORNERS + 2 * p + 2, :] = plane[rows - 2 : rows]
+    around = planes[3] + planes[4]
+    around = around + pltpu.roll(around, 1, 0)
+    around = KE_DIAGONAL * (around + lane_roll(around, SLOTS))
+    inv = jnp.where(around > 0.0, 1.0 / around, 0.0)
+    corners = [plane[0:1] for plane in planes[0:3]]
+    corners += [(plane * inv)[1:2] for plane in planes[0:3]]
+    corners += [plane[0:1] for plane in planes[3:6]]
+    for p, value in enumerate(corners):
+        down_out[DOWN_CORNERS + p : DOWN_CORNERS + p + 1, :] = value
+    layers, cn = nodes - 1, 3 * nodes
+    tall = lax.broadcasted_iota(jnp.int32, (layers, LANES), 0)
+    wide = lax.broadcasted_iota(jnp.int32, (layers, LANES), 1)
+    edge = jnp.broadcast_to(planes[4][0:1] + planes[4][1:2], (layers, LANES))
+    edge = jnp.sum(jnp.where(wide == SLOTS * tall, edge, 0.0), axis=1, keepdims=True)
+    dense[...] = jnp.zeros(dense.shape, jnp.float32)
+    dense[1 : layers + 1, :] = pair[...] + jnp.where(wide == 0, edge, pltpu.roll(pair[...], 1, 1))
+    inv = 1.0 / (KE_DIAGONAL * (dense[0:nodes, :] + dense[1 : nodes + 1, :]))
+    for c in range(3):
+        at = cn + layers + nodes + c * nodes
+        down_out[at : at + nodes, :] = down[at : at + nodes, :] * inv
 
 
 PLANE = ("", "1", "2", "12")
@@ -213,7 +233,7 @@
 def operator_kernel(
     rhs_0, rhs_1, rhs_2, phase, fixed, strip, lo, hi,
     base, second, edges, sums,
-    held, residual, inverse, dense, far_base,
+    held, residual, inverse, turned,
 ):
     rhs, comps = (rhs_0, rhs_1, rhs_2), 3
     nodes, rows, width = rhs_0.shape
@@ -233,9 +253,6 @@
     def node_rows(x, x_m2):
         return x + jnp.where(below, x_m2, roll_down(x))
 
-    def node_row_7(x, x_7):
-        return jnp.broadcast_to(x[6:7], (8, LANES)) + x_7
-
     def plane_modes(x, y, x_up, y_up):
         near, far, near_up, far_up = x + y, y - x, x_up + y_up, y_up - x_up
         return {"": near + near_up, "1": near_up - near, "2": far + far_up, "12": far_up - far}
@@ -251,38 +268,26 @@
     def products(totals, d0, image, z, s, v):
         return tuple(t + x for t, x in zip(totals, (d0 * image, image * z, s * v, v * image)))
 
-    def corner(ref, p, which):
-        return spread(ref, (UP_CORNERS if ref is lo else DOWN_CORNERS) + 2 * p + which)
+    def above(p):
+        return spread(hi, DOWN_CORNERS + p)
+
+    def under(p, which):
+        return spread(lo, UP_CORNERS + 2 * p + which)
 
     tiles = [
-        jnp.where(row < 6, strip[p], jnp.where(last_row, corner(hi, p, 0), corner(lo, p, 1))) for p in range(6)
-    ]
-    sevens = [corner(hi, p, 1) for p in range(5)]
+        jnp.where(row < 6, strip[p], jnp.where(last_row, above(p if p < 3 else p + 3), under(p, 1))) for p in range(6)
+    ]
     left, right = tiles[3], tiles[4]
-    edge_rows = node_rows(right, corner(lo, 4, 0))
-    edge_rows_7 = node_row_7(right, sevens[4])
-
-    tall = lax.broadcasted_iota(jnp.int32, (layers, LANES), 0)
-    wide = lax.broadcasted_iota(jnp.int32, (layers, LANES), 1)
-    pair = hi[cn : cn + layers, :] + hi[cn + layers : cn + 2 * layers, :]
-    edge = jnp.broadcast_to(edge_rows_7[0:1], (layers, LANES))
-    edge = jnp.sum(jnp.where(wide == SLOTS * tall, edge, 0.0), axis=1, keepdims=True)
-    dense[...] = jnp.zeros(dense.shape, jnp.float32)
-    dense[1 : layers + 1, :] = pair + jnp.where(wide == 0, edge, pltpu.roll(pair, 1, 1))
-    inv_7 = dense[0:24, :] + dense[1:25, :]
-    inv_7 = jnp.where(inv_7 > 0.0, 1.0 / (KE_DIAGONAL * inv_7), 0.0)
-    for c in range(3):
-        x_7 = hi[cn + 2 * layers + c * nodes : cn + 2 * layers + c * nodes + 24, :] * inv_7
-        far_base[c] = x_7
-        far_base[3 + c] = pltpu.roll(x_7, LANES - 1, 1)
+    edge_rows = node_rows(right, under(4, 0))
+    row_7 = cn + layers + nodes
+    first_7 = row_7 // 8 * 8
+    turned[...] = pltpu.roll(hi[first_7:DOWN, :], LANES - 1, 1)
 
     def strip_diagonal(x):
         return KE_DIAGONAL * (x + lane_roll(x, SLOTS))
 
-    strip_diag = strip_diagonal(node_rows(left + right, corner(lo, 3, 0) + corner(lo, 4, 0)))
-    strip_diag_7 = strip_diagonal(node_row_7(left + right, sevens[3] + sevens[4]))
+    strip_diag = strip_diagonal(node_rows(left + right, under(3, 0) + under(4, 0)))
     strip_inv = jnp.where(strip_diag > 0.0, 1.0 / strip_diag, 0.0)
-    strip_inv_7 = jnp.where(strip_diag_7 > 0.0, 1.0 / strip_diag_7, 0.0)
     slot = lax.rem(lane, SLOTS)
     strip_scale = jnp.where((slot == 2) | (slot == 6), 0.0, right)
     strip_base = [tiles[c] * strip_inv for c in range(3)]
@@ -292,7 +297,7 @@
 
     lower = []
     for c in range(3):
-        x, x_7 = strip_base[c], sevens[c] * strip_inv_7
+        x, x_7 = strip_base[c], above(3 + c)
         y, y_7 = lane_roll(x, -1), lane_roll(x_7, -1)
         lower.append(plane_modes(x, y, jnp.where(last_row, x_7, roll_up(x)), jnp.where(last_row, y_7, roll_up(y))))
     f_low, f_up = join_layers([strip_scale * x for x in stress(split_layers(lower, strip_layers(lower)))])
@@ -330,15 +335,15 @@
             x = residual[q] * inv
             base[q] = x
             y = lane_roll(x, -1)
-            x_up = jnp.where(last_row, spread(far_base.at[c], k), roll_up(x))
-            y_up = jnp.where(last_row, spread(far_base.at[3 + c], k), roll_up(y))
+            x_up = jnp.where(last_row, spread(hi, row_7 + q), roll_up(x))
+            y_up = jnp.where(last_row, spread(turned, row_7 - first_7 + q), roll_up(y))
             out.append(plane_modes(x, y, x_up, y_up))
         return out
 
     def finish_layer(k, f, totals):
         inv = inverse[k]
         held[1, 0:rows, :] = 1.0 - fixed[k].astype(jnp.float32)
-        held[1, 6:7, :] = hi[pl.ds(2 * cn + 2 * layers + k, 1), :]
+        held[1, 6:7, :] = hi[pl.ds(cn + layers + k, 1), :]
         free = held[1] > 0.0
         inv = jnp.where(free, inv, 1.0)
         a, rest = totals[0], totals[1:]
@@ -409,10 +414,10 @@
     totals.append(
         jnp.where(mine & (lane < LANES - 1), total, 0.0) + jnp.where(mine & (slot == 4), strip_e, 0.0)
     )
+    rows_of = zero
     for i, x in enumerate(totals):
-        x = jnp.sum(jnp.sum(x, axis=0, keepdims=True), axis=1, keepdims=True)
-        sums[i : i + 1, :] = jnp.broadcast_to(x, (1, LANES))
-    sums[6:, :] = jnp.zeros((2, LANES), jnp.float32)
+        rows_of = jnp.where(row == i, jnp.broadcast_to(jnp.sum(x, axis=0, keepdims=True), (8, LANES)), rows_of)
+    sums[...] = jnp.broadcast_to(jnp.sum(rows_of, axis=1, keepdims=True), (8, LANES))
 
 
 def energy_kernel(base, second, edges, phase, energy):
@@ -511,14 +516,15 @@
     own, col1, col2 = call(
         functools.partial(column_kernel, paired),
         (jax.ShapeDtypeStruct((5, 8, LANES), f32), column, column),
-        [pltpu.VMEM((5 * nodes, 8, LANES), f32)],
+        [pltpu.VMEM((5, 8, LANES), f32)],
     )(*rhs, phase, fixed)
-    down, up = call(row_kernel, messages)(*rhs, phase, fixed)
+    down, up, pair = call(row_kernel, messages + (jax.ShapeDtypeStruct((layers, LANES), f32),))(*rhs, phase, fixed)
     near, far = (exchange_pairs if paired else exchange)(col1, col2, "gy")
     strip, down, up = call(
         functools.partial(strip_kernel, nodes, paired),
         (strips,) + messages,
-    )(own, far, near, down, up)
+        [pltpu.VMEM((32, LANES), f32)],
+    )(own, far, near, down, up, pair)
     high, low = exchange(down, up, "gx")
     field = jax.ShapeDtypeStruct((comps * nodes, 8, LANES), f32)
     base, second, edges, sums = call(
@@ -533,8 +539,7 @@
             pltpu.VMEM((3, 8, LANES), f32),
             pltpu.VMEM((comps * nodes, 8, LANES), f32),
             pltpu.VMEM((nodes, 8, LANES), f32),
-            pltpu.VMEM((32, LANES), f32),
-            pltpu.VMEM((6, 24, LANES), f32),
+            pltpu.VMEM((DOWN - (comps * nodes + layers + nodes) // 8 * 8, LANES), f32),
         ],
     )(*rhs, phase, fixed, strip, low, high)
     energy = call(energy_kernel, jax.ShapeDtypeStruct((3,) + phase.shape, f32))(base, second, edges, phase)

time: 27 us -> 26.9 us (level)
  waiting for transfers between devices: 8.27 us -> 7.84 us
    ppermute x1, waiting for transfers between devices: 3.14 us -> 2.64 us  [exchange(): low = lax.ppermute(up, axis, [(i, (i + 1) % count) for i in range(count)])]
where the time goes in v6:
time: 26.9 us; the launch traced here: 26.6 us
  starting transfers between devices  13.6 us (51%)
  waiting for transfers between devices  7.84 us (29%)
  Pallas kernels  3.34 us (12%)
  other arithmetic  1.05 us (4%)
  between operations  0.7 us (3%)
    ppermute x6, starting transfers between devices, total_over(): lax.ppermute(x, axis, pairs)  6.14 us
    ppermute x6, waiting for transfers between devices, total_over(): lax.ppermute(x, axis, pairs)  3.6 us
    ppermute x1, waiting for transfers between devices, exchange(): low = lax.ppermute(up, axis, [(i, (i + 1) % count) for i in range(count)])  2.64 us
    ppermute x1, starting transfers between devices, exchange_pairs(): lax.ppermute(two, axis, [(i, (i - 1) % count if i % 2 == 0 else (i + 1) %...  2.43 us
    ppermute x1, starting transfers between devices, exchange(): low = lax.ppermute(up, axis, [(i, (i + 1) % count) for i in range(count)])  2.31 us
    ppermute x1, starting transfers between devices, exchange(): lax.ppermute(down, axis, [((i + 1) % count, i) for i in range(count)])  2.09 us
    pallas_call x1, Pallas kernels, body(): call(operator_kernel, (field, field, strips, jax.ShapeDtypeStruct((8, LAN...  1.34 us
    mul x1, other arithmetic, body(): rhs = [(1 - fixed).astype(jnp.float32) * force[c] for c in range(comps)]  1.04 us
  transfers between devices with their start and end apart: 10, of which 9 were waited for; matrix products, arithmetic and copies ran while one was open for 0% of the time, Pallas kernels for 3%

profile of v6, /device:TPU:0, one launch (start us, length us, event | category | flops | bytes accessed | tf_op | source)
XLA Modules:
  0.0 26.6 jit_solution(8706071673394857685)
XLA Ops:
  0.6 0.0 copy-start
  0.6 0.0 copy-start.1
  0.6 1.0 %bitcast_multiply_fusion = (f32[17,6,128]{2,1,0:T(8,128)S(1)}, f32[17,6,128]{2,1,0:T(8,128)S(1)}, f32[17,6,128]{2,1,0:T(8,128)S(1)}) fusion(f32[3,17,6,128]{3,2,1,0:T(8,128)} %param.3, s32[17,6,128]{2,1,0:T(8,128)} %fixed.5), kind=kLoop, calls=%fused_computation | loop fusion | flops 65280 | bytes 365568 | tf_op jit(solution)/shard_map/mul | solution.py:506
  1.7 0.0 copy-done
  1.7 0.0 copy-done.1
  1.7 0.2 shard_map.50
  2.0 2.4 %collective-permute-start = (f32[2,8,128]{2,1,0:T(8,128)S(1)}, f32[2,8,128]{2,1,0:T(8,128)S(1)}, u32[]{:S(2)}, u32[]{:S(2)}) collective-permute-start(f32[2,8,128]{2,1,0:T(8,128)S(1)} %get-tuple-element.18), channel_id=1, source_target_pairs={{0,3},{1,2},{2,1},{3,0},{4,7},{5,6},{6,5},{7,4},{8,11},{9,10},{10,... | collective-permute-start | bytes 24584 | tf_op jit(solution)/shard_map/ppermute | solution.py:474
  4.4 0.7 %collective-permute-start.1 = (f32[2,8,128]{2,1,0:T(8,128)S(1)}, f32[2,8,128]{2,1,0:T(8,128)S(1)}, u32[]{:S(2)}, u32[]{:S(2)}) collective-permute-start(f32[2,8,128]{2,1,0:T(8,128)S(1)} %get-tuple-element.19), channel_id=1, source_target_pairs={{0,1},{1,0},{2,3},{3,2},{4,5},{5,4},{6,7},{7,6},{8,9},{9,8},{10,11... | collective-permute-start | bytes 24584 | tf_op jit(solution)/shard_map/ppermute | solution.py:475
  5.1 0.1 shard_map.51
  5.1 0.6 %collective-permute-done.got2 = f32[2,8,128]{2,1,0:T(8,128)S(1)} collective-permute-done((f32[2,8,128]{2,1,0:T(8,128)S(1)}, f32[2,8,128]{2,1,0:T(8,128)S(1)}, u32[]{:S(2)}, u32[]{:S(2)}) %collective-permute-start) | collective-permute-done | bytes 8224 | tf_op jit(solution)/shard_map/ppermute | solution.py:474
  5.7 0.1 collective-permute-done.1.got1
  5.9 0.2 shard_map.52
  6.1 2.3 %collective-permute-start.2 = (f32[144,128]{1,0:T(8,128)S(1)}, f32[144,128]{1,0:T(8,128)S(1)}, u32[]{:S(2)}, u32[]{:S(2)}) collective-permute-start(f32[144,128]{1,0:T(8,128)S(1)} %get-tuple-element.24), channel_id=1, source_target_pairs={{0,4},{4,8},{8,12},{12,0},{1,5},{5,9},{9,13},{13,1},{2,6},{6,10},{... | collective-permute-start | bytes 221192 | tf_op jit(solution)/shard_map/ppermute | solution.py:481
  8.4 2.1 %collective-permute-start.3 = (f32[144,128]{1,0:T(8,128)S(1)}, f32[144,128]{1,0:T(8,128)S(1)}, u32[]{:S(2)}, u32[]{:S(2)}) collective-permute-start(f32[144,128]{1,0:T(8,128)S(1)} %get-tuple-element.25), channel_id=1, source_target_pairs={{4,0},{8,4},{12,8},{0,12},{5,1},{9,5},{13,9},{1,13},{6,2},{10,6},{... | collective-permute-start | bytes 221192 | tf_op jit(solution)/shard_map/ppermute | solution.py:482
  10.5 2.6 %collective-permute-done.2.lo = f32[144,128]{1,0:T(8,128)S(1)} collective-permute-done((f32[144,128]{1,0:T(8,128)S(1)}, f32[144,128]{1,0:T(8,128)S(1)}, u32[]{:S(2)}, u32[]{:S(2)}) %collective-permute-start.2) | collective-permute-done | bytes 73760 | tf_op jit(solution)/shard_map/ppermute | solution.py:481
  13.1 0.9 %collective-permute-done.3.hi = f32[144,128]{1,0:T(8,128)S(1)} collective-permute-done((f32[144,128]{1,0:T(8,128)S(1)}, f32[144,128]{1,0:T(8,128)S(1)}, u32[]{:S(2)}, u32[]{:S(2)}) %collective-permute-start.3) | collective-permute-done | bytes 73760 | tf_op jit(solution)/shard_map/ppermute | solution.py:482
  14.0 1.3 %shard_map.53 = (f32[51,8,128]{2,1,0:T(8,128)S(1)}, f32[51,8,128]{2,1,0:T(8,128)S(1)}, f32[6,8,128]{2,1,0:T(8,128)S(1)}, f32[8,128]{1,0:T(8,128)S(1)}) custom-call(f32[17,6,128]{2,1,0:T(8,128)S(1)} %get-tuple-element.33.rhs_0, f32[17,6,128]{2,1,0:T(8,128)S(1)} %get-tuple-element.34.rhs_1, f32[17,6,128]{2,1,0:T(8,128)S(1)} %get-tuple-element.32.rhs_2, ...), custom_call_target="tpu_custom_call" | custom-call | tf_op jit(solution)/shard_map/pallas_call | solution.py:530
  15.3 1.1 %collective-permute-start.6 = (f32[8,128]{1,0:T(8,128)S(1)}, f32[8,128]{1,0:T(8,128)S(1)}, u32[]{:S(2)}, u32[]{:S(2)}) collective-permute-start(f32[8,128]{1,0:T(8,128)S(1)} %get-tuple-element.29), channel_id=1, source_target_pairs={{0,4},{4,8},{8,12},{12,0},{1,5},{5,9},{9,13},{13,1},{2,6},{6,10},{... | collective-permute-start | bytes 12296 | tf_op jit(solution)/shard_map/ppermute | solution.py:497
  16.4 2.1 %collective-permute-start.5 = (f32[8,128]{1,0:T(8,128)S(1)}, f32[8,128]{1,0:T(8,128)S(1)}, u32[]{:S(2)}, u32[]{:S(2)}) collective-permute-start(f32[8,128]{1,0:T(8,128)S(1)} %get-tuple-element.29), channel_id=1, source_target_pairs={{0,8},{4,12},{8,0},{12,4},{1,9},{5,13},{9,1},{13,5},{2,10},{6,14},... | collective-permute-start | bytes 12296 | tf_op jit(solution)/shard_map/ppermute | solution.py:497
  18.5 1.1 %collective-permute-start.4 = (f32[8,128]{1,0:T(8,128)S(1)}, f32[8,128]{1,0:T(8,128)S(1)}, u32[]{:S(2)}, u32[]{:S(2)}) collective-permute-start(f32[8,128]{1,0:T(8,128)S(1)} %get-tuple-element.29), channel_id=1, source_target_pairs={{0,12},{4,0},{8,4},{12,8},{1,13},{5,1},{9,5},{13,9},{2,14},{6,2},{... | collective-permute-start | bytes 12296 | tf_op jit(solution)/shard_map/ppermute | solution.py:497
  19.6 1.1 %collective-permute-done.6 = f32[8,128]{1,0:T(8,128)S(1)} collective-permute-done((f32[8,128]{1,0:T(8,128)S(1)}, f32[8,128]{1,0:T(8,128)S(1)}, u32[]{:S(2)}, u32[]{:S(2)}) %collective-permute-start.6) | collective-permute-done | bytes 4128 | tf_op jit(solution)/shard_map/ppermute | solution.py:497
  20.7 0.2 collective-permute-done.5
  21.0 1.2 %collective-permute-done.4 = f32[8,128]{1,0:T(8,128)S(1)} collective-permute-done((f32[8,128]{1,0:T(8,128)S(1)}, f32[8,128]{1,0:T(8,128)S(1)}, u32[]{:S(2)}, u32[]{:S(2)}) %collective-permute-start.4) | collective-permute-done | bytes 4128 | tf_op jit(solution)/shard_map/ppermute | solution.py:497
  22.2 0.0 collective-permute-start.9
  22.2 1.8 %collective-permute-start.8 = (f32[8,128]{1,0:T(8,128)S(1)}, f32[8,128]{1,0:T(8,128)S(1)}, u32[]{:S(2)}, u32[]{:S(2)}) collective-permute-start(f32[8,128]{1,0:T(8,128)S(1)} %add_add_fusion.1), channel_id=1, source_target_pairs={{0,2},{1,3},{2,0},{3,1},{4,6},{5,7},{6,4},{7,5},{8,10},{9,11},{10,... | collective-permute-start | bytes 12296 | tf_op jit(solution)/shard_map/ppermute | solution.py:497
  23.9 0.1 collective-permute-start.7
  24.0 0.8 %shard_map.54.energy = f32[3,96,128]{2,1,0:T(8,128)S(1)} custom-call(f32[51,8,128]{2,1,0:T(8,128)S(1)} %get-tuple-element.26.base, f32[51,8,128]{2,1,0:T(8,128)S(1)} %get-tuple-element.27.second, f32[6,8,128]{2,1,0:T(8,128)S(1)} %get-tuple-element.28.edges, s32[96,128]{1,0:T(8,128)S(1)} %bitcast.15), custom_call_target="tpu_custom_call" | custom-call | tf_op jit(solution)/shard_map/pallas_call | solution.py:545
  24.8 0.4 %collective-permute-done.9 = f32[8,128]{1,0:T(8,128)S(1)} collective-permute-done((f32[8,128]{1,0:T(8,128)S(1)}, f32[8,128]{1,0:T(8,128)S(1)}, u32[]{:S(2)}, u32[]{:S(2)}) %collective-permute-start.9) | collective-permute-done | bytes 4128 | tf_op jit(solution)/shard_map/ppermute | solution.py:497
  25.2 0.6 %collective-permute-done.8 = f32[8,128]{1,0:T(8,128)S(1)} collective-permute-done((f32[8,128]{1,0:T(8,128)S(1)}, f32[8,128]{1,0:T(8,128)S(1)}, u32[]{:S(2)}, u32[]{:S(2)}) %collective-permute-start.8) | collective-permute-done | bytes 4128 | tf_op jit(solution)/shard_map/ppermute | solution.py:497
  25.8 0.0 collective-permute-done.7
  25.8 0.7 %shard_map.55 = (f32[3,17,6,128]{3,2,1,0:T(8,128)}, f32[96,128]{1,0:T(8,128)}) custom-call(f32[51,8,128]{2,1,0:T(8,128)S(1)} %get-tuple-element.26.base, f32[51,8,128]{2,1,0:T(8,128)S(1)} %get-tuple-element.27.second, f32[3,96,128]{2,1,0:T(8,128)S(1)} %shard_map.54.energy, f32[8,128]{1,0:T(8,128)S(1)} %add_add_fusion.sums), custom_call_target="tpu_custom_call" | custom-call | tf_op jit(solution)/shard_map/pallas_call | solution.py:547
  (2 shorter events, 0.0 us)
Async XLA Ops:
  0.6 1.1 %copy-start = (s32[17,6,128]{2,1,0:T(8,128)S(1)}, s32[17,6,128]{2,1,0:T(8,128)}, u32[]{:S(2)}) copy-start(s32[17,6,128]{2,1,0:T(8,128)} %fixed.5) | copy-start | bytes 156676
  0.6 1.1 %copy-start.1 = (s32[16,6,128]{2,0,1:T(8,128)S(1)}, s32[16,6,128]{2,0,1:T(8,128)}, u32[]{:S(2)}) copy-start(s32[16,6,128]{2,0,1:T(8,128)} %param.4) | copy-start | bytes 147460
  2.0 3.8 %collective-permute-start = (f32[2,8,128]{2,1,0:T(8,128)S(1)}, f32[2,8,128]{2,1,0:T(8,128)S(1)}, u32[]{:S(2)}, u32[]{:S(2)}) collective-permute-start(f32[2,8,128]{2,1,0:T(8,128)S(1)} %get-tuple-element.18), channel_id=1, source_target_pairs={{0,3},{1,2},{2,1},{3,0},{4,7},{5,6},{6,5},{7,4},{8,11},{9,10},{10,... | collective-permute-start | bytes 24584 | tf_op jit(solution)/shard_map/ppermute | solution.py:474
  4.4 1.5 %collective-permute-start.1 = (f32[2,8,128]{2,1,0:T(8,128)S(1)}, f32[2,8,128]{2,1,0:T(8,128)S(1)}, u32[]{:S(2)}, u32[]{:S(2)}) collective-permute-start(f32[2,8,128]{2,1,0:T(8,128)S(1)} %get-tuple-element.19), channel_id=1, source_target_pairs={{0,1},{1,0},{2,3},{3,2},{4,5},{5,4},{6,7},{7,6},{8,9},{9,8},{10,11... | collective-permute-start | bytes 24584 | tf_op jit(solution)/shard_map/ppermute | solution.py:475
  6.1 7.0 %collective-permute-start.2 = (f32[144,128]{1,0:T(8,128)S(1)}, f32[144,128]{1,0:T(8,128)S(1)}, u32[]{:S(2)}, u32[]{:S(2)}) collective-permute-start(f32[144,128]{1,0:T(8,128)S(1)} %get-tuple-element.24), channel_id=1, source_target_pairs={{0,4},{4,8},{8,12},{12,0},{1,5},{5,9},{9,13},{13,1},{2,6},{6,10},{... | collective-permute-start | bytes 221192 | tf_op jit(solution)/shard_map/ppermute | solution.py:481
  8.4 5.6 %collective-permute-start.3 = (f32[144,128]{1,0:T(8,128)S(1)}, f32[144,128]{1,0:T(8,128)S(1)}, u32[]{:S(2)}, u32[]{:S(2)}) collective-permute-start(f32[144,128]{1,0:T(8,128)S(1)} %get-tuple-element.25), channel_id=1, source_target_pairs={{4,0},{8,4},{12,8},{0,12},{5,1},{9,5},{13,9},{1,13},{6,2},{10,6},{... | collective-permute-start | bytes 221192 | tf_op jit(solution)/shard_map/ppermute | solution.py:482
  15.3 5.4 %collective-permute-start.6 = (f32[8,128]{1,0:T(8,128)S(1)}, f32[8,128]{1,0:T(8,128)S(1)}, u32[]{:S(2)}, u32[]{:S(2)}) collective-permute-start(f32[8,128]{1,0:T(8,128)S(1)} %get-tuple-element.29), channel_id=1, source_target_pairs={{0,4},{4,8},{8,12},{12,0},{1,5},{5,9},{9,13},{13,1},{2,6},{6,10},{... | collective-permute-start | bytes 12296 | tf_op jit(solution)/shard_map/ppermute | solution.py:497
  16.4 4.5 %collective-permute-start.5 = (f32[8,128]{1,0:T(8,128)S(1)}, f32[8,128]{1,0:T(8,128)S(1)}, u32[]{:S(2)}, u32[]{:S(2)}) collective-permute-start(f32[8,128]{1,0:T(8,128)S(1)} %get-tuple-element.29), channel_id=1, source_target_pairs={{0,8},{4,12},{8,0},{12,4},{1,9},{5,13},{9,1},{13,5},{2,10},{6,14},... | collective-permute-start | bytes 12296 | tf_op jit(solution)/shard_map/ppermute | solution.py:497
  18.5 3.6 %collective-permute-start.4 = (f32[8,128]{1,0:T(8,128)S(1)}, f32[8,128]{1,0:T(8,128)S(1)}, u32[]{:S(2)}, u32[]{:S(2)}) collective-permute-start(f32[8,128]{1,0:T(8,128)S(1)} %get-tuple-element.29), channel_id=1, source_target_pairs={{0,12},{4,0},{8,4},{12,8},{1,13},{5,1},{9,5},{13,9},{2,14},{6,2},{... | collective-permute-start | bytes 12296 | tf_op jit(solution)/shard_map/ppermute | solution.py:497
  22.2 3.0 %collective-permute-start.9 = (f32[8,128]{1,0:T(8,128)S(1)}, f32[8,128]{1,0:T(8,128)S(1)}, u32[]{:S(2)}, u32[]{:S(2)}) collective-permute-start(f32[8,128]{1,0:T(8,128)S(1)} %add_add_fusion.1), channel_id=1, source_target_pairs={{0,3},{1,2},{2,1},{3,0},{4,7},{5,6},{6,5},{7,4},{8,11},{9,10},{10,... | collective-permute-start | bytes 12296 | tf_op jit(solution)/shard_map/ppermute | solution.py:497
  22.2 3.7 %collective-permute-start.8 = (f32[8,128]{1,0:T(8,128)S(1)}, f32[8,128]{1,0:T(8,128)S(1)}, u32[]{:S(2)}, u32[]{:S(2)}) collective-permute-start(f32[8,128]{1,0:T(8,128)S(1)} %add_add_fusion.1), channel_id=1, source_target_pairs={{0,2},{1,3},{2,0},{3,1},{4,6},{5,7},{6,4},{7,5},{8,10},{9,11},{10,... | collective-permute-start | bytes 12296 | tf_op jit(solution)/shard_map/ppermute | solution.py:497
  23.9 1.9 %collective-permute-start.7 = (f32[8,128]{1,0:T(8,128)S(1)}, f32[8,128]{1,0:T(8,128)S(1)}, u32[]{:S(2)}, u32[]{:S(2)}) collective-permute-start(f32[8,128]{1,0:T(8,128)S(1)} %add_add_fusion.1), channel_id=1, source_target_pairs={{0,1},{1,0},{2,3},{3,2},{4,5},{5,4},{6,7},{7,6},{8,9},{9,8},{10,11... | collective-permute-start | bytes 12296 | tf_op jit(solution)/shard_map/ppermute | solution.py:497

commit v7 on v6

--- a/solution.py
+++ b/solution.py
@@ -233,7 +233,7 @@
 def operator_kernel(
     rhs_0, rhs_1, rhs_2, phase, fixed, strip, lo, hi,
     base, second, edges, sums,
-    held, residual, inverse, turned,
+    scales, frees, residual, inverse, turned,
 ):
     rhs, comps = (rhs_0, rhs_1, rhs_2), 3
     nodes, rows, width = rhs_0.shape
@@ -316,10 +316,10 @@
     strip_e = strip_scale * inner(stress(m), m)
 
     def box(k):
-        held[0, 0:rows, :] = table(element_rows(phase, k, layers), PHASE_STIFFNESS)
-        held[0, 6:7, :] = hi[pl.ds(cn + k, 1), :]
-        held[0, 7:8, :] = lo[pl.ds(cn + layers + k, 1), :]
-        x = held[0]
+        scales[k, 0:rows, :] = table(element_rows(phase, k, layers), PHASE_STIFFNESS)
+        scales[k, 6:7, :] = hi[pl.ds(cn + k, 1), :]
+        scales[k, 7:8, :] = lo[pl.ds(cn + layers + k, 1), :]
+        x = scales[k]
         r = node_rows(x, spread(lo, cn + k))
         return x, r + jnp.where(lane == 0, lane_roll(edge_rows, -SLOTS * k), lane_roll(r, 1))
 
@@ -342,9 +342,10 @@
 
     def finish_layer(k, f, totals):
         inv = inverse[k]
-        held[1, 0:rows, :] = 1.0 - fixed[k].astype(jnp.float32)
-        held[1, 6:7, :] = hi[pl.ds(cn + layers + k, 1), :]
-        free = held[1] > 0.0
+        frees[k, 0:rows, :] = 1.0 - fixed[k].astype(jnp.float32)
+        frees[k, 6:7, :] = hi[pl.ds(cn + layers + k, 1), :]
+        frees[k, 7:8, :] = jnp.zeros((1, LANES), jnp.float32)
+        free = frees[k] > 0.0
         inv = jnp.where(free, inv, 1.0)
         a, rest = totals[0], totals[1:]
         for c in range(3):
@@ -366,8 +367,6 @@
         return [{m: x[4 * c + i] for i, m in enumerate(PLANE)} for c in range(3)]
 
     zero = jnp.zeros((8, LANES), jnp.float32)
-    held[1] = zero
-    held[2] = zero
 
     def element(k, low_modes, high_modes, scale, pending, totals):
         g = stress(split_layers(low_modes, high_modes))
@@ -401,8 +400,7 @@
         low_modes, total = carry
         high = second_layer(k + 1)
         m = split_layers(unflat(low_modes), high)
-        held[2, 0:rows, :] = table(element_rows(phase, k, layers), PHASE_STIFFNESS)
-        return flat(high), total + held[2] * inner(stress(m), m)
+        return flat(high), total + scales[k] * inner(stress(m), m)
 
     _, total = lax.fori_loop(0, layers, again, (flat(second_layer(0)), zero), unroll=True)
     mine = row < rows
@@ -536,7 +534,8 @@
             jax.ShapeDtypeStruct((8, LANES), f32),
         ),
         [
-            pltpu.VMEM((3, 8, LANES), f32),
+            pltpu.VMEM((layers, 8, LANES), f32),
+            pltpu.VMEM((nodes, 8, LANES), f32),
             pltpu.VMEM((comps * nodes, 8, LANES), f32),
             pltpu.VMEM((nodes, 8, LANES), f32),
             pltpu.VMEM((DOWN - (comps * nodes + layers + nodes) // 8 * 8, LANES), f32),

time: 26.9 us -> 26.9 us (level)
  no operation moved by 1% of the time
where the time goes in v7:
time: 26.9 us; the launch traced here: 26.6 us
  starting transfers between devices  13.6 us (51%)
  waiting for transfers between devices  7.84 us (29%)
  Pallas kernels  3.31 us (12%)
  other arithmetic  1.05 us (4%)
  between operations  0.7 us (3%)
    ppermute x6, starting transfers between devices, total_over(): lax.ppermute(x, axis, pairs)  6.14 us
    ppermute x6, waiting for transfers between devices, total_over(): lax.ppermute(x, axis, pairs)  3.6 us
    ppermute x1, waiting for transfers between devices, exchange(): low = lax.ppermute(up, axis, [(i, (i + 1) % count) for i in range(count)])  2.64 us
    ppermute x1, starting transfers between devices, exchange_pairs(): lax.ppermute(two, axis, [(i, (i - 1) % count if i % 2 == 0 else (i + 1) %...  2.43 us
    ppermute x1, starting transfers between devices, exchange(): low = lax.ppermute(up, axis, [(i, (i + 1) % count) for i in range(count)])  2.31 us
    ppermute x1, starting transfers between devices, exchange(): lax.ppermute(down, axis, [((i + 1) % count, i) for i in range(count)])  2.09 us
    pallas_call x1, Pallas kernels, body(): call(operator_kernel, (field, field, strips, jax.ShapeDtypeStruct((8, LAN...  1.31 us
    mul x1, other arithmetic, body(): rhs = [(1 - fixed).astype(jnp.float32) * force[c] for c in range(comps)]  1.04 us
  transfers between devices with their start and end apart: 10, of which 9 were waited for; matrix products, arithmetic and copies ran while one was open for 0% of the time, Pallas kernels for 3%

profile of v7, /device:TPU:0, one launch (start us, length us, event | category | flops | bytes accessed | tf_op | source)
XLA Modules:
  0.0 26.6 jit_solution(9918187636913227659)
XLA Ops:
  0.6 0.0 copy-start
  0.6 0.0 copy-start.1
  0.6 1.0 %bitcast_multiply_fusion = (f32[17,6,128]{2,1,0:T(8,128)S(1)}, f32[17,6,128]{2,1,0:T(8,128)S(1)}, f32[17,6,128]{2,1,0:T(8,128)S(1)}) fusion(f32[3,17,6,128]{3,2,1,0:T(8,128)} %param.3, s32[17,6,128]{2,1,0:T(8,128)} %fixed.5), kind=kLoop, calls=%fused_computation | loop fusion | flops 65280 | bytes 365568 | tf_op jit(solution)/shard_map/mul | solution.py:504
  1.7 0.0 copy-done
  1.7 0.0 copy-done.1
  1.7 0.2 shard_map.50
  2.0 2.4 %collective-permute-start = (f32[2,8,128]{2,1,0:T(8,128)S(1)}, f32[2,8,128]{2,1,0:T(8,128)S(1)}, u32[]{:S(2)}, u32[]{:S(2)}) collective-permute-start(f32[2,8,128]{2,1,0:T(8,128)S(1)} %get-tuple-element.18), channel_id=1, source_target_pairs={{0,3},{1,2},{2,1},{3,0},{4,7},{5,6},{6,5},{7,4},{8,11},{9,10},{10,... | collective-permute-start | bytes 24584 | tf_op jit(solution)/shard_map/ppermute | solution.py:472
  4.4 0.7 %collective-permute-start.1 = (f32[2,8,128]{2,1,0:T(8,128)S(1)}, f32[2,8,128]{2,1,0:T(8,128)S(1)}, u32[]{:S(2)}, u32[]{:S(2)}) collective-permute-start(f32[2,8,128]{2,1,0:T(8,128)S(1)} %get-tuple-element.19), channel_id=1, source_target_pairs={{0,1},{1,0},{2,3},{3,2},{4,5},{5,4},{6,7},{7,6},{8,9},{9,8},{10,11... | collective-permute-start | bytes 24584 | tf_op jit(solution)/shard_map/ppermute | solution.py:473
  5.1 0.1 shard_map.51
  5.1 0.6 %collective-permute-done.got2 = f32[2,8,128]{2,1,0:T(8,128)S(1)} collective-permute-done((f32[2,8,128]{2,1,0:T(8,128)S(1)}, f32[2,8,128]{2,1,0:T(8,128)S(1)}, u32[]{:S(2)}, u32[]{:S(2)}) %collective-permute-start) | collective-permute-done | bytes 8224 | tf_op jit(solution)/shard_map/ppermute | solution.py:472
  5.7 0.1 collective-permute-done.1.got1
  5.9 0.2 shard_map.52
  6.1 2.3 %collective-permute-start.2 = (f32[144,128]{1,0:T(8,128)S(1)}, f32[144,128]{1,0:T(8,128)S(1)}, u32[]{:S(2)}, u32[]{:S(2)}) collective-permute-start(f32[144,128]{1,0:T(8,128)S(1)} %get-tuple-element.24), channel_id=1, source_target_pairs={{0,4},{4,8},{8,12},{12,0},{1,5},{5,9},{9,13},{13,1},{2,6},{6,10},{... | collective-permute-start | bytes 221192 | tf_op jit(solution)/shard_map/ppermute | solution.py:479
  8.4 2.1 %collective-permute-start.3 = (f32[144,128]{1,0:T(8,128)S(1)}, f32[144,128]{1,0:T(8,128)S(1)}, u32[]{:S(2)}, u32[]{:S(2)}) collective-permute-start(f32[144,128]{1,0:T(8,128)S(1)} %get-tuple-element.25), channel_id=1, source_target_pairs={{4,0},{8,4},{12,8},{0,12},{5,1},{9,5},{13,9},{1,13},{6,2},{10,6},{... | collective-permute-start | bytes 221192 | tf_op jit(solution)/shard_map/ppermute | solution.py:480
  10.5 2.6 %collective-permute-done.2.lo = f32[144,128]{1,0:T(8,128)S(1)} collective-permute-done((f32[144,128]{1,0:T(8,128)S(1)}, f32[144,128]{1,0:T(8,128)S(1)}, u32[]{:S(2)}, u32[]{:S(2)}) %collective-permute-start.2) | collective-permute-done | bytes 73760 | tf_op jit(solution)/shard_map/ppermute | solution.py:479
  13.1 0.9 %collective-permute-done.3.hi = f32[144,128]{1,0:T(8,128)S(1)} collective-permute-done((f32[144,128]{1,0:T(8,128)S(1)}, f32[144,128]{1,0:T(8,128)S(1)}, u32[]{:S(2)}, u32[]{:S(2)}) %collective-permute-start.3) | collective-permute-done | bytes 73760 | tf_op jit(solution)/shard_map/ppermute | solution.py:480
  14.0 1.3 %shard_map.53 = (f32[51,8,128]{2,1,0:T(8,128)S(1)}, f32[51,8,128]{2,1,0:T(8,128)S(1)}, f32[6,8,128]{2,1,0:T(8,128)S(1)}, f32[8,128]{1,0:T(8,128)S(1)}) custom-call(f32[17,6,128]{2,1,0:T(8,128)S(1)} %get-tuple-element.33.rhs_0, f32[17,6,128]{2,1,0:T(8,128)S(1)} %get-tuple-element.34.rhs_1, f32[17,6,128]{2,1,0:T(8,128)S(1)} %get-tuple-element.32.rhs_2, ...), custom_call_target="tpu_custom_call" | custom-call | tf_op jit(solution)/shard_map/pallas_call | solution.py:528
  15.3 1.1 %collective-permute-start.6 = (f32[8,128]{1,0:T(8,128)S(1)}, f32[8,128]{1,0:T(8,128)S(1)}, u32[]{:S(2)}, u32[]{:S(2)}) collective-permute-start(f32[8,128]{1,0:T(8,128)S(1)} %get-tuple-element.29), channel_id=1, source_target_pairs={{0,4},{4,8},{8,12},{12,0},{1,5},{5,9},{9,13},{13,1},{2,6},{6,10},{... | collective-permute-start | bytes 12296 | tf_op jit(solution)/shard_map/ppermute | solution.py:495
  16.4 2.1 %collective-permute-start.5 = (f32[8,128]{1,0:T(8,128)S(1)}, f32[8,128]{1,0:T(8,128)S(1)}, u32[]{:S(2)}, u32[]{:S(2)}) collective-permute-start(f32[8,128]{1,0:T(8,128)S(1)} %get-tuple-element.29), channel_id=1, source_target_pairs={{0,8},{4,12},{8,0},{12,4},{1,9},{5,13},{9,1},{13,5},{2,10},{6,14},... | collective-permute-start | bytes 12296 | tf_op jit(solution)/shard_map/ppermute | solution.py:495
  18.5 1.1 %collective-permute-start.4 = (f32[8,128]{1,0:T(8,128)S(1)}, f32[8,128]{1,0:T(8,128)S(1)}, u32[]{:S(2)}, u32[]{:S(2)}) collective-permute-start(f32[8,128]{1,0:T(8,128)S(1)} %get-tuple-element.29), channel_id=1, source_target_pairs={{0,12},{4,0},{8,4},{12,8},{1,13},{5,1},{9,5},{13,9},{2,14},{6,2},{... | collective-permute-start | bytes 12296 | tf_op jit(solution)/shard_map/ppermute | solution.py:495
  19.6 1.1 %collective-permute-done.6 = f32[8,128]{1,0:T(8,128)S(1)} collective-permute-done((f32[8,128]{1,0:T(8,128)S(1)}, f32[8,128]{1,0:T(8,128)S(1)}, u32[]{:S(2)}, u32[]{:S(2)}) %collective-permute-start.6) | collective-permute-done | bytes 4128 | tf_op jit(solution)/shard_map/ppermute | solution.py:495
  20.7 0.2 collective-permute-done.5
  20.9 1.2 %collective-permute-done.4 = f32[8,128]{1,0:T(8,128)S(1)} collective-permute-done((f32[8,128]{1,0:T(8,128)S(1)}, f32[8,128]{1,0:T(8,128)S(1)}, u32[]{:S(2)}, u32[]{:S(2)}) %collective-permute-start.4) | collective-permute-done | bytes 4128 | tf_op jit(solution)/shard_map/ppermute | solution.py:495
  22.1 0.0 collective-permute-start.9
  22.1 1.8 %collective-permute-start.8 = (f32[8,128]{1,0:T(8,128)S(1)}, f32[8,128]{1,0:T(8,128)S(1)}, u32[]{:S(2)}, u32[]{:S(2)}) collective-permute-start(f32[8,128]{1,0:T(8,128)S(1)} %add_add_fusion.1), channel_id=1, source_target_pairs={{0,2},{1,3},{2,0},{3,1},{4,6},{5,7},{6,4},{7,5},{8,10},{9,11},{10,... | collective-permute-start | bytes 12296 | tf_op jit(solution)/shard_map/ppermute | solution.py:495
  23.9 0.1 collective-permute-start.7
  24.0 0.8 %shard_map.54.energy = f32[3,96,128]{2,1,0:T(8,128)S(1)} custom-call(f32[51,8,128]{2,1,0:T(8,128)S(1)} %get-tuple-element.26.base, f32[51,8,128]{2,1,0:T(8,128)S(1)} %get-tuple-element.27.second, f32[6,8,128]{2,1,0:T(8,128)S(1)} %get-tuple-element.28.edges, s32[96,128]{1,0:T(8,128)S(1)} %bitcast.15), custom_call_target="tpu_custom_call" | custom-call | tf_op jit(solution)/shard_map/pallas_call | solution.py:544
  24.8 0.4 %collective-permute-done.9 = f32[8,128]{1,0:T(8,128)S(1)} collective-permute-done((f32[8,128]{1,0:T(8,128)S(1)}, f32[8,128]{1,0:T(8,128)S(1)}, u32[]{:S(2)}, u32[]{:S(2)}) %collective-permute-start.9) | collective-permute-done | bytes 4128 | tf_op jit(solution)/shard_map/ppermute | solution.py:495
  25.2 0.6 %collective-permute-done.8 = f32[8,128]{1,0:T(8,128)S(1)} collective-permute-done((f32[8,128]{1,0:T(8,128)S(1)}, f32[8,128]{1,0:T(8,128)S(1)}, u32[]{:S(2)}, u32[]{:S(2)}) %collective-permute-start.8) | collective-permute-done | bytes 4128 | tf_op jit(solution)/shard_map/ppermute | solution.py:495
  25.8 0.0 collective-permute-done.7
  25.8 0.7 %shard_map.55 = (f32[3,17,6,128]{3,2,1,0:T(8,128)}, f32[96,128]{1,0:T(8,128)}) custom-call(f32[51,8,128]{2,1,0:T(8,128)S(1)} %get-tuple-element.26.base, f32[51,8,128]{2,1,0:T(8,128)S(1)} %get-tuple-element.27.second, f32[3,96,128]{2,1,0:T(8,128)S(1)} %shard_map.54.energy, f32[8,128]{1,0:T(8,128)S(1)} %add_add_fusion.sums), custom_call_target="tpu_custom_call" | custom-call | tf_op jit(solution)/shard_map/pallas_call | solution.py:546
  (2 shorter events, 0.0 us)
Async XLA Ops:
  0.6 1.1 %copy-start = (s32[17,6,128]{2,1,0:T(8,128)S(1)}, s32[17,6,128]{2,1,0:T(8,128)}, u32[]{:S(2)}) copy-start(s32[17,6,128]{2,1,0:T(8,128)} %fixed.5) | copy-start | bytes 156676
  0.6 1.1 %copy-start.1 = (s32[16,6,128]{2,0,1:T(8,128)S(1)}, s32[16,6,128]{2,0,1:T(8,128)}, u32[]{:S(2)}) copy-start(s32[16,6,128]{2,0,1:T(8,128)} %param.4) | copy-start | bytes 147460
  2.0 3.8 %collective-permute-start = (f32[2,8,128]{2,1,0:T(8,128)S(1)}, f32[2,8,128]{2,1,0:T(8,128)S(1)}, u32[]{:S(2)}, u32[]{:S(2)}) collective-permute-start(f32[2,8,128]{2,1,0:T(8,128)S(1)} %get-tuple-element.18), channel_id=1, source_target_pairs={{0,3},{1,2},{2,1},{3,0},{4,7},{5,6},{6,5},{7,4},{8,11},{9,10},{10,... | collective-permute-start | bytes 24584 | tf_op jit(solution)/shard_map/ppermute | solution.py:472
  4.4 1.5 %collective-permute-start.1 = (f32[2,8,128]{2,1,0:T(8,128)S(1)}, f32[2,8,128]{2,1,0:T(8,128)S(1)}, u32[]{:S(2)}, u32[]{:S(2)}) collective-permute-start(f32[2,8,128]{2,1,0:T(8,128)S(1)} %get-tuple-element.19), channel_id=1, source_target_pairs={{0,1},{1,0},{2,3},{3,2},{4,5},{5,4},{6,7},{7,6},{8,9},{9,8},{10,11... | collective-permute-start | bytes 24584 | tf_op jit(solution)/shard_map/ppermute | solution.py:473
  6.1 7.0 %collective-permute-start.2 = (f32[144,128]{1,0:T(8,128)S(1)}, f32[144,128]{1,0:T(8,128)S(1)}, u32[]{:S(2)}, u32[]{:S(2)}) collective-permute-start(f32[144,128]{1,0:T(8,128)S(1)} %get-tuple-element.24), channel_id=1, source_target_pairs={{0,4},{4,8},{8,12},{12,0},{1,5},{5,9},{9,13},{13,1},{2,6},{6,10},{... | collective-permute-start | bytes 221192 | tf_op jit(solution)/shard_map/ppermute | solution.py:479
  8.4 5.6 %collective-permute-start.3 = (f32[144,128]{1,0:T(8,128)S(1)}, f32[144,128]{1,0:T(8,128)S(1)}, u32[]{:S(2)}, u32[]{:S(2)}) collective-permute-start(f32[144,128]{1,0:T(8,128)S(1)} %get-tuple-element.25), channel_id=1, source_target_pairs={{4,0},{8,4},{12,8},{0,12},{5,1},{9,5},{13,9},{1,13},{6,2},{10,6},{... | collective-permute-start | bytes 221192 | tf_op jit(solution)/shard_map/ppermute | solution.py:480
  15.3 5.4 %collective-permute-start.6 = (f32[8,128]{1,0:T(8,128)S(1)}, f32[8,128]{1,0:T(8,128)S(1)}, u32[]{:S(2)}, u32[]{:S(2)}) collective-permute-start(f32[8,128]{1,0:T(8,128)S(1)} %get-tuple-element.29), channel_id=1, source_target_pairs={{0,4},{4,8},{8,12},{12,0},{1,5},{5,9},{9,13},{13,1},{2,6},{6,10},{... | collective-permute-start | bytes 12296 | tf_op jit(solution)/shard_map/ppermute | solution.py:495
  16.4 4.5 %collective-permute-start.5 = (f32[8,128]{1,0:T(8,128)S(1)}, f32[8,128]{1,0:T(8,128)S(1)}, u32[]{:S(2)}, u32[]{:S(2)}) collective-permute-start(f32[8,128]{1,0:T(8,128)S(1)} %get-tuple-element.29), channel_id=1, source_target_pairs={{0,8},{4,12},{8,0},{12,4},{1,9},{5,13},{9,1},{13,5},{2,10},{6,14},... | collective-permute-start | bytes 12296 | tf_op jit(solution)/shard_map/ppermute | solution.py:495
  18.5 3.6 %collective-permute-start.4 = (f32[8,128]{1,0:T(8,128)S(1)}, f32[8,128]{1,0:T(8,128)S(1)}, u32[]{:S(2)}, u32[]{:S(2)}) collective-permute-start(f32[8,128]{1,0:T(8,128)S(1)} %get-tuple-element.29), channel_id=1, source_target_pairs={{0,12},{4,0},{8,4},{12,8},{1,13},{5,1},{9,5},{13,9},{2,14},{6,2},{... | collective-permute-start | bytes 12296 | tf_op jit(solution)/shard_map/ppermute | solution.py:495
  22.1 3.0 %collective-permute-start.9 = (f32[8,128]{1,0:T(8,128)S(1)}, f32[8,128]{1,0:T(8,128)S(1)}, u32[]{:S(2)}, u32[]{:S(2)}) collective-permute-start(f32[8,128]{1,0:T(8,128)S(1)} %add_add_fusion.1), channel_id=1, source_target_pairs={{0,3},{1,2},{2,1},{3,0},{4,7},{5,6},{6,5},{7,4},{8,11},{9,10},{10,... | collective-permute-start | bytes 12296 | tf_op jit(solution)/shard_map/ppermute | solution.py:495
  22.1 3.7 %collective-permute-start.8 = (f32[8,128]{1,0:T(8,128)S(1)}, f32[8,128]{1,0:T(8,128)S(1)}, u32[]{:S(2)}, u32[]{:S(2)}) collective-permute-start(f32[8,128]{1,0:T(8,128)S(1)} %add_add_fusion.1), channel_id=1, source_target_pairs={{0,2},{1,3},{2,0},{3,1},{4,6},{5,7},{6,4},{7,5},{8,10},{9,11},{10,... | collective-permute-start | bytes 12296 | tf_op jit(solution)/shard_map/ppermute | solution.py:495
  23.9 1.9 %collective-permute-start.7 = (f32[8,128]{1,0:T(8,128)S(1)}, f32[8,128]{1,0:T(8,128)S(1)}, u32[]{:S(2)}, u32[]{:S(2)}) collective-permute-start(f32[8,128]{1,0:T(8,128)S(1)} %add_add_fusion.1), channel_id=1, source_target_pairs={{0,1},{1,0},{2,3},{3,2},{4,5},{5,4},{6,7},{7,6},{8,9},{9,8},{10,11... | collective-permute-start | bytes 12296 | tf_op jit(solution)/shard_map/ppermute | solution.py:495

commit v8 on v7

--- a/solution.py
+++ b/solution.py
@@ -20,7 +20,6 @@
 DOWN, DOWN_CORNERS = 144, 135
 UP, UP_CORNERS = 144, 83
 
-VMEM = pl.BlockSpec(memory_space=pltpu.VMEM)
 PARAMS = pltpu.CompilerParams(vmem_limit_bytes=32 * 1024 * 1024)
 
 
@@ -302,12 +301,14 @@
         lower.append(plane_modes(x, y, jnp.where(last_row, x_7, roll_up(x)), jnp.where(last_row, y_7, roll_up(y))))
     f_low, f_up = join_layers([strip_scale * x for x in stress(split_layers(lower, strip_layers(lower)))])
     strip_second, strip_sums = [], (0.0,) * 4
+    strip_free = tiles[5] > 0.0
+    free_inv = jnp.where(strip_free, strip_inv, 1.0)
     for c in range(3):
         f = node_forces({m: f_low[c][m] + lane_roll(f_up[c][m], SLOTS) for m in PLANE}, 1)
-        image = jnp.where(tiles[5] > 0.0, f, 0.0)
-        s = jnp.where(tiles[5] > 0.0, f - tiles[c], 0.0)
-        strip_second.append(s * strip_inv)
-        strip_sums = products(strip_sums, strip_base[c], image, image * strip_inv, s, strip_second[c])
+        image = jnp.where(strip_free, f, tiles[c])
+        s = image - tiles[c]
+        strip_second.append(s * free_inv)
+        strip_sums = products(strip_sums, tiles[c] * free_inv, image, image * free_inv, s, strip_second[c])
         edges[c] = strip_base[c]
         edges[3 + c] = strip_second[c]
     ends = [jnp.where(slot == 4, x, lane_roll(x, 4)) for x in strip_second]

time: 26.9 us -> 26.9 us (level)
  no operation moved by 1% of the time
where the time goes in v8:
time: 26.9 us; the launch traced here: 26.6 us
  starting transfers between devices  13.6 us (51%)
  waiting for transfers between devices  7.84 us (29%)
  Pallas kernels  3.31 us (12%)
  other arithmetic  1.05 us (4%)
  between operations  0.7 us (3%)
    ppermute x6, starting transfers between devices, total_over(): lax.ppermute(x, axis, pairs)  6.14 us
    ppermute x6, waiting for transfers between devices, total_over(): lax.ppermute(x, axis, pairs)  3.6 us
    ppermute x1, waiting for transfers between devices, exchange(): low = lax.ppermute(up, axis, [(i, (i + 1) % count) for i in range(count)])  2.64 us
    ppermute x1, starting transfers between devices, exchange_pairs(): lax.ppermute(two, axis, [(i, (i - 1) % count if i % 2 == 0 else (i + 1) %...  2.43 us
    ppermute x1, starting transfers between devices, exchange(): low = lax.ppermute(up, axis, [(i, (i + 1) % count) for i in range(count)])  2.31 us
    ppermute x1, starting transfers between devices, exchange(): lax.ppermute(down, axis, [((i + 1) % count, i) for i in range(count)])  2.09 us
    pallas_call x1, Pallas kernels, body(): call(operator_kernel, (field, field, strips, jax.ShapeDtypeStruct((8, LAN...  1.32 us
    mul x1, other arithmetic, body(): rhs = [(1 - fixed).astype(jnp.float32) * force[c] for c in range(comps)]  1.04 us
  transfers between devices with their start and end apart: 10, of which 9 were waited for; matrix products, arithmetic and copies ran while one was open for 0% of the time, Pallas kernels for 3%

profile of v8, /device:TPU:0, one launch (start us, length us, event | category | flops | bytes accessed | tf_op | source)
XLA Modules:
  0.0 26.6 jit_solution(16227014975502940813)
XLA Ops:
  0.6 0.0 copy-start
  0.6 0.0 copy-start.1
  0.6 1.0 %bitcast_multiply_fusion = (f32[17,6,128]{2,1,0:T(8,128)S(1)}, f32[17,6,128]{2,1,0:T(8,128)S(1)}, f32[17,6,128]{2,1,0:T(8,128)S(1)}) fusion(f32[3,17,6,128]{3,2,1,0:T(8,128)} %param.3, s32[17,6,128]{2,1,0:T(8,128)} %fixed.5), kind=kLoop, calls=%fused_computation | loop fusion | flops 65280 | bytes 365568 | tf_op jit(solution)/shard_map/mul | solution.py:505
  1.7 0.0 copy-done
  1.7 0.0 copy-done.1
  1.7 0.2 shard_map.50
  2.0 2.4 %collective-permute-start = (f32[2,8,128]{2,1,0:T(8,128)S(1)}, f32[2,8,128]{2,1,0:T(8,128)S(1)}, u32[]{:S(2)}, u32[]{:S(2)}) collective-permute-start(f32[2,8,128]{2,1,0:T(8,128)S(1)} %get-tuple-element.18), channel_id=1, source_target_pairs={{0,3},{1,2},{2,1},{3,0},{4,7},{5,6},{6,5},{7,4},{8,11},{9,10},{10,... | collective-permute-start | bytes 24584 | tf_op jit(solution)/shard_map/ppermute | solution.py:473
  4.4 0.7 %collective-permute-start.1 = (f32[2,8,128]{2,1,0:T(8,128)S(1)}, f32[2,8,128]{2,1,0:T(8,128)S(1)}, u32[]{:S(2)}, u32[]{:S(2)}) collective-permute-start(f32[2,8,128]{2,1,0:T(8,128)S(1)} %get-tuple-element.19), channel_id=1, source_target_pairs={{0,1},{1,0},{2,3},{3,2},{4,5},{5,4},{6,7},{7,6},{8,9},{9,8},{10,11... | collective-permute-start | bytes 24584 | tf_op jit(solution)/shard_map/ppermute | solution.py:474
  5.1 0.1 shard_map.51
  5.1 0.6 %collective-permute-done.got2 = f32[2,8,128]{2,1,0:T(8,128)S(1)} collective-permute-done((f32[2,8,128]{2,1,0:T(8,128)S(1)}, f32[2,8,128]{2,1,0:T(8,128)S(1)}, u32[]{:S(2)}, u32[]{:S(2)}) %collective-permute-start) | collective-permute-done | bytes 8224 | tf_op jit(solution)/shard_map/ppermute | solution.py:473
  5.7 0.1 collective-permute-done.1.got1
  5.9 0.2 shard_map.52
  6.1 2.3 %collective-permute-start.2 = (f32[144,128]{1,0:T(8,128)S(1)}, f32[144,128]{1,0:T(8,128)S(1)}, u32[]{:S(2)}, u32[]{:S(2)}) collective-permute-start(f32[144,128]{1,0:T(8,128)S(1)} %get-tuple-element.24), channel_id=1, source_target_pairs={{0,4},{4,8},{8,12},{12,0},{1,5},{5,9},{9,13},{13,1},{2,6},{6,10},{... | collective-permute-start | bytes 221192 | tf_op jit(solution)/shard_map/ppermute | solution.py:480
  8.4 2.1 %collective-permute-start.3 = (f32[144,128]{1,0:T(8,128)S(1)}, f32[144,128]{1,0:T(8,128)S(1)}, u32[]{:S(2)}, u32[]{:S(2)}) collective-permute-start(f32[144,128]{1,0:T(8,128)S(1)} %get-tuple-element.25), channel_id=1, source_target_pairs={{4,0},{8,4},{12,8},{0,12},{5,1},{9,5},{13,9},{1,13},{6,2},{10,6},{... | collective-permute-start | bytes 221192 | tf_op jit(solution)/shard_map/ppermute | solution.py:481
  10.5 2.6 %collective-permute-done.2.lo = f32[144,128]{1,0:T(8,128)S(1)} collective-permute-done((f32[144,128]{1,0:T(8,128)S(1)}, f32[144,128]{1,0:T(8,128)S(1)}, u32[]{:S(2)}, u32[]{:S(2)}) %collective-permute-start.2) | collective-permute-done | bytes 73760 | tf_op jit(solution)/shard_map/ppermute | solution.py:480
  13.1 0.9 %collective-permute-done.3.hi = f32[144,128]{1,0:T(8,128)S(1)} collective-permute-done((f32[144,128]{1,0:T(8,128)S(1)}, f32[144,128]{1,0:T(8,128)S(1)}, u32[]{:S(2)}, u32[]{:S(2)}) %collective-permute-start.3) | collective-permute-done | bytes 73760 | tf_op jit(solution)/shard_map/ppermute | solution.py:481
  14.0 1.3 %shard_map.53 = (f32[51,8,128]{2,1,0:T(8,128)S(1)}, f32[51,8,128]{2,1,0:T(8,128)S(1)}, f32[6,8,128]{2,1,0:T(8,128)S(1)}, f32[8,128]{1,0:T(8,128)S(1)}) custom-call(f32[17,6,128]{2,1,0:T(8,128)S(1)} %get-tuple-element.33.rhs_0, f32[17,6,128]{2,1,0:T(8,128)S(1)} %get-tuple-element.34.rhs_1, f32[17,6,128]{2,1,0:T(8,128)S(1)} %get-tuple-element.32.rhs_2, ...), custom_call_target="tpu_custom_call" | custom-call | tf_op jit(solution)/shard_map/pallas_call | solution.py:529
  15.3 1.1 %collective-permute-start.6 = (f32[8,128]{1,0:T(8,128)S(1)}, f32[8,128]{1,0:T(8,128)S(1)}, u32[]{:S(2)}, u32[]{:S(2)}) collective-permute-start(f32[8,128]{1,0:T(8,128)S(1)} %get-tuple-element.29), channel_id=1, source_target_pairs={{0,4},{4,8},{8,12},{12,0},{1,5},{5,9},{9,13},{13,1},{2,6},{6,10},{... | collective-permute-start | bytes 12296 | tf_op jit(solution)/shard_map/ppermute | solution.py:496
  16.4 2.1 %collective-permute-start.5 = (f32[8,128]{1,0:T(8,128)S(1)}, f32[8,128]{1,0:T(8,128)S(1)}, u32[]{:S(2)}, u32[]{:S(2)}) collective-permute-start(f32[8,128]{1,0:T(8,128)S(1)} %get-tuple-element.29), channel_id=1, source_target_pairs={{0,8},{4,12},{8,0},{12,4},{1,9},{5,13},{9,1},{13,5},{2,10},{6,14},... | collective-permute-start | bytes 12296 | tf_op jit(solution)/shard_map/ppermute | solution.py:496
  18.5 1.1 %collective-permute-start.4 = (f32[8,128]{1,0:T(8,128)S(1)}, f32[8,128]{1,0:T(8,128)S(1)}, u32[]{:S(2)}, u32[]{:S(2)}) collective-permute-start(f32[8,128]{1,0:T(8,128)S(1)} %get-tuple-element.29), channel_id=1, source_target_pairs={{0,12},{4,0},{8,4},{12,8},{1,13},{5,1},{9,5},{13,9},{2,14},{6,2},{... | collective-permute-start | bytes 12296 | tf_op jit(solution)/shard_map/ppermute | solution.py:496
  19.6 1.1 %collective-permute-done.6 = f32[8,128]{1,0:T(8,128)S(1)} collective-permute-done((f32[8,128]{1,0:T(8,128)S(1)}, f32[8,128]{1,0:T(8,128)S(1)}, u32[]{:S(2)}, u32[]{:S(2)}) %collective-permute-start.6) | collective-permute-done | bytes 4128 | tf_op jit(solution)/shard_map/ppermute | solution.py:496
  20.7 0.2 collective-permute-done.5
  20.9 1.2 %collective-permute-done.4 = f32[8,128]{1,0:T(8,128)S(1)} collective-permute-done((f32[8,128]{1,0:T(8,128)S(1)}, f32[8,128]{1,0:T(8,128)S(1)}, u32[]{:S(2)}, u32[]{:S(2)}) %collective-permute-start.4) | collective-permute-done | bytes 4128 | tf_op jit(solution)/shard_map/ppermute | solution.py:496
  22.1 0.0 collective-permute-start.9
  22.1 1.8 %collective-permute-start.8 = (f32[8,128]{1,0:T(8,128)S(1)}, f32[8,128]{1,0:T(8,128)S(1)}, u32[]{:S(2)}, u32[]{:S(2)}) collective-permute-start(f32[8,128]{1,0:T(8,128)S(1)} %add_add_fusion.1), channel_id=1, source_target_pairs={{0,2},{1,3},{2,0},{3,1},{4,6},{5,7},{6,4},{7,5},{8,10},{9,11},{10,... | collective-permute-start | bytes 12296 | tf_op jit(solution)/shard_map/ppermute | solution.py:496
  23.9 0.1 collective-permute-start.7
  24.0 0.8 %shard_map.54.energy = f32[3,96,128]{2,1,0:T(8,128)S(1)} custom-call(f32[51,8,128]{2,1,0:T(8,128)S(1)} %get-tuple-element.26.base, f32[51,8,128]{2,1,0:T(8,128)S(1)} %get-tuple-element.27.second, f32[6,8,128]{2,1,0:T(8,128)S(1)} %get-tuple-element.28.edges, s32[96,128]{1,0:T(8,128)S(1)} %bitcast.15), custom_call_target="tpu_custom_call" | custom-call | tf_op jit(solution)/shard_map/pallas_call | solution.py:545
  24.8 0.4 %collective-permute-done.9 = f32[8,128]{1,0:T(8,128)S(1)} collective-permute-done((f32[8,128]{1,0:T(8,128)S(1)}, f32[8,128]{1,0:T(8,128)S(1)}, u32[]{:S(2)}, u32[]{:S(2)}) %collective-permute-start.9) | collective-permute-done | bytes 4128 | tf_op jit(solution)/shard_map/ppermute | solution.py:496
  25.2 0.6 %collective-permute-done.8 = f32[8,128]{1,0:T(8,128)S(1)} collective-permute-done((f32[8,128]{1,0:T(8,128)S(1)}, f32[8,128]{1,0:T(8,128)S(1)}, u32[]{:S(2)}, u32[]{:S(2)}) %collective-permute-start.8) | collective-permute-done | bytes 4128 | tf_op jit(solution)/shard_map/ppermute | solution.py:496
  25.8 0.0 collective-permute-done.7
  25.8 0.7 %shard_map.55 = (f32[3,17,6,128]{3,2,1,0:T(8,128)}, f32[96,128]{1,0:T(8,128)}) custom-call(f32[51,8,128]{2,1,0:T(8,128)S(1)} %get-tuple-element.26.base, f32[51,8,128]{2,1,0:T(8,128)S(1)} %get-tuple-element.27.second, f32[3,96,128]{2,1,0:T(8,128)S(1)} %shard_map.54.energy, f32[8,128]{1,0:T(8,128)S(1)} %add_add_fusion.sums), custom_call_target="tpu_custom_call" | custom-call | tf_op jit(solution)/shard_map/pallas_call | solution.py:547
  (2 shorter events, 0.0 us)
Async XLA Ops:
  0.6 1.1 %copy-start = (s32[17,6,128]{2,1,0:T(8,128)S(1)}, s32[17,6,128]{2,1,0:T(8,128)}, u32[]{:S(2)}) copy-start(s32[17,6,128]{2,1,0:T(8,128)} %fixed.5) | copy-start | bytes 156676
  0.6 1.1 %copy-start.1 = (s32[16,6,128]{2,0,1:T(8,128)S(1)}, s32[16,6,128]{2,0,1:T(8,128)}, u32[]{:S(2)}) copy-start(s32[16,6,128]{2,0,1:T(8,128)} %param.4) | copy-start | bytes 147460
  2.0 3.8 %collective-permute-start = (f32[2,8,128]{2,1,0:T(8,128)S(1)}, f32[2,8,128]{2,1,0:T(8,128)S(1)}, u32[]{:S(2)}, u32[]{:S(2)}) collective-permute-start(f32[2,8,128]{2,1,0:T(8,128)S(1)} %get-tuple-element.18), channel_id=1, source_target_pairs={{0,3},{1,2},{2,1},{3,0},{4,7},{5,6},{6,5},{7,4},{8,11},{9,10},{10,... | collective-permute-start | bytes 24584 | tf_op jit(solution)/shard_map/ppermute | solution.py:473
  4.4 1.5 %collective-permute-start.1 = (f32[2,8,128]{2,1,0:T(8,128)S(1)}, f32[2,8,128]{2,1,0:T(8,128)S(1)}, u32[]{:S(2)}, u32[]{:S(2)}) collective-permute-start(f32[2,8,128]{2,1,0:T(8,128)S(1)} %get-tuple-element.19), channel_id=1, source_target_pairs={{0,1},{1,0},{2,3},{3,2},{4,5},{5,4},{6,7},{7,6},{8,9},{9,8},{10,11... | collective-permute-start | bytes 24584 | tf_op jit(solution)/shard_map/ppermute | solution.py:474
  6.1 7.0 %collective-permute-start.2 = (f32[144,128]{1,0:T(8,128)S(1)}, f32[144,128]{1,0:T(8,128)S(1)}, u32[]{:S(2)}, u32[]{:S(2)}) collective-permute-start(f32[144,128]{1,0:T(8,128)S(1)} %get-tuple-element.24), channel_id=1, source_target_pairs={{0,4},{4,8},{8,12},{12,0},{1,5},{5,9},{9,13},{13,1},{2,6},{6,10},{... | collective-permute-start | bytes 221192 | tf_op jit(solution)/shard_map/ppermute | solution.py:480
  8.4 5.6 %collective-permute-start.3 = (f32[144,128]{1,0:T(8,128)S(1)}, f32[144,128]{1,0:T(8,128)S(1)}, u32[]{:S(2)}, u32[]{:S(2)}) collective-permute-start(f32[144,128]{1,0:T(8,128)S(1)} %get-tuple-element.25), channel_id=1, source_target_pairs={{4,0},{8,4},{12,8},{0,12},{5,1},{9,5},{13,9},{1,13},{6,2},{10,6},{... | collective-permute-start | bytes 221192 | tf_op jit(solution)/shard_map/ppermute | solution.py:481
  15.3 5.4 %collective-permute-start.6 = (f32[8,128]{1,0:T(8,128)S(1)}, f32[8,128]{1,0:T(8,128)S(1)}, u32[]{:S(2)}, u32[]{:S(2)}) collective-permute-start(f32[8,128]{1,0:T(8,128)S(1)} %get-tuple-element.29), channel_id=1, source_target_pairs={{0,4},{4,8},{8,12},{12,0},{1,5},{5,9},{9,13},{13,1},{2,6},{6,10},{... | collective-permute-start | bytes 12296 | tf_op jit(solution)/shard_map/ppermute | solution.py:496
  16.4 4.5 %collective-permute-start.5 = (f32[8,128]{1,0:T(8,128)S(1)}, f32[8,128]{1,0:T(8,128)S(1)}, u32[]{:S(2)}, u32[]{:S(2)}) collective-permute-start(f32[8,128]{1,0:T(8,128)S(1)} %get-tuple-element.29), channel_id=1, source_target_pairs={{0,8},{4,12},{8,0},{12,4},{1,9},{5,13},{9,1},{13,5},{2,10},{6,14},... | collective-permute-start | bytes 12296 | tf_op jit(solution)/shard_map/ppermute | solution.py:496
  18.5 3.6 %collective-permute-start.4 = (f32[8,128]{1,0:T(8,128)S(1)}, f32[8,128]{1,0:T(8,128)S(1)}, u32[]{:S(2)}, u32[]{:S(2)}) collective-permute-start(f32[8,128]{1,0:T(8,128)S(1)} %get-tuple-element.29), channel_id=1, source_target_pairs={{0,12},{4,0},{8,4},{12,8},{1,13},{5,1},{9,5},{13,9},{2,14},{6,2},{... | collective-permute-start | bytes 12296 | tf_op jit(solution)/shard_map/ppermute | solution.py:496
  22.1 3.0 %collective-permute-start.9 = (f32[8,128]{1,0:T(8,128)S(1)}, f32[8,128]{1,0:T(8,128)S(1)}, u32[]{:S(2)}, u32[]{:S(2)}) collective-permute-start(f32[8,128]{1,0:T(8,128)S(1)} %add_add_fusion.1), channel_id=1, source_target_pairs={{0,3},{1,2},{2,1},{3,0},{4,7},{5,6},{6,5},{7,4},{8,11},{9,10},{10,... | collective-permute-start | bytes 12296 | tf_op jit(solution)/shard_map/ppermute | solution.py:496
  22.1 3.7 %collective-permute-start.8 = (f32[8,128]{1,0:T(8,128)S(1)}, f32[8,128]{1,0:T(8,128)S(1)}, u32[]{:S(2)}, u32[]{:S(2)}) collective-permute-start(f32[8,128]{1,0:T(8,128)S(1)} %add_add_fusion.1), channel_id=1, source_target_pairs={{0,2},{1,3},{2,0},{3,1},{4,6},{5,7},{6,4},{7,5},{8,10},{9,11},{10,... | collective-permute-start | bytes 12296 | tf_op jit(solution)/shard_map/ppermute | solution.py:496
  23.9 1.9 %collective-permute-start.7 = (f32[8,128]{1,0:T(8,128)S(1)}, f32[8,128]{1,0:T(8,128)S(1)}, u32[]{:S(2)}, u32[]{:S(2)}) collective-permute-start(f32[8,128]{1,0:T(8,128)S(1)} %add_add_fusion.1), channel_id=1, source_target_pairs={{0,1},{1,0},{2,3},{3,2},{4,5},{5,4},{6,7},{7,6},{8,9},{9,8},{10,11... | collective-permute-start | bytes 12296 | tf_op jit(solution)/shard_map/ppermute | solution.py:496

commit v9 on v8

--- a/solution.py
+++ b/solution.py
@@ -120,7 +120,7 @@
     up[UP_CORNERS:, :] = jnp.zeros((UP - UP_CORNERS, LANES), jnp.float32)
 
 
-def strip_kernel(nodes, paired, own, got2, got1, down, up, pair, strip, down_out, up_out, dense):
+def strip_kernel(nodes, paired, own, got2, got1, up, strip, up_out):
     even_y = is_even("gy") if paired else True
     if paired:
         from_low = jnp.where(even_y, got2[0], got1[0])
@@ -136,11 +136,15 @@
     planes.append(gather(nodes, (from_low, -4, 0, 1), (scale, -2, 1, 2), (scale, 2, 3, 2), (from_high[1], 2, 5, 2)))
     planes.append(gather(nodes, (own[4], -2, 1, 1), (own[4], 2, 4, 1), (from_high[0], -1, 5, 1)))
     rows = 6
-    down_out[...] = down[...]
     up_out[...] = up[...]
     for p, plane in enumerate(planes):
         strip[p] = plane
         up_out[UP_CORNERS + 2 * p : UP_CORNERS + 2 * p + 2, :] = plane[rows - 2 : rows]
+
+
+def lower_kernel(nodes, strip, down, pair, down_out, dense):
+    planes = [strip[p] for p in range(6)]
+    down_out[...] = down[...]
     around = planes[3] + planes[4]
     around = around + pltpu.roll(around, 1, 0)
     around = KE_DIAGONAL * (around + lane_roll(around, SLOTS))
@@ -519,11 +523,12 @@
     )(*rhs, phase, fixed)
     down, up, pair = call(row_kernel, messages + (jax.ShapeDtypeStruct((layers, LANES), f32),))(*rhs, phase, fixed)
     near, far = (exchange_pairs if paired else exchange)(col1, col2, "gy")
-    strip, down, up = call(
-        functools.partial(strip_kernel, nodes, paired),
-        (strips,) + messages,
+    strip, up = call(functools.partial(strip_kernel, nodes, paired), (strips, messages[1]))(own, far, near, up)
+    down = call(
+        functools.partial(lower_kernel, nodes),
+        messages[0],
         [pltpu.VMEM((32, LANES), f32)],
-    )(own, far, near, down, up, pair)
+    )(strip, down, pair)
     high, low = exchange(down, up, "gx")
     field = jax.ShapeDtypeStruct((comps * nodes, 8, LANES), f32)
     base, second, edges, sums = call(

time: 26.9 us -> 26.9 us (level)
  no operation moved by 1% of the time
where the time goes in v9:
time: 26.9 us; the launch traced here: 26.6 us
  starting transfers between devices  13.7 us (51%)
  waiting for transfers between devices  7.82 us (29%)
  Pallas kernels  3.32 us (12%)
  other arithmetic  1.05 us (4%)
  between operations  0.7 us (3%)
    ppermute x6, starting transfers between devices, total_over(): lax.ppermute(x, axis, pairs)  6.16 us
    ppermute x6, waiting for transfers between devices, total_over(): lax.ppermute(x, axis, pairs)  3.53 us
    ppermute x1, waiting for transfers between devices, exchange(): low = lax.ppermute(up, axis, [(i, (i + 1) % count) for i in range(count)])  2.53 us
    ppermute x1, starting transfers between devices, exchange_pairs(): lax.ppermute(two, axis, [(i, (i - 1) % count if i % 2 == 0 else (i + 1) %...  2.43 us
    ppermute x1, starting transfers between devices, exchange(): low = lax.ppermute(up, axis, [(i, (i + 1) % count) for i in range(count)])  2.31 us
    ppermute x1, starting transfers between devices, exchange(): lax.ppermute(down, axis, [((i + 1) % count, i) for i in range(count)])  2.09 us
    pallas_call x1, Pallas kernels, body(): call(operator_kernel, (field, field, strips, jax.ShapeDtypeStruct((8, LAN...  1.31 us
    mul x1, other arithmetic, body(): rhs = [(1 - fixed).astype(jnp.float32) * force[c] for c in range(comps)]  1.04 us
  transfers between devices with their start and end apart: 10, of which 9 were waited for; matrix products, arithmetic and copies ran while one was open for 0% of the time, Pallas kernels for 3%

profile of v9, /device:TPU:0, one launch (start us, length us, event | category | flops | bytes accessed | tf_op | source)
XLA Modules:
  0.0 26.6 jit_solution(10528476265699959987)
XLA Ops:
  0.6 0.0 copy-start
  0.6 0.0 copy-start.1
  0.6 1.0 %bitcast_multiply_fusion = (f32[17,6,128]{2,1,0:T(8,128)S(1)}, f32[17,6,128]{2,1,0:T(8,128)S(1)}, f32[17,6,128]{2,1,0:T(8,128)S(1)}) fusion(f32[3,17,6,128]{3,2,1,0:T(8,128)} %param.3, s32[17,6,128]{2,1,0:T(8,128)} %fixed.5), kind=kLoop, calls=%fused_computation | loop fusion | flops 65280 | bytes 365568 | tf_op jit(solution)/shard_map/mul | solution.py:509
  1.7 0.0 copy-done
  1.7 0.0 copy-done.1
  1.7 0.2 shard_map.50
  2.0 2.4 %collective-permute-start = (f32[2,8,128]{2,1,0:T(8,128)S(1)}, f32[2,8,128]{2,1,0:T(8,128)S(1)}, u32[]{:S(2)}, u32[]{:S(2)}) collective-permute-start(f32[2,8,128]{2,1,0:T(8,128)S(1)} %get-tuple-element.17), channel_id=1, source_target_pairs={{0,3},{1,2},{2,1},{3,0},{4,7},{5,6},{6,5},{7,4},{8,11},{9,10},{10,... | collective-permute-start | bytes 24584 | tf_op jit(solution)/shard_map/ppermute | solution.py:477
  4.4 0.7 %collective-permute-start.1 = (f32[2,8,128]{2,1,0:T(8,128)S(1)}, f32[2,8,128]{2,1,0:T(8,128)S(1)}, u32[]{:S(2)}, u32[]{:S(2)}) collective-permute-start(f32[2,8,128]{2,1,0:T(8,128)S(1)} %get-tuple-element.18), channel_id=1, source_target_pairs={{0,1},{1,0},{2,3},{3,2},{4,5},{5,4},{6,7},{7,6},{8,9},{9,8},{10,11... | collective-permute-start | bytes 24584 | tf_op jit(solution)/shard_map/ppermute | solution.py:478
  5.1 0.1 shard_map.51
  5.1 0.6 %collective-permute-done.got2 = f32[2,8,128]{2,1,0:T(8,128)S(1)} collective-permute-done((f32[2,8,128]{2,1,0:T(8,128)S(1)}, f32[2,8,128]{2,1,0:T(8,128)S(1)}, u32[]{:S(2)}, u32[]{:S(2)}) %collective-permute-start) | collective-permute-done | bytes 8224 | tf_op jit(solution)/shard_map/ppermute | solution.py:477
  5.7 0.1 collective-permute-done.1.got1
  5.9 0.1 shard_map.52
  6.0 2.3 %collective-permute-start.2 = (f32[144,128]{1,0:T(8,128)S(1)}, f32[144,128]{1,0:T(8,128)S(1)}, u32[]{:S(2)}, u32[]{:S(2)}) collective-permute-start(f32[144,128]{1,0:T(8,128)S(1)} %get-tuple-element.21), channel_id=1, source_target_pairs={{0,4},{4,8},{8,12},{12,0},{1,5},{5,9},{9,13},{13,1},{2,6},{6,10},{... | collective-permute-start | bytes 221192 | tf_op jit(solution)/shard_map/ppermute | solution.py:484
  8.3 0.1 shard_map.53
  8.4 2.1 %collective-permute-start.3 = (f32[144,128]{1,0:T(8,128)S(1)}, f32[144,128]{1,0:T(8,128)S(1)}, u32[]{:S(2)}, u32[]{:S(2)}) collective-permute-start(f32[144,128]{1,0:T(8,128)S(1)} %shard_map.53), channel_id=1, source_target_pairs={{4,0},{8,4},{12,8},{0,12},{5,1},{9,5},{13,9},{1,13},{6,2},{10,6},{... | collective-permute-start | bytes 221192 | tf_op jit(solution)/shard_map/ppermute | solution.py:485
  10.5 2.5 %collective-permute-done.2.lo = f32[144,128]{1,0:T(8,128)S(1)} collective-permute-done((f32[144,128]{1,0:T(8,128)S(1)}, f32[144,128]{1,0:T(8,128)S(1)}, u32[]{:S(2)}, u32[]{:S(2)}) %collective-permute-start.2) | collective-permute-done | bytes 73760 | tf_op jit(solution)/shard_map/ppermute | solution.py:484
  13.0 1.0 %collective-permute-done.3.hi = f32[144,128]{1,0:T(8,128)S(1)} collective-permute-done((f32[144,128]{1,0:T(8,128)S(1)}, f32[144,128]{1,0:T(8,128)S(1)}, u32[]{:S(2)}, u32[]{:S(2)}) %collective-permute-start.3) | collective-permute-done | bytes 73760 | tf_op jit(solution)/shard_map/ppermute | solution.py:485
  14.0 1.3 %shard_map.54 = (f32[51,8,128]{2,1,0:T(8,128)S(1)}, f32[51,8,128]{2,1,0:T(8,128)S(1)}, f32[6,8,128]{2,1,0:T(8,128)S(1)}, f32[8,128]{1,0:T(8,128)S(1)}) custom-call(f32[17,6,128]{2,1,0:T(8,128)S(1)} %get-tuple-element.31.rhs_0, f32[17,6,128]{2,1,0:T(8,128)S(1)} %get-tuple-element.32.rhs_1, f32[17,6,128]{2,1,0:T(8,128)S(1)} %get-tuple-element.30.rhs_2, ...), custom_call_target="tpu_custom_call" | custom-call | tf_op jit(solution)/shard_map/pallas_call | solution.py:534
  15.4 1.0 %collective-permute-start.6 = (f32[8,128]{1,0:T(8,128)S(1)}, f32[8,128]{1,0:T(8,128)S(1)}, u32[]{:S(2)}, u32[]{:S(2)}) collective-permute-start(f32[8,128]{1,0:T(8,128)S(1)} %get-tuple-element.27), channel_id=1, source_target_pairs={{0,4},{4,8},{8,12},{12,0},{1,5},{5,9},{9,13},{13,1},{2,6},{6,10},{... | collective-permute-start | bytes 12296 | tf_op jit(solution)/shard_map/ppermute | solution.py:500
  16.3 2.2 %collective-permute-start.5 = (f32[8,128]{1,0:T(8,128)S(1)}, f32[8,128]{1,0:T(8,128)S(1)}, u32[]{:S(2)}, u32[]{:S(2)}) collective-permute-start(f32[8,128]{1,0:T(8,128)S(1)} %get-tuple-element.27), channel_id=1, source_target_pairs={{0,8},{4,12},{8,0},{12,4},{1,9},{5,13},{9,1},{13,5},{2,10},{6,14},... | collective-permute-start | bytes 12296 | tf_op jit(solution)/shard_map/ppermute | solution.py:500
  18.5 1.1 %collective-permute-start.4 = (f32[8,128]{1,0:T(8,128)S(1)}, f32[8,128]{1,0:T(8,128)S(1)}, u32[]{:S(2)}, u32[]{:S(2)}) collective-permute-start(f32[8,128]{1,0:T(8,128)S(1)} %get-tuple-element.27), channel_id=1, source_target_pairs={{0,12},{4,0},{8,4},{12,8},{1,13},{5,1},{9,5},{13,9},{2,14},{6,2},{... | collective-permute-start | bytes 12296 | tf_op jit(solution)/shard_map/ppermute | solution.py:500
  19.6 1.1 %collective-permute-done.6 = f32[8,128]{1,0:T(8,128)S(1)} collective-permute-done((f32[8,128]{1,0:T(8,128)S(1)}, f32[8,128]{1,0:T(8,128)S(1)}, u32[]{:S(2)}, u32[]{:S(2)}) %collective-permute-start.6) | collective-permute-done | bytes 4128 | tf_op jit(solution)/shard_map/ppermute | solution.py:500
  20.8 0.1 collective-permute-done.5
  20.9 1.3 %collective-permute-done.4 = f32[8,128]{1,0:T(8,128)S(1)} collective-permute-done((f32[8,128]{1,0:T(8,128)S(1)}, f32[8,128]{1,0:T(8,128)S(1)}, u32[]{:S(2)}, u32[]{:S(2)}) %collective-permute-start.4) | collective-permute-done | bytes 4128 | tf_op jit(solution)/shard_map/ppermute | solution.py:500
  22.1 0.0 collective-permute-start.9
  22.1 1.8 %collective-permute-start.8 = (f32[8,128]{1,0:T(8,128)S(1)}, f32[8,128]{1,0:T(8,128)S(1)}, u32[]{:S(2)}, u32[]{:S(2)}) collective-permute-start(f32[8,128]{1,0:T(8,128)S(1)} %add_add_fusion.1), channel_id=1, source_target_pairs={{0,2},{1,3},{2,0},{3,1},{4,6},{5,7},{6,4},{7,5},{8,10},{9,11},{10,... | collective-permute-start | bytes 12296 | tf_op jit(solution)/shard_map/ppermute | solution.py:500
  23.9 0.1 collective-permute-start.7
  24.0 0.8 %shard_map.55.energy = f32[3,96,128]{2,1,0:T(8,128)S(1)} custom-call(f32[51,8,128]{2,1,0:T(8,128)S(1)} %get-tuple-element.24.base, f32[51,8,128]{2,1,0:T(8,128)S(1)} %get-tuple-element.25.second, f32[6,8,128]{2,1,0:T(8,128)S(1)} %get-tuple-element.26.edges, s32[96,128]{1,0:T(8,128)S(1)} %bitcast.15), custom_call_target="tpu_custom_call" | custom-call | tf_op jit(solution)/shard_map/pallas_call | solution.py:550
  24.8 0.4 %collective-permute-done.9 = f32[8,128]{1,0:T(8,128)S(1)} collective-permute-done((f32[8,128]{1,0:T(8,128)S(1)}, f32[8,128]{1,0:T(8,128)S(1)}, u32[]{:S(2)}, u32[]{:S(2)}) %collective-permute-start.9) | collective-permute-done | bytes 4128 | tf_op jit(solution)/shard_map/ppermute | solution.py:500
  25.2 0.6 %collective-permute-done.8 = f32[8,128]{1,0:T(8,128)S(1)} collective-permute-done((f32[8,128]{1,0:T(8,128)S(1)}, f32[8,128]{1,0:T(8,128)S(1)}, u32[]{:S(2)}, u32[]{:S(2)}) %collective-permute-start.8) | collective-permute-done | bytes 4128 | tf_op jit(solution)/shard_map/ppermute | solution.py:500
  25.8 0.0 collective-permute-done.7
  25.8 0.7 %shard_map.56 = (f32[3,17,6,128]{3,2,1,0:T(8,128)}, f32[96,128]{1,0:T(8,128)}) custom-call(f32[51,8,128]{2,1,0:T(8,128)S(1)} %get-tuple-element.24.base, f32[51,8,128]{2,1,0:T(8,128)S(1)} %get-tuple-element.25.second, f32[3,96,128]{2,1,0:T(8,128)S(1)} %shard_map.55.energy, f32[8,128]{1,0:T(8,128)S(1)} %add_add_fusion.sums), custom_call_target="tpu_custom_call" | custom-call | tf_op jit(solution)/shard_map/pallas_call | solution.py:552
  (2 shorter events, 0.0 us)
Async XLA Ops:
  0.6 1.1 %copy-start = (s32[17,6,128]{2,1,0:T(8,128)S(1)}, s32[17,6,128]{2,1,0:T(8,128)}, u32[]{:S(2)}) copy-start(s32[17,6,128]{2,1,0:T(8,128)} %fixed.5) | copy-start | bytes 156676
  0.6 1.1 %copy-start.1 = (s32[16,6,128]{2,0,1:T(8,128)S(1)}, s32[16,6,128]{2,0,1:T(8,128)}, u32[]{:S(2)}) copy-start(s32[16,6,128]{2,0,1:T(8,128)} %param.4) | copy-start | bytes 147460
  2.0 3.8 %collective-permute-start = (f32[2,8,128]{2,1,0:T(8,128)S(1)}, f32[2,8,128]{2,1,0:T(8,128)S(1)}, u32[]{:S(2)}, u32[]{:S(2)}) collective-permute-start(f32[2,8,128]{2,1,0:T(8,128)S(1)} %get-tuple-element.17), channel_id=1, source_target_pairs={{0,3},{1,2},{2,1},{3,0},{4,7},{5,6},{6,5},{7,4},{8,11},{9,10},{10,... | collective-permute-start | bytes 24584 | tf_op jit(solution)/shard_map/ppermute | solution.py:477
  4.4 1.5 %collective-permute-start.1 = (f32[2,8,128]{2,1,0:T(8,128)S(1)}, f32[2,8,128]{2,1,0:T(8,128)S(1)}, u32[]{:S(2)}, u32[]{:S(2)}) collective-permute-start(f32[2,8,128]{2,1,0:T(8,128)S(1)} %get-tuple-element.18), channel_id=1, source_target_pairs={{0,1},{1,0},{2,3},{3,2},{4,5},{5,4},{6,7},{7,6},{8,9},{9,8},{10,11... | collective-permute-start | bytes 24584 | tf_op jit(solution)/shard_map/ppermute | solution.py:478
  6.0 7.0 %collective-permute-start.2 = (f32[144,128]{1,0:T(8,128)S(1)}, f32[144,128]{1,0:T(8,128)S(1)}, u32[]{:S(2)}, u32[]{:S(2)}) collective-permute-start(f32[144,128]{1,0:T(8,128)S(1)} %get-tuple-element.21), channel_id=1, source_target_pairs={{0,4},{4,8},{8,12},{12,0},{1,5},{5,9},{9,13},{13,1},{2,6},{6,10},{... | collective-permute-start | bytes 221192 | tf_op jit(solution)/shard_map/ppermute | solution.py:484
  8.4 5.6 %collective-permute-start.3 = (f32[144,128]{1,0:T(8,128)S(1)}, f32[144,128]{1,0:T(8,128)S(1)}, u32[]{:S(2)}, u32[]{:S(2)}) collective-permute-start(f32[144,128]{1,0:T(8,128)S(1)} %shard_map.53), channel_id=1, source_target_pairs={{4,0},{8,4},{12,8},{0,12},{5,1},{9,5},{13,9},{1,13},{6,2},{10,6},{... | collective-permute-start | bytes 221192 | tf_op jit(solution)/shard_map/ppermute | solution.py:485
  15.4 5.4 %collective-permute-start.6 = (f32[8,128]{1,0:T(8,128)S(1)}, f32[8,128]{1,0:T(8,128)S(1)}, u32[]{:S(2)}, u32[]{:S(2)}) collective-permute-start(f32[8,128]{1,0:T(8,128)S(1)} %get-tuple-element.27), channel_id=1, source_target_pairs={{0,4},{4,8},{8,12},{12,0},{1,5},{5,9},{9,13},{13,1},{2,6},{6,10},{... | collective-permute-start | bytes 12296 | tf_op jit(solution)/shard_map/ppermute | solution.py:500
  16.3 4.5 %collective-permute-start.5 = (f32[8,128]{1,0:T(8,128)S(1)}, f32[8,128]{1,0:T(8,128)S(1)}, u32[]{:S(2)}, u32[]{:S(2)}) collective-permute-start(f32[8,128]{1,0:T(8,128)S(1)} %get-tuple-element.27), channel_id=1, source_target_pairs={{0,8},{4,12},{8,0},{12,4},{1,9},{5,13},{9,1},{13,5},{2,10},{6,14},... | collective-permute-start | bytes 12296 | tf_op jit(solution)/shard_map/ppermute | solution.py:500
  18.5 3.6 %collective-permute-start.4 = (f32[8,128]{1,0:T(8,128)S(1)}, f32[8,128]{1,0:T(8,128)S(1)}, u32[]{:S(2)}, u32[]{:S(2)}) collective-permute-start(f32[8,128]{1,0:T(8,128)S(1)} %get-tuple-element.27), channel_id=1, source_target_pairs={{0,12},{4,0},{8,4},{12,8},{1,13},{5,1},{9,5},{13,9},{2,14},{6,2},{... | collective-permute-start | bytes 12296 | tf_op jit(solution)/shard_map/ppermute | solution.py:500
  22.1 3.0 %collective-permute-start.9 = (f32[8,128]{1,0:T(8,128)S(1)}, f32[8,128]{1,0:T(8,128)S(1)}, u32[]{:S(2)}, u32[]{:S(2)}) collective-permute-start(f32[8,128]{1,0:T(8,128)S(1)} %add_add_fusion.1), channel_id=1, source_target_pairs={{0,3},{1,2},{2,1},{3,0},{4,7},{5,6},{6,5},{7,4},{8,11},{9,10},{10,... | collective-permute-start | bytes 12296 | tf_op jit(solution)/shard_map/ppermute | solution.py:500
  22.1 3.7 %collective-permute-start.8 = (f32[8,128]{1,0:T(8,128)S(1)}, f32[8,128]{1,0:T(8,128)S(1)}, u32[]{:S(2)}, u32[]{:S(2)}) collective-permute-start(f32[8,128]{1,0:T(8,128)S(1)} %add_add_fusion.1), channel_id=1, source_target_pairs={{0,2},{1,3},{2,0},{3,1},{4,6},{5,7},{6,4},{7,5},{8,10},{9,11},{10,... | collective-permute-start | bytes 12296 | tf_op jit(solution)/shard_map/ppermute | solution.py:500
  23.9 1.9 %collective-permute-start.7 = (f32[8,128]{1,0:T(8,128)S(1)}, f32[8,128]{1,0:T(8,128)S(1)}, u32[]{:S(2)}, u32[]{:S(2)}) collective-permute-start(f32[8,128]{1,0:T(8,128)S(1)} %add_add_fusion.1), channel_id=1, source_target_pairs={{0,1},{1,0},{2,3},{3,2},{4,5},{5,4},{6,7},{7,6},{8,9},{9,8},{10,11... | collective-permute-start | bytes 12296 | tf_op jit(solution)/shard_map/ppermute | solution.py:500

commit v10 on v8

--- a/solution.py
+++ b/solution.py
@@ -416,7 +416,8 @@
     rows_of = zero
     for i, x in enumerate(totals):
         rows_of = jnp.where(row == i, jnp.broadcast_to(jnp.sum(x, axis=0, keepdims=True), (8, LANES)), rows_of)
-    sums[...] = jnp.broadcast_to(jnp.sum(rows_of, axis=1, keepdims=True), (8, LANES))
+    rows_of = jnp.broadcast_to(jnp.sum(rows_of, axis=1, keepdims=True), (8, LANES))
+    sums[...] = jnp.sum(jnp.where(lane == row, rows_of, 0.0), axis=0, keepdims=True)
 
 
 def energy_kernel(base, second, edges, phase, energy):
@@ -450,7 +451,10 @@
 
 
 def combine_kernel(base, second, energy, sums, displacement, sensitivity):
-    a, curve, plain, shifted, cross, bend = (sums[i : i + 1, :] for i in range(6))
+    lane = lax.broadcasted_iota(jnp.int32, (1, LANES), 1)
+    a, curve, plain, shifted, cross, bend = (
+        jnp.sum(jnp.where(lane == i, sums[...], 0.0), axis=1, keepdims=True) for i in range(6)
+    )
     slope = curve / a
     alpha = a / curve
     less = 1.0 - slope
@@ -532,7 +536,7 @@
             field,
             field,
             strips,
-            jax.ShapeDtypeStruct((8, LANES), f32),
+            jax.ShapeDtypeStruct((1, LANES), f32),
         ),
         [
             pltpu.VMEM((layers, 8, LANES), f32),

time: 26.9 us -> 26.8 us (level)
  no operation moved by 1% of the time
where the time goes in v10:
time: 26.8 us; the launch traced here: 26.5 us
  starting transfers between devices  13.6 us (51%)
  waiting for transfers between devices  7.71 us (29%)
  Pallas kernels  3.4 us (13%)
  other arithmetic  1.05 us (4%)
  between operations  0.7 us (3%)
    ppermute x6, starting transfers between devices, total_over(): lax.ppermute(x, axis, pairs)  6.14 us
    ppermute x6, waiting for transfers between devices, total_over(): lax.ppermute(x, axis, pairs)  3.46 us
    ppermute x1, waiting for transfers between devices, exchange(): low = lax.ppermute(up, axis, [(i, (i + 1) % count) for i in range(count)])  2.64 us
    ppermute x1, starting transfers between devices, exchange_pairs(): lax.ppermute(two, axis, [(i, (i - 1) % count if i % 2 == 0 else (i + 1) %...  2.43 us
    ppermute x1, starting transfers between devices, exchange(): low = lax.ppermute(up, axis, [(i, (i + 1) % count) for i in range(count)])  2.31 us
    ppermute x1, starting transfers between devices, exchange(): lax.ppermute(down, axis, [((i + 1) % count, i) for i in range(count)])  2.09 us
    pallas_call x1, Pallas kernels, body(): call(operator_kernel, (field, field, strips, jax.ShapeDtypeStruct((1, LAN...  1.32 us
    mul x1, other arithmetic, body(): rhs = [(1 - fixed).astype(jnp.float32) * force[c] for c in range(comps)]  1.04 us
  transfers between devices with their start and end apart: 10, of which 9 were waited for; matrix products, arithmetic and copies ran while one was open for 0% of the time, Pallas kernels for 3%

profile of v10, /device:TPU:0, one launch (start us, length us, event | category | flops | bytes accessed | tf_op | source)
XLA Modules:
  0.0 26.5 jit_solution(6792339391627112924)
XLA Ops:
  0.6 0.0 copy-start
  0.6 0.0 copy-start.1
  0.6 1.0 %bitcast_multiply_fusion = (f32[17,6,128]{2,1,0:T(8,128)S(1)}, f32[17,6,128]{2,1,0:T(8,128)S(1)}, f32[17,6,128]{2,1,0:T(8,128)S(1)}) fusion(f32[3,17,6,128]{3,2,1,0:T(8,128)} %param.3, s32[17,6,128]{2,1,0:T(8,128)} %fixed.5), kind=kLoop, calls=%fused_computation | loop fusion | flops 65280 | bytes 365568 | tf_op jit(solution)/shard_map/mul | solution.py:509
  1.7 0.0 copy-done
  1.7 0.0 copy-done.1
  1.7 0.2 shard_map.50
  2.0 2.4 %collective-permute-start = (f32[2,8,128]{2,1,0:T(8,128)S(1)}, f32[2,8,128]{2,1,0:T(8,128)S(1)}, u32[]{:S(2)}, u32[]{:S(2)}) collective-permute-start(f32[2,8,128]{2,1,0:T(8,128)S(1)} %get-tuple-element.18), channel_id=1, source_target_pairs={{0,3},{1,2},{2,1},{3,0},{4,7},{5,6},{6,5},{7,4},{8,11},{9,10},{10,... | collective-permute-start | bytes 24584 | tf_op jit(solution)/shard_map/ppermute | solution.py:477
  4.4 0.7 %collective-permute-start.1 = (f32[2,8,128]{2,1,0:T(8,128)S(1)}, f32[2,8,128]{2,1,0:T(8,128)S(1)}, u32[]{:S(2)}, u32[]{:S(2)}) collective-permute-start(f32[2,8,128]{2,1,0:T(8,128)S(1)} %get-tuple-element.19), channel_id=1, source_target_pairs={{0,1},{1,0},{2,3},{3,2},{4,5},{5,4},{6,7},{7,6},{8,9},{9,8},{10,11... | collective-permute-start | bytes 24584 | tf_op jit(solution)/shard_map/ppermute | solution.py:478
  5.1 0.1 shard_map.51
  5.1 0.6 %collective-permute-done.got2 = f32[2,8,128]{2,1,0:T(8,128)S(1)} collective-permute-done((f32[2,8,128]{2,1,0:T(8,128)S(1)}, f32[2,8,128]{2,1,0:T(8,128)S(1)}, u32[]{:S(2)}, u32[]{:S(2)}) %collective-permute-start) | collective-permute-done | bytes 8224 | tf_op jit(solution)/shard_map/ppermute | solution.py:477
  5.7 0.1 collective-permute-done.1.got1
  5.9 0.2 shard_map.52
  6.1 2.3 %collective-permute-start.2 = (f32[144,128]{1,0:T(8,128)S(1)}, f32[144,128]{1,0:T(8,128)S(1)}, u32[]{:S(2)}, u32[]{:S(2)}) collective-permute-start(f32[144,128]{1,0:T(8,128)S(1)} %get-tuple-element.24), channel_id=1, source_target_pairs={{0,4},{4,8},{8,12},{12,0},{1,5},{5,9},{9,13},{13,1},{2,6},{6,10},{... | collective-permute-start | bytes 221192 | tf_op jit(solution)/shard_map/ppermute | solution.py:484
  8.4 2.1 %collective-permute-start.3 = (f32[144,128]{1,0:T(8,128)S(1)}, f32[144,128]{1,0:T(8,128)S(1)}, u32[]{:S(2)}, u32[]{:S(2)}) collective-permute-start(f32[144,128]{1,0:T(8,128)S(1)} %get-tuple-element.25), channel_id=1, source_target_pairs={{4,0},{8,4},{12,8},{0,12},{5,1},{9,5},{13,9},{1,13},{6,2},{10,6},{... | collective-permute-start | bytes 221192 | tf_op jit(solution)/shard_map/ppermute | solution.py:485
  10.5 2.6 %collective-permute-done.2.lo = f32[144,128]{1,0:T(8,128)S(1)} collective-permute-done((f32[144,128]{1,0:T(8,128)S(1)}, f32[144,128]{1,0:T(8,128)S(1)}, u32[]{:S(2)}, u32[]{:S(2)}) %collective-permute-start.2) | collective-permute-done | bytes 73760 | tf_op jit(solution)/shard_map/ppermute | solution.py:484
  13.1 0.9 %collective-permute-done.3.hi = f32[144,128]{1,0:T(8,128)S(1)} collective-permute-done((f32[144,128]{1,0:T(8,128)S(1)}, f32[144,128]{1,0:T(8,128)S(1)}, u32[]{:S(2)}, u32[]{:S(2)}) %collective-permute-start.3) | collective-permute-done | bytes 73760 | tf_op jit(solution)/shard_map/ppermute | solution.py:485
  14.0 1.3 %shard_map.53 = (f32[51,8,128]{2,1,0:T(8,128)S(1)}, f32[51,8,128]{2,1,0:T(8,128)S(1)}, f32[6,8,128]{2,1,0:T(8,128)S(1)}, f32[1,128]{1,0:T(1,128)S(1)}) custom-call(f32[17,6,128]{2,1,0:T(8,128)S(1)} %get-tuple-element.33.rhs_0, f32[17,6,128]{2,1,0:T(8,128)S(1)} %get-tuple-element.34.rhs_1, f32[17,6,128]{2,1,0:T(8,128)S(1)} %get-tuple-element.32.rhs_2, ...), custom_call_target="tpu_custom_call" | custom-call | tf_op jit(solution)/shard_map/pallas_call | solution.py:533
  15.3 1.1 %collective-permute-start.6 = (f32[1,128]{1,0:T(1,128)S(1)}, f32[1,128]{1,0:T(1,128)S(1)}, u32[]{:S(2)}, u32[]{:S(2)}) collective-permute-start(f32[1,128]{1,0:T(1,128)S(1)} %get-tuple-element.29), channel_id=1, source_target_pairs={{0,4},{4,8},{8,12},{12,0},{1,5},{5,9},{9,13},{13,1},{2,6},{6,10},{... | collective-permute-start | bytes 1544 | tf_op jit(solution)/shard_map/ppermute | solution.py:500
  16.4 2.1 %collective-permute-start.5 = (f32[1,128]{1,0:T(1,128)S(1)}, f32[1,128]{1,0:T(1,128)S(1)}, u32[]{:S(2)}, u32[]{:S(2)}) collective-permute-start(f32[1,128]{1,0:T(1,128)S(1)} %get-tuple-element.29), channel_id=1, source_target_pairs={{0,8},{4,12},{8,0},{12,4},{1,9},{5,13},{9,1},{13,5},{2,10},{6,14},... | collective-permute-start | bytes 1544 | tf_op jit(solution)/shard_map/ppermute | solution.py:500
  18.5 1.1 %collective-permute-start.4 = (f32[1,128]{1,0:T(1,128)S(1)}, f32[1,128]{1,0:T(1,128)S(1)}, u32[]{:S(2)}, u32[]{:S(2)}) collective-permute-start(f32[1,128]{1,0:T(1,128)S(1)} %get-tuple-element.29), channel_id=1, source_target_pairs={{0,12},{4,0},{8,4},{12,8},{1,13},{5,1},{9,5},{13,9},{2,14},{6,2},{... | collective-permute-start | bytes 1544 | tf_op jit(solution)/shard_map/ppermute | solution.py:500
  19.6 1.1 %collective-permute-done.6 = f32[1,128]{1,0:T(1,128)S(1)} collective-permute-done((f32[1,128]{1,0:T(1,128)S(1)}, f32[1,128]{1,0:T(1,128)S(1)}, u32[]{:S(2)}, u32[]{:S(2)}) %collective-permute-start.6) | collective-permute-done | bytes 544 | tf_op jit(solution)/shard_map/ppermute | solution.py:500
  20.6 0.2 collective-permute-done.5
  20.9 1.2 %collective-permute-done.4 = f32[1,128]{1,0:T(1,128)S(1)} collective-permute-done((f32[1,128]{1,0:T(1,128)S(1)}, f32[1,128]{1,0:T(1,128)S(1)}, u32[]{:S(2)}, u32[]{:S(2)}) %collective-permute-start.4) | collective-permute-done | bytes 544 | tf_op jit(solution)/shard_map/ppermute | solution.py:500
  22.1 0.0 collective-permute-start.9
  22.1 1.8 %collective-permute-start.8 = (f32[1,128]{1,0:T(1,128)S(1)}, f32[1,128]{1,0:T(1,128)S(1)}, u32[]{:S(2)}, u32[]{:S(2)}) collective-permute-start(f32[1,128]{1,0:T(1,128)S(1)} %add_add_fusion.1), channel_id=1, source_target_pairs={{0,2},{1,3},{2,0},{3,1},{4,6},{5,7},{6,4},{7,5},{8,10},{9,11},{10,... | collective-permute-start | bytes 1544 | tf_op jit(solution)/shard_map/ppermute | solution.py:500
  23.8 0.1 collective-permute-start.7
  23.9 0.8 %shard_map.54.energy = f32[3,96,128]{2,1,0:T(8,128)S(1)} custom-call(f32[51,8,128]{2,1,0:T(8,128)S(1)} %get-tuple-element.26.base, f32[51,8,128]{2,1,0:T(8,128)S(1)} %get-tuple-element.27.second, f32[6,8,128]{2,1,0:T(8,128)S(1)} %get-tuple-element.28.edges, s32[96,128]{1,0:T(8,128)S(1)} %bitcast.15), custom_call_target="tpu_custom_call" | custom-call | tf_op jit(solution)/shard_map/pallas_call | solution.py:549
  24.7 0.3 %collective-permute-done.9 = f32[1,128]{1,0:T(1,128)S(1)} collective-permute-done((f32[1,128]{1,0:T(1,128)S(1)}, f32[1,128]{1,0:T(1,128)S(1)}, u32[]{:S(2)}, u32[]{:S(2)}) %collective-permute-start.9) | collective-permute-done | bytes 544 | tf_op jit(solution)/shard_map/ppermute | solution.py:500
  25.0 0.6 %collective-permute-done.8 = f32[1,128]{1,0:T(1,128)S(1)} collective-permute-done((f32[1,128]{1,0:T(1,128)S(1)}, f32[1,128]{1,0:T(1,128)S(1)}, u32[]{:S(2)}, u32[]{:S(2)}) %collective-permute-start.8) | collective-permute-done | bytes 544 | tf_op jit(solution)/shard_map/ppermute | solution.py:500
  25.7 0.0 collective-permute-done.7
  25.7 0.8 %shard_map.55 = (f32[3,17,6,128]{3,2,1,0:T(8,128)}, f32[96,128]{1,0:T(8,128)}) custom-call(f32[51,8,128]{2,1,0:T(8,128)S(1)} %get-tuple-element.26.base, f32[51,8,128]{2,1,0:T(8,128)S(1)} %get-tuple-element.27.second, f32[3,96,128]{2,1,0:T(8,128)S(1)} %shard_map.54.energy, f32[1,128]{1,0:T(1,128)S(1)} %add_add_fusion.sums), custom_call_target="tpu_custom_call" | custom-call | tf_op jit(solution)/shard_map/pallas_call | solution.py:551
  (2 shorter events, 0.0 us)
Async XLA Ops:
  0.6 1.1 %copy-start = (s32[17,6,128]{2,1,0:T(8,128)S(1)}, s32[17,6,128]{2,1,0:T(8,128)}, u32[]{:S(2)}) copy-start(s32[17,6,128]{2,1,0:T(8,128)} %fixed.5) | copy-start | bytes 156676
  0.6 1.1 %copy-start.1 = (s32[16,6,128]{2,0,1:T(8,128)S(1)}, s32[16,6,128]{2,0,1:T(8,128)}, u32[]{:S(2)}) copy-start(s32[16,6,128]{2,0,1:T(8,128)} %param.4) | copy-start | bytes 147460
  2.0 3.8 %collective-permute-start = (f32[2,8,128]{2,1,0:T(8,128)S(1)}, f32[2,8,128]{2,1,0:T(8,128)S(1)}, u32[]{:S(2)}, u32[]{:S(2)}) collective-permute-start(f32[2,8,128]{2,1,0:T(8,128)S(1)} %get-tuple-element.18), channel_id=1, source_target_pairs={{0,3},{1,2},{2,1},{3,0},{4,7},{5,6},{6,5},{7,4},{8,11},{9,10},{10,... | collective-permute-start | bytes 24584 | tf_op jit(solution)/shard_map/ppermute | solution.py:477
  4.4 1.5 %collective-permute-start.1 = (f32[2,8,128]{2,1,0:T(8,128)S(1)}, f32[2,8,128]{2,1,0:T(8,128)S(1)}, u32[]{:S(2)}, u32[]{:S(2)}) collective-permute-start(f32[2,8,128]{2,1,0:T(8,128)S(1)} %get-tuple-element.19), channel_id=1, source_target_pairs={{0,1},{1,0},{2,3},{3,2},{4,5},{5,4},{6,7},{7,6},{8,9},{9,8},{10,11... | collective-permute-start | bytes 24584 | tf_op jit(solution)/shard_map/ppermute | solution.py:478
  6.1 7.0 %collective-permute-start.2 = (f32[144,128]{1,0:T(8,128)S(1)}, f32[144,128]{1,0:T(8,128)S(1)}, u32[]{:S(2)}, u32[]{:S(2)}) collective-permute-start(f32[144,128]{1,0:T(8,128)S(1)} %get-tuple-element.24), channel_id=1, source_target_pairs={{0,4},{4,8},{8,12},{12,0},{1,5},{5,9},{9,13},{13,1},{2,6},{6,10},{... | collective-permute-start | bytes 221192 | tf_op jit(solution)/shard_map/ppermute | solution.py:484
  8.4 5.6 %collective-permute-start.3 = (f32[144,128]{1,0:T(8,128)S(1)}, f32[144,128]{1,0:T(8,128)S(1)}, u32[]{:S(2)}, u32[]{:S(2)}) collective-permute-start(f32[144,128]{1,0:T(8,128)S(1)} %get-tuple-element.25), channel_id=1, source_target_pairs={{4,0},{8,4},{12,8},{0,12},{5,1},{9,5},{13,9},{1,13},{6,2},{10,6},{... | collective-permute-start | bytes 221192 | tf_op jit(solution)/shard_map/ppermute | solution.py:485
  15.3 5.3 %collective-permute-start.6 = (f32[1,128]{1,0:T(1,128)S(1)}, f32[1,128]{1,0:T(1,128)S(1)}, u32[]{:S(2)}, u32[]{:S(2)}) collective-permute-start(f32[1,128]{1,0:T(1,128)S(1)} %get-tuple-element.29), channel_id=1, source_target_pairs={{0,4},{4,8},{8,12},{12,0},{1,5},{5,9},{9,13},{13,1},{2,6},{6,10},{... | collective-permute-start | bytes 1544 | tf_op jit(solution)/shard_map/ppermute | solution.py:500
  16.4 4.4 %collective-permute-start.5 = (f32[1,128]{1,0:T(1,128)S(1)}, f32[1,128]{1,0:T(1,128)S(1)}, u32[]{:S(2)}, u32[]{:S(2)}) collective-permute-start(f32[1,128]{1,0:T(1,128)S(1)} %get-tuple-element.29), channel_id=1, source_target_pairs={{0,8},{4,12},{8,0},{12,4},{1,9},{5,13},{9,1},{13,5},{2,10},{6,14},... | collective-permute-start | bytes 1544 | tf_op jit(solution)/shard_map/ppermute | solution.py:500
  18.5 3.5 %collective-permute-start.4 = (f32[1,128]{1,0:T(1,128)S(1)}, f32[1,128]{1,0:T(1,128)S(1)}, u32[]{:S(2)}, u32[]{:S(2)}) collective-permute-start(f32[1,128]{1,0:T(1,128)S(1)} %get-tuple-element.29), channel_id=1, source_target_pairs={{0,12},{4,0},{8,4},{12,8},{1,13},{5,1},{9,5},{13,9},{2,14},{6,2},{... | collective-permute-start | bytes 1544 | tf_op jit(solution)/shard_map/ppermute | solution.py:500
  22.1 3.0 %collective-permute-start.9 = (f32[1,128]{1,0:T(1,128)S(1)}, f32[1,128]{1,0:T(1,128)S(1)}, u32[]{:S(2)}, u32[]{:S(2)}) collective-permute-start(f32[1,128]{1,0:T(1,128)S(1)} %add_add_fusion.1), channel_id=1, source_target_pairs={{0,3},{1,2},{2,1},{3,0},{4,7},{5,6},{6,5},{7,4},{8,11},{9,10},{10,... | collective-permute-start | bytes 1544 | tf_op jit(solution)/shard_map/ppermute | solution.py:500
  22.1 3.6 %collective-permute-start.8 = (f32[1,128]{1,0:T(1,128)S(1)}, f32[1,128]{1,0:T(1,128)S(1)}, u32[]{:S(2)}, u32[]{:S(2)}) collective-permute-start(f32[1,128]{1,0:T(1,128)S(1)} %add_add_fusion.1), channel_id=1, source_target_pairs={{0,2},{1,3},{2,0},{3,1},{4,6},{5,7},{6,4},{7,5},{8,10},{9,11},{10,... | collective-permute-start | bytes 1544 | tf_op jit(solution)/shard_map/ppermute | solution.py:500
  23.8 1.8 %collective-permute-start.7 = (f32[1,128]{1,0:T(1,128)S(1)}, f32[1,128]{1,0:T(1,128)S(1)}, u32[]{:S(2)}, u32[]{:S(2)}) collective-permute-start(f32[1,128]{1,0:T(1,128)S(1)} %add_add_fusion.1), channel_id=1, source_target_pairs={{0,1},{1,0},{2,3},{3,2},{4,5},{5,4},{6,7},{7,6},{8,9},{9,8},{10,11... | collective-permute-start | bytes 1544 | tf_op jit(solution)/shard_map/ppermute | solution.py:500

commit v11 on v9

--- a/solution.py
+++ b/solution.py
@@ -420,7 +420,8 @@
     rows_of = zero
     for i, x in enumerate(totals):
         rows_of = jnp.where(row == i, jnp.broadcast_to(jnp.sum(x, axis=0, keepdims=True), (8, LANES)), rows_of)
-    sums[...] = jnp.broadcast_to(jnp.sum(rows_of, axis=1, keepdims=True), (8, LANES))
+    rows_of = jnp.broadcast_to(jnp.sum(rows_of, axis=1, keepdims=True), (8, LANES))
+    sums[...] = jnp.sum(jnp.where(lane == row, rows_of, 0.0), axis=0, keepdims=True)
 
 
 def energy_kernel(base, second, edges, phase, energy):
@@ -454,7 +455,10 @@
 
 
 def combine_kernel(base, second, energy, sums, displacement, sensitivity):
-    a, curve, plain, shifted, cross, bend = (sums[i : i + 1, :] for i in range(6))
+    lane = lax.broadcasted_iota(jnp.int32, (1, LANES), 1)
+    a, curve, plain, shifted, cross, bend = (
+        jnp.sum(jnp.where(lane == i, sums[...], 0.0), axis=1, keepdims=True) for i in range(6)
+    )
     slope = curve / a
     alpha = a / curve
     less = 1.0 - slope
@@ -537,7 +541,7 @@
             field,
             field,
             strips,
-            jax.ShapeDtypeStruct((8, LANES), f32),
+            jax.ShapeDtypeStruct((1, LANES), f32),
         ),
         [
             pltpu.VMEM((layers, 8, LANES), f32),

time: 26.9 us -> 26.9 us (level)
  no operation moved by 1% of the time
where the time goes in v11:
time: 26.9 us; the launch traced here: 26.5 us
  starting transfers between devices  13.7 us (51%)
  waiting for transfers between devices  7.69 us (29%)
  Pallas kernels  3.39 us (13%)
  other arithmetic  1.05 us (4%)
  between operations  0.7 us (3%)
    ppermute x6, starting transfers between devices, total_over(): lax.ppermute(x, axis, pairs)  6.16 us
    ppermute x6, waiting for transfers between devices, total_over(): lax.ppermute(x, axis, pairs)  3.39 us
    ppermute x1, waiting for transfers between devices, exchange(): low = lax.ppermute(up, axis, [(i, (i + 1) % count) for i in range(count)])  2.53 us
    ppermute x1, starting transfers between devices, exchange_pairs(): lax.ppermute(two, axis, [(i, (i - 1) % count if i % 2 == 0 else (i + 1) %...  2.43 us
    ppermute x1, starting transfers between devices, exchange(): low = lax.ppermute(up, axis, [(i, (i + 1) % count) for i in range(count)])  2.31 us
    ppermute x1, starting transfers between devices, exchange(): lax.ppermute(down, axis, [((i + 1) % count, i) for i in range(count)])  2.09 us
    pallas_call x1, Pallas kernels, body(): call(operator_kernel, (field, field, strips, jax.ShapeDtypeStruct((1, LAN...  1.32 us
    mul x1, other arithmetic, body(): rhs = [(1 - fixed).astype(jnp.float32) * force[c] for c in range(comps)]  1.04 us
  transfers between devices with their start and end apart: 10, of which 9 were waited for; matrix products, arithmetic and copies ran while one was open for 0% of the time, Pallas kernels for 3%

profile of v11, /device:TPU:0, one launch (start us, length us, event | category | flops | bytes accessed | tf_op | source)
XLA Modules:
  0.0 26.5 jit_solution(15027003115418668759)
XLA Ops:
  0.6 0.0 copy-start
  0.6 0.0 copy-start.1
  0.6 1.0 %bitcast_multiply_fusion = (f32[17,6,128]{2,1,0:T(8,128)S(1)}, f32[17,6,128]{2,1,0:T(8,128)S(1)}, f32[17,6,128]{2,1,0:T(8,128)S(1)}) fusion(f32[3,17,6,128]{3,2,1,0:T(8,128)} %param.3, s32[17,6,128]{2,1,0:T(8,128)} %fixed.5), kind=kLoop, calls=%fused_computation | loop fusion | flops 65280 | bytes 365568 | tf_op jit(solution)/shard_map/mul | solution.py:513
  1.7 0.0 copy-done
  1.7 0.0 copy-done.1
  1.7 0.2 shard_map.50
  2.0 2.4 %collective-permute-start = (f32[2,8,128]{2,1,0:T(8,128)S(1)}, f32[2,8,128]{2,1,0:T(8,128)S(1)}, u32[]{:S(2)}, u32[]{:S(2)}) collective-permute-start(f32[2,8,128]{2,1,0:T(8,128)S(1)} %get-tuple-element.17), channel_id=1, source_target_pairs={{0,3},{1,2},{2,1},{3,0},{4,7},{5,6},{6,5},{7,4},{8,11},{9,10},{10,... | collective-permute-start | bytes 24584 | tf_op jit(solution)/shard_map/ppermute | solution.py:481
  4.4 0.7 %collective-permute-start.1 = (f32[2,8,128]{2,1,0:T(8,128)S(1)}, f32[2,8,128]{2,1,0:T(8,128)S(1)}, u32[]{:S(2)}, u32[]{:S(2)}) collective-permute-start(f32[2,8,128]{2,1,0:T(8,128)S(1)} %get-tuple-element.18), channel_id=1, source_target_pairs={{0,1},{1,0},{2,3},{3,2},{4,5},{5,4},{6,7},{7,6},{8,9},{9,8},{10,11... | collective-permute-start | bytes 24584 | tf_op jit(solution)/shard_map/ppermute | solution.py:482
  5.1 0.1 shard_map.51
  5.1 0.6 %collective-permute-done.got2 = f32[2,8,128]{2,1,0:T(8,128)S(1)} collective-permute-done((f32[2,8,128]{2,1,0:T(8,128)S(1)}, f32[2,8,128]{2,1,0:T(8,128)S(1)}, u32[]{:S(2)}, u32[]{:S(2)}) %collective-permute-start) | collective-permute-done | bytes 8224 | tf_op jit(solution)/shard_map/ppermute | solution.py:481
  5.7 0.1 collective-permute-done.1.got1
  5.9 0.1 shard_map.52
  6.0 2.3 %collective-permute-start.2 = (f32[144,128]{1,0:T(8,128)S(1)}, f32[144,128]{1,0:T(8,128)S(1)}, u32[]{:S(2)}, u32[]{:S(2)}) collective-permute-start(f32[144,128]{1,0:T(8,128)S(1)} %get-tuple-element.21), channel_id=1, source_target_pairs={{0,4},{4,8},{8,12},{12,0},{1,5},{5,9},{9,13},{13,1},{2,6},{6,10},{... | collective-permute-start | bytes 221192 | tf_op jit(solution)/shard_map/ppermute | solution.py:488
  8.3 0.1 shard_map.53
  8.4 2.1 %collective-permute-start.3 = (f32[144,128]{1,0:T(8,128)S(1)}, f32[144,128]{1,0:T(8,128)S(1)}, u32[]{:S(2)}, u32[]{:S(2)}) collective-permute-start(f32[144,128]{1,0:T(8,128)S(1)} %shard_map.53), channel_id=1, source_target_pairs={{4,0},{8,4},{12,8},{0,12},{5,1},{9,5},{13,9},{1,13},{6,2},{10,6},{... | collective-permute-start | bytes 221192 | tf_op jit(solution)/shard_map/ppermute | solution.py:489
  10.5 2.5 %collective-permute-done.2.lo = f32[144,128]{1,0:T(8,128)S(1)} collective-permute-done((f32[144,128]{1,0:T(8,128)S(1)}, f32[144,128]{1,0:T(8,128)S(1)}, u32[]{:S(2)}, u32[]{:S(2)}) %collective-permute-start.2) | collective-permute-done | bytes 73760 | tf_op jit(solution)/shard_map/ppermute | solution.py:488
  13.0 1.0 %collective-permute-done.3.hi = f32[144,128]{1,0:T(8,128)S(1)} collective-permute-done((f32[144,128]{1,0:T(8,128)S(1)}, f32[144,128]{1,0:T(8,128)S(1)}, u32[]{:S(2)}, u32[]{:S(2)}) %collective-permute-start.3) | collective-permute-done | bytes 73760 | tf_op jit(solution)/shard_map/ppermute | solution.py:489
  14.0 1.3 %shard_map.54 = (f32[51,8,128]{2,1,0:T(8,128)S(1)}, f32[51,8,128]{2,1,0:T(8,128)S(1)}, f32[6,8,128]{2,1,0:T(8,128)S(1)}, f32[1,128]{1,0:T(1,128)S(1)}) custom-call(f32[17,6,128]{2,1,0:T(8,128)S(1)} %get-tuple-element.31.rhs_0, f32[17,6,128]{2,1,0:T(8,128)S(1)} %get-tuple-element.32.rhs_1, f32[17,6,128]{2,1,0:T(8,128)S(1)} %get-tuple-element.30.rhs_2, ...), custom_call_target="tpu_custom_call" | custom-call | tf_op jit(solution)/shard_map/pallas_call | solution.py:538
  15.4 1.0 %collective-permute-start.6 = (f32[1,128]{1,0:T(1,128)S(1)}, f32[1,128]{1,0:T(1,128)S(1)}, u32[]{:S(2)}, u32[]{:S(2)}) collective-permute-start(f32[1,128]{1,0:T(1,128)S(1)} %get-tuple-element.27), channel_id=1, source_target_pairs={{0,4},{4,8},{8,12},{12,0},{1,5},{5,9},{9,13},{13,1},{2,6},{6,10},{... | collective-permute-start | bytes 1544 | tf_op jit(solution)/shard_map/ppermute | solution.py:504
  16.3 2.2 %collective-permute-start.5 = (f32[1,128]{1,0:T(1,128)S(1)}, f32[1,128]{1,0:T(1,128)S(1)}, u32[]{:S(2)}, u32[]{:S(2)}) collective-permute-start(f32[1,128]{1,0:T(1,128)S(1)} %get-tuple-element.27), channel_id=1, source_target_pairs={{0,8},{4,12},{8,0},{12,4},{1,9},{5,13},{9,1},{13,5},{2,10},{6,14},... | collective-permute-start | bytes 1544 | tf_op jit(solution)/shard_map/ppermute | solution.py:504
  18.5 1.1 %collective-permute-start.4 = (f32[1,128]{1,0:T(1,128)S(1)}, f32[1,128]{1,0:T(1,128)S(1)}, u32[]{:S(2)}, u32[]{:S(2)}) collective-permute-start(f32[1,128]{1,0:T(1,128)S(1)} %get-tuple-element.27), channel_id=1, source_target_pairs={{0,12},{4,0},{8,4},{12,8},{1,13},{5,1},{9,5},{13,9},{2,14},{6,2},{... | collective-permute-start | bytes 1544 | tf_op jit(solution)/shard_map/ppermute | solution.py:504
  19.6 1.1 %collective-permute-done.6 = f32[1,128]{1,0:T(1,128)S(1)} collective-permute-done((f32[1,128]{1,0:T(1,128)S(1)}, f32[1,128]{1,0:T(1,128)S(1)}, u32[]{:S(2)}, u32[]{:S(2)}) %collective-permute-start.6) | collective-permute-done | bytes 544 | tf_op jit(solution)/shard_map/ppermute | solution.py:504
  20.7 0.1 collective-permute-done.5
  20.8 1.3 %collective-permute-done.4 = f32[1,128]{1,0:T(1,128)S(1)} collective-permute-done((f32[1,128]{1,0:T(1,128)S(1)}, f32[1,128]{1,0:T(1,128)S(1)}, u32[]{:S(2)}, u32[]{:S(2)}) %collective-permute-start.4) | collective-permute-done | bytes 544 | tf_op jit(solution)/shard_map/ppermute | solution.py:504
  22.1 0.0 collective-permute-start.9
  22.1 1.8 %collective-permute-start.8 = (f32[1,128]{1,0:T(1,128)S(1)}, f32[1,128]{1,0:T(1,128)S(1)}, u32[]{:S(2)}, u32[]{:S(2)}) collective-permute-start(f32[1,128]{1,0:T(1,128)S(1)} %add_add_fusion.1), channel_id=1, source_target_pairs={{0,2},{1,3},{2,0},{3,1},{4,6},{5,7},{6,4},{7,5},{8,10},{9,11},{10,... | collective-permute-start | bytes 1544 | tf_op jit(solution)/shard_map/ppermute | solution.py:504
  23.9 0.1 collective-permute-start.7
  24.0 0.8 %shard_map.55.energy = f32[3,96,128]{2,1,0:T(8,128)S(1)} custom-call(f32[51,8,128]{2,1,0:T(8,128)S(1)} %get-tuple-element.24.base, f32[51,8,128]{2,1,0:T(8,128)S(1)} %get-tuple-element.25.second, f32[6,8,128]{2,1,0:T(8,128)S(1)} %get-tuple-element.26.edges, s32[96,128]{1,0:T(8,128)S(1)} %bitcast.15), custom_call_target="tpu_custom_call" | custom-call | tf_op jit(solution)/shard_map/pallas_call | solution.py:554
  24.7 0.3 %collective-permute-done.9 = f32[1,128]{1,0:T(1,128)S(1)} collective-permute-done((f32[1,128]{1,0:T(1,128)S(1)}, f32[1,128]{1,0:T(1,128)S(1)}, u32[]{:S(2)}, u32[]{:S(2)}) %collective-permute-start.9) | collective-permute-done | bytes 544 | tf_op jit(solution)/shard_map/ppermute | solution.py:504
  25.0 0.6 %collective-permute-done.8 = f32[1,128]{1,0:T(1,128)S(1)} collective-permute-done((f32[1,128]{1,0:T(1,128)S(1)}, f32[1,128]{1,0:T(1,128)S(1)}, u32[]{:S(2)}, u32[]{:S(2)}) %collective-permute-start.8) | collective-permute-done | bytes 544 | tf_op jit(solution)/shard_map/ppermute | solution.py:504
  25.7 0.0 collective-permute-done.7
  25.7 0.8 %shard_map.56 = (f32[3,17,6,128]{3,2,1,0:T(8,128)}, f32[96,128]{1,0:T(8,128)}) custom-call(f32[51,8,128]{2,1,0:T(8,128)S(1)} %get-tuple-element.24.base, f32[51,8,128]{2,1,0:T(8,128)S(1)} %get-tuple-element.25.second, f32[3,96,128]{2,1,0:T(8,128)S(1)} %shard_map.55.energy, f32[1,128]{1,0:T(1,128)S(1)} %add_add_fusion.sums), custom_call_target="tpu_custom_call" | custom-call | tf_op jit(solution)/shard_map/pallas_call | solution.py:556
  (2 shorter events, 0.0 us)
Async XLA Ops:
  0.6 1.1 %copy-start = (s32[17,6,128]{2,1,0:T(8,128)S(1)}, s32[17,6,128]{2,1,0:T(8,128)}, u32[]{:S(2)}) copy-start(s32[17,6,128]{2,1,0:T(8,128)} %fixed.5) | copy-start | bytes 156676
  0.6 1.1 %copy-start.1 = (s32[16,6,128]{2,0,1:T(8,128)S(1)}, s32[16,6,128]{2,0,1:T(8,128)}, u32[]{:S(2)}) copy-start(s32[16,6,128]{2,0,1:T(8,128)} %param.4) | copy-start | bytes 147460
  2.0 3.8 %collective-permute-start = (f32[2,8,128]{2,1,0:T(8,128)S(1)}, f32[2,8,128]{2,1,0:T(8,128)S(1)}, u32[]{:S(2)}, u32[]{:S(2)}) collective-permute-start(f32[2,8,128]{2,1,0:T(8,128)S(1)} %get-tuple-element.17), channel_id=1, source_target_pairs={{0,3},{1,2},{2,1},{3,0},{4,7},{5,6},{6,5},{7,4},{8,11},{9,10},{10,... | collective-permute-start | bytes 24584 | tf_op jit(solution)/shard_map/ppermute | solution.py:481
  4.4 1.5 %collective-permute-start.1 = (f32[2,8,128]{2,1,0:T(8,128)S(1)}, f32[2,8,128]{2,1,0:T(8,128)S(1)}, u32[]{:S(2)}, u32[]{:S(2)}) collective-permute-start(f32[2,8,128]{2,1,0:T(8,128)S(1)} %get-tuple-element.18), channel_id=1, source_target_pairs={{0,1},{1,0},{2,3},{3,2},{4,5},{5,4},{6,7},{7,6},{8,9},{9,8},{10,11... | collective-permute-start | bytes 24584 | tf_op jit(solution)/shard_map/ppermute | solution.py:482
  6.0 7.0 %collective-permute-start.2 = (f32[144,128]{1,0:T(8,128)S(1)}, f32[144,128]{1,0:T(8,128)S(1)}, u32[]{:S(2)}, u32[]{:S(2)}) collective-permute-start(f32[144,128]{1,0:T(8,128)S(1)} %get-tuple-element.21), channel_id=1, source_target_pairs={{0,4},{4,8},{8,12},{12,0},{1,5},{5,9},{9,13},{13,1},{2,6},{6,10},{... | collective-permute-start | bytes 221192 | tf_op jit(solution)/shard_map/ppermute | solution.py:488
  8.4 5.6 %collective-permute-start.3 = (f32[144,128]{1,0:T(8,128)S(1)}, f32[144,128]{1,0:T(8,128)S(1)}, u32[]{:S(2)}, u32[]{:S(2)}) collective-permute-start(f32[144,128]{1,0:T(8,128)S(1)} %shard_map.53), channel_id=1, source_target_pairs={{4,0},{8,4},{12,8},{0,12},{5,1},{9,5},{13,9},{1,13},{6,2},{10,6},{... | collective-permute-start | bytes 221192 | tf_op jit(solution)/shard_map/ppermute | solution.py:489
  15.4 5.3 %collective-permute-start.6 = (f32[1,128]{1,0:T(1,128)S(1)}, f32[1,128]{1,0:T(1,128)S(1)}, u32[]{:S(2)}, u32[]{:S(2)}) collective-permute-start(f32[1,128]{1,0:T(1,128)S(1)} %get-tuple-element.27), channel_id=1, source_target_pairs={{0,4},{4,8},{8,12},{12,0},{1,5},{5,9},{9,13},{13,1},{2,6},{6,10},{... | collective-permute-start | bytes 1544 | tf_op jit(solution)/shard_map/ppermute | solution.py:504
  16.3 4.4 %collective-permute-start.5 = (f32[1,128]{1,0:T(1,128)S(1)}, f32[1,128]{1,0:T(1,128)S(1)}, u32[]{:S(2)}, u32[]{:S(2)}) collective-permute-start(f32[1,128]{1,0:T(1,128)S(1)} %get-tuple-element.27), channel_id=1, source_target_pairs={{0,8},{4,12},{8,0},{12,4},{1,9},{5,13},{9,1},{13,5},{2,10},{6,14},... | collective-permute-start | bytes 1544 | tf_op jit(solution)/shard_map/ppermute | solution.py:504
  18.5 3.5 %collective-permute-start.4 = (f32[1,128]{1,0:T(1,128)S(1)}, f32[1,128]{1,0:T(1,128)S(1)}, u32[]{:S(2)}, u32[]{:S(2)}) collective-permute-start(f32[1,128]{1,0:T(1,128)S(1)} %get-tuple-element.27), channel_id=1, source_target_pairs={{0,12},{4,0},{8,4},{12,8},{1,13},{5,1},{9,5},{13,9},{2,14},{6,2},{... | collective-permute-start | bytes 1544 | tf_op jit(solution)/shard_map/ppermute | solution.py:504
  22.1 3.0 %collective-permute-start.9 = (f32[1,128]{1,0:T(1,128)S(1)}, f32[1,128]{1,0:T(1,128)S(1)}, u32[]{:S(2)}, u32[]{:S(2)}) collective-permute-start(f32[1,128]{1,0:T(1,128)S(1)} %add_add_fusion.1), channel_id=1, source_target_pairs={{0,3},{1,2},{2,1},{3,0},{4,7},{5,6},{6,5},{7,4},{8,11},{9,10},{10,... | collective-permute-start | bytes 1544 | tf_op jit(solution)/shard_map/ppermute | solution.py:504
  22.1 3.6 %collective-permute-start.8 = (f32[1,128]{1,0:T(1,128)S(1)}, f32[1,128]{1,0:T(1,128)S(1)}, u32[]{:S(2)}, u32[]{:S(2)}) collective-permute-start(f32[1,128]{1,0:T(1,128)S(1)} %add_add_fusion.1), channel_id=1, source_target_pairs={{0,2},{1,3},{2,0},{3,1},{4,6},{5,7},{6,4},{7,5},{8,10},{9,11},{10,... | collective-permute-start | bytes 1544 | tf_op jit(solution)/shard_map/ppermute | solution.py:504
  23.9 1.8 %collective-permute-start.7 = (f32[1,128]{1,0:T(1,128)S(1)}, f32[1,128]{1,0:T(1,128)S(1)}, u32[]{:S(2)}, u32[]{:S(2)}) collective-permute-start(f32[1,128]{1,0:T(1,128)S(1)} %add_add_fusion.1), channel_id=1, source_target_pairs={{0,1},{1,0},{2,3},{3,2},{4,5},{5,4},{6,7},{7,6},{8,9},{9,8},{10,11... | collective-permute-start | bytes 1544 | tf_op jit(solution)/shard_map/ppermute | solution.py:504
